TPU v7x, 32 devices: a whole 2x2x4 slice. The times are simulated.
32 devices in a mesh: parts: 2 (over y), wide: 8 (over z, x), tensor: 2 (over core).
Axes of the slice: x: 2, y: 2, z: 4, core: 2. Of those that a mesh axis runs over, the one named last changes fastest.
Arguments:
- tokens: bfloat16 [256, 8192], P(('parts', 'wide'), 'tensor'), parts along dimension 0, may hold values from -6 to 6
- gate_weight: bfloat16 [8192, 16384], P('tensor', 'wide'), may hold values from -0.0625 to 0.0625
- up_weight: bfloat16 [8192, 16384], P('tensor', 'wide'), may hold values from -0.0625 to 0.0625
- down_weight: bfloat16 [16384, 8192], P('wide', 'tensor'), may hold values from -0.046875 to 0.046875
- adapter_down: bfloat16 [128, 16, 16384], P('parts', None, 'wide'), parts along dimension 0, may hold values from -0.046875 to 0.046875
- adapter_up: bfloat16 [128, 16, 8192], P(('parts', 'wide'), None, 'tensor'), parts along dimension 0, may hold values from -1.5 to 1.5
- row_adapter: int32 [256], P('parts'), parts along dimension 0, may hold values from 0 to 63, as said below
- block_first: int32 [20], P('parts'), parts along dimension 0, may hold values from 0 to 128, as said below
- page_table: int32 [128], P('parts'), parts along dimension 0, may hold values from 0 to 63, each once
Outputs:
- layer_out: bfloat16 [256, 8192], P(('parts', 'wide'), 'tensor'), parts along dimension 0
There are 2 independent parts, one for each index of `parts`. A program takes and returns all parts, laid end to end along the dimension named above; an argument that names none is the same for every part. Nothing has to cross between parts.
Inputs may be any that keep to these rules, and one draw needn't show every extreme that they name: row_adapter never falls along the rows and takes exactly 8 distinct values; its runs of equal values are the segments. block_first never falls; a segment that starts at row s and holds l rows owns the entries s, s + 128, s + 256 and so on, ceil(l / 128) of them, in order of segments; all later entries equal 128, and there is at least one such entry. `page_table`: every page is named once; page p lies on index p // 8 of wide.
All inputs are finite; a program needn't handle non-finite values.
Results may differ from a plain program's by a relative error of at most 0.0053.
Values may be sent and summed in bfloat16 or wider, within the bound.
No kernel may reach another device: no remote copies, remote signals or barrier semaphores. Data moves between devices by JAX's collectives and lax.ppermute only.
A program may use at most 128 MiB of HBM per device.

v0:
```python
import jax
import jax.numpy as jnp
from jax import lax
from jax.sharding import PartitionSpec as P

BLOCK = 128
SEGS = 8


def from_root(shard, axis, root):
    mine = lax.axis_index(axis) == root
    return lax.psum(jnp.where(mine, shard, jnp.zeros_like(shard)), axis)


def block_shrink(hidden, adapter_down, row_adapter, block_first):
    total_rows, hidden_local = hidden.shape
    adapter_rank = adapter_down.shape[1]
    padded = jnp.concatenate([hidden, jnp.zeros((BLOCK, hidden_local), hidden.dtype)], axis=0)
    marked = jnp.concatenate([row_adapter, jnp.full((BLOCK,), -1, jnp.int32)], axis=0)

    def one_block(position, totals):
        opening = block_first[position]
        adapter = row_adapter[jnp.minimum(opening, total_rows - 1)]
        keeping = lax.dynamic_slice_in_dim(marked, opening, BLOCK) == adapter
        window = lax.dynamic_slice_in_dim(padded, opening, BLOCK, 0)
        window = jnp.where(keeping[:, None], window, jnp.zeros((), window.dtype))
        term = lax.dot_general(
            window,
            adapter_down[adapter],
            (((1,), (1,)), ((), ())),
            preferred_element_type=jnp.float32,
        )
        before = lax.dynamic_slice_in_dim(totals, opening, BLOCK, 0)
        return lax.dynamic_update_slice_in_dim(totals, before + term, opening, 0)

    start_totals = jnp.zeros((total_rows + BLOCK, adapter_rank), jnp.float32)
    totals = lax.fori_loop(0, block_first.shape[0], one_block, start_totals)
    return totals[:total_rows]


def segment_pages(row_adapter, page_table):
    changes = jnp.concatenate(
        [jnp.ones((1,), jnp.int32), (row_adapter[1:] != row_adapter[:-1]).astype(jnp.int32)]
    )
    segment_of_row = jnp.cumsum(changes) - 1
    labels = lax.iota(jnp.int32, SEGS)
    opening = (segment_of_row[None, :] == labels[:, None]) & (changes[None, :] == 1)
    segment_adapter = jnp.sum(jnp.where(opening, row_adapter[None, :], 0), axis=1)
    return (segment_of_row, page_table[segment_adapter])


def local(
    tokens,
    gate_weight,
    up_weight,
    down_weight,
    adapter_down,
    adapter_up,
    row_adapter,
    block_first,
    page_table,
):
    rows_dev = tokens.shape[0]
    hidden_local = gate_weight.shape[1]
    width_local = down_weight.shape[1]
    adapter_rank = adapter_up.shape[1]
    pages_dev = adapter_up.shape[0]
    wide_index = lax.axis_index("wide")
    piece = lax.all_gather(tokens, "wide", axis=0, tiled=True)
    gate_part = jnp.dot(piece, gate_weight, preferred_element_type=jnp.float32)
    up_part = jnp.dot(piece, up_weight, preferred_element_type=jnp.float32)
    partial_sums = jnp.concatenate([gate_part, up_part], axis=1)
    both_sums = lax.psum(partial_sums, "tensor")
    hidden = (jax.nn.silu(both_sums[:, :hidden_local]) * both_sums[:, hidden_local:]).astype(
        jnp.bfloat16
    )
    shrink_terms = block_shrink(hidden, adapter_down, row_adapter, block_first)
    base_term = jnp.dot(hidden, down_weight, preferred_element_type=jnp.float32)
    summed = lax.psum_scatter(
        jnp.concatenate([base_term, shrink_terms], axis=1), "wide", scatter_dimension=0, tiled=True
    )
    shrunk_mine = summed[:, width_local:].astype(jnp.bfloat16)
    summed = summed[:, :width_local]
    segment_of_row, segment_page = segment_pages(row_adapter, page_table)
    owners = segment_page // pages_dev
    slots = segment_page % pages_dev
    copies = []
    for label in range(SEGS):
        copies.append(from_root(adapter_up[slots[label]], "wide", owners[label]))
    fetched = jnp.stack(copies, axis=0)
    my_segments = lax.dynamic_slice_in_dim(segment_of_row, wide_index * rows_dev, rows_dev)
    selected = my_segments[:, None] == lax.iota(jnp.int32, SEGS)[None, :]
    spread = jnp.where(selected[:, :, None], shrunk_mine[:, None, :], jnp.zeros((), jnp.bfloat16))
    spread = spread.reshape(rows_dev, SEGS * adapter_rank)
    delta = jnp.dot(
        spread,
        fetched.reshape(SEGS * adapter_rank, width_local),
        preferred_element_type=jnp.float32,
    )
    return (summed + delta).astype(jnp.bfloat16)


def solution(mesh):
    in_specs = (
        P(("parts", "wide"), "tensor"),
        P("tensor", "wide"),
        P("tensor", "wide"),
        P("wide", "tensor"),
        P("parts", None, "wide"),
        P(("parts", "wide"), None, "tensor"),
        P("parts"),
        P("parts"),
        P("parts"),
    )
    out_specs = P(("parts", "wide"), "tensor")
    return jax.shard_map(local, mesh=mesh, in_specs=in_specs, out_specs=out_specs, check_vma=False)
```

profile of v0, /device:TPU:0, one launch (start us, length us, event | category | flops | bytes accessed | tf_op | source)
XLA Modules:
  0.0 254.8 jit_solution(10664352586530542611)
XLA Ops:
  6.5 0.7 all-gather.2.cloned.1.call-update
  7.3 45.1 %all-gather.2.cloned.1.call-done = bf16[128,4096]{1,0:T(8,128)(2,1)} async-done(((bf16[16,4096]{1,0:T(8,128)(2,1)}), bf16[128,4096]{1,0:T(8,128)(2,1)}) %all-gather.2.cloned.1.call-update) | async-done | bytes 1048592 | tf_op jit(solution)/shard_map/all_gather | solution.py:69
  52.4 8.6 %fusion.23 = f32[128,2048]{1,0:T(8,128)S(1)} fusion(bf16[128,4096]{1,0:T(8,128)(2,1)} %all-gather.2.cloned.1.call-done, bf16[4096,2048]{1,0:T(8,128)(2,1)} %param.13), kind=kOutput, calls=%fused_computation.62 | convolution fusion | flops 2147483648 | bytes 18874368 | tf_op jit(solution)/shard_map/dot_general | solution.py:71
  60.9 2.3 copy-done.1
  63.5 2.4 fusion.22
  65.9 1.4 pad_maximum_fusion.1
  68.1 0.6 gather_fusion
  68.8 0.7 fusion.20
  89.6 1.0 dynamic-slice_select_fusion
  90.7 1.8 fusion.10
  92.7 71.5 %while.13 = (s32[]{:T(128)}, f32[256,16]{0,1:T(8,128)S(1)}, s32[10]{0:T(128)S(1)}, s32[256]{0:T(256)S(1)}, s32[128]{0:T(128)S(1)}, /*index=5*/bf16[256,2048]{1,0...) while((s32[]{:T(128)}, f32[256,16]{0,1:T(8,128)S(1)}, ...), condition=%wide.region_2.3_spmd, body=%wide.region_1.2_spmd.sunk | while | flops 8652940 | bytes 625563 | solution.py:37
  92.7 0.6 dynamic_slice.110
  95.5 0.6 dynamic_slice.111
  97.8 0.6 dynamic-slice_compare_fusion.2
  98.4 1.1 convolution_add_fusion.2
  99.9 0.6 dynamic_slice.110
  102.7 0.6 dynamic_slice.111
  104.9 0.6 dynamic-slice_compare_fusion.2
  105.6 1.1 convolution_add_fusion.2
  107.0 0.6 dynamic_slice.110
  109.9 0.6 dynamic_slice.111
  112.1 0.6 dynamic-slice_compare_fusion.2
  112.8 1.1 convolution_add_fusion.2
  114.2 0.6 dynamic_slice.110
  117.0 0.6 dynamic_slice.111
  119.3 0.6 dynamic-slice_compare_fusion.2
  119.9 1.1 convolution_add_fusion.2
  121.4 0.6 dynamic_slice.110
  124.2 0.6 dynamic_slice.111
  126.5 0.6 dynamic-slice_compare_fusion.2
  127.1 1.1 convolution_add_fusion.2
  128.5 0.6 dynamic_slice.110
  131.4 0.6 dynamic_slice.111
  133.6 0.6 dynamic-slice_compare_fusion.2
  134.3 1.1 convolution_add_fusion.2
  135.7 0.6 dynamic_slice.110
  138.5 0.6 dynamic_slice.111
  140.8 0.6 dynamic-slice_compare_fusion.2
  141.4 1.1 convolution_add_fusion.2
  142.9 0.6 dynamic_slice.110
  145.7 0.6 dynamic_slice.111
  148.0 0.6 dynamic-slice_compare_fusion.2
  148.6 1.1 convolution_add_fusion.2
  150.1 0.6 dynamic_slice.110
  152.9 0.6 dynamic_slice.111
  155.2 0.6 dynamic-slice_compare_fusion.2
  155.8 1.1 convolution_add_fusion.2
  157.1 0.6 dynamic_slice.110
  160.0 0.6 dynamic_slice.111
  162.2 0.6 dynamic-slice_compare_fusion.2
  162.9 1.1 convolution_add_fusion.2
  164.2 8.2 %fusion.24 = f32[128,4096]{1,0:T(8,128)S(1)} fusion(bf16[128,2048]{1,0:T(8,128)(2,1)S(1)} %fusion.10, bf16[2048,4096]{1,0:T(8,128)(2,1)} %param.14), kind=kOutput, calls=%fused_computation.63 | convolution fusion | flops 2147483648 | bytes 19398656 | tf_op jit(solution)/shard_map/dot_general | solution.py:78
  172.5 1.5 pad_maximum_fusion
  174.6 0.9 constant_dynamic-update-slice_fusion.7
  175.5 0.9 constant_dynamic-update-slice_fusion.6
  176.4 0.9 constant_dynamic-update-slice_fusion.5
  177.3 0.9 constant_dynamic-update-slice_fusion.4
  178.3 0.9 constant_dynamic-update-slice_fusion.3
  179.2 0.9 constant_dynamic-update-slice_fusion.2
  180.1 0.9 constant_dynamic-update-slice_fusion.1
  181.0 0.9 constant_dynamic-update-slice_fusion
  181.9 63.5 %reduce-scatter.2.cloned.1.call-done = f32[16,4112]{1,0:T(8,128)} async-done(((f32[128,4112]{1,0:T(8,128)}), f32[16,4112]{1,0:T(8,128)}) %reduce-scatter.2.cloned.1.call-update) | async-done | bytes 263184 | tf_op jit(solution)/shard_map/reduce_scatter | solution.py:79
  245.4 0.7 slice.107
  246.1 2.1 fusion.9
  (46 shorter events, 4.7 us)
Async XLA Ops:
  6.5 61.6 %copy-start = (s32[64]{0:T(128)S(1)}, s32[64]{0:T(128)}, u32[]{:S(2)}) copy-start(s32[64]{0:T(128)} %param.19) | copy-start | bytes 772
  6.5 45.8 %all-gather.2.cloned.1.call-start = ((), (), s32[]{:S(2)}) async-start(), calls=%async_computation.1 | async-start | bytes 1179648 | tf_op jit(solution)/shard_map/all_gather | solution.py:69
  7.3 83.5 %all-reduce.6.cloned.1.call-start = ((), (), s32[]{:S(2)}) async-start(), calls=%async_computation.2 | async-start | bytes 4194304 | tf_op jit(solution)/shard_map/psum | solution.py:73
  52.4 10.9 %copy-start.1 = (bf16[4096,2048]{1,0:T(8,128)(2,1)S(1)}, bf16[4096,2048]{1,0:T(8,128)(2,1)}, u32[]{:S(2)}) copy-start(bf16[4096,2048]{1,0:T(8,128)(2,1)} %param.12) | copy-start | bytes 50331652
  52.4 11.1 %copy-start.2 = (bf16[128,4096]{1,0:T(8,128)(2,1)S(1)}, bf16[128,4096]{1,0:T(8,128)(2,1)}, u32[]{:S(2)}) copy-start(bf16[128,4096]{1,0:T(8,128)(2,1)} %all-gather.2.cloned.1.call-done) | copy-start | bytes 3145732
  65.8 1.5 copy-start.4
  65.8 23.8 %copy-start.3 = (bf16[8,16,4096]{2,1,0:T(8,128)(2,1)S(1)}, bf16[8,16,4096]{2,1,0:T(8,128)(2,1)}, u32[]{:S(2)}) copy-start(bf16[8,16,4096]{2,1,0:T(8,128)(2,1)} %param.16) | copy-start | bytes 3145732
  67.3 107.3 %all-reduce.8.cloned.1.call-start = ((), (), s32[]{:S(2)}) async-start(), calls=%async_computation.4 | async-start | bytes 2097152 | tf_op jit(solution)/shard_map/psum | solution.py:12
  67.7 25.0 %copy-start.5 = (s32[10]{0:T(128)S(1)}, s32[10]{0:T(128)}, u32[]{:S(2)}) copy-start(s32[10]{0:T(128)} %param.18) | copy-start | bytes 124
  90.6 154.8 %reduce-scatter.2.cloned.1.call-start = ((), (), s32[]{:S(2)}) async-start(), calls=%async_computation.3 | async-start | bytes 2433024 | tf_op jit(solution)/shard_map/reduce_scatter | solution.py:79
Sparse Core Ops, SparseCore 0:
  9.5 42.8 all-gather.1
  67.4 19.9 all-reduce.5
  92.6 81.9 all-reduce.7
  177.9 67.4 reduce-scatter.1
where the time goes:
time: 257 us; the launch traced here: 255 us
  waiting for transfers between devices  110 us (43%)
  loops' own time  39.4 us (15%)
  between operations  33.4 us (13%)
  matrix products  32.5 us (13%)
  local copies, waits for them, and re-layouts  26.9 us (10%)
  other arithmetic  12.7 us (5%)
    reduce_scatter x1, waiting for transfers between devices, local(): lax.psum_scatter(jnp.concatenate([base_term, shrink_terms], axis=1), 'wid...  63.5 us
    all_gather x1, waiting for transfers between devices, local(): piece = lax.all_gather(tokens, 'wide', axis=0, tiled=True)  45.1 us
    another operation x1, loops' own time, block_shrink(): totals = lax.fori_loop(0, block_first.shape[0], one_block, start_totals)  39.4 us
    dot_general x10, matrix products, one_block(): lax.dot_general(window, adapter_down[adapter], (((1,), (1,)), ((), ())),...  11.2 us
    unnamed x19, local copies, waits for them, and re-layouts  8.93 us
    dot_general x1, matrix products, local(): up_part = jnp.dot(piece, up_weight, preferred_element_type=jnp.float32)  8.56 us
    dot_general x1, matrix products, local(): base_term = jnp.dot(hidden, down_weight, preferred_element_type=jnp.float32)  8.21 us
    eq x10, other arithmetic, one_block(): keeping = lax.dynamic_slice_in_dim(marked, opening, BLOCK) == adapter  6.37 us
  transfers between devices with their start and end apart: 4, of which 3 were waited for; matrix products, arithmetic and copies ran while one was open for 21% of the time, Pallas kernels for 0%

commit v1 on v0

v1 whole, which is shorter than its diff:
```python
import functools

import jax
import jax.numpy as jnp
from jax import lax
from jax.experimental import pallas as pl
from jax.experimental.pallas import tpu as pltpu
from jax.sharding import PartitionSpec as P

BLOCK = 128
CHUNKS = 2
MIB = 1 << 20

SMEM = pl.BlockSpec(memory_space=pltpu.SMEM)
VMEM = pl.BlockSpec(memory_space=pltpu.VMEM)
ANY = pl.BlockSpec(memory_space=pl.ANY)


def dot(a, b, dims=((1,), (0,))):
    return lax.dot_general(a, b, (dims, ((), ())), preferred_element_type=jnp.float32)


def swap(x, axis, n, k):
    return lax.ppermute(x, axis, [(i, i ^ k) for i in range(n)])


def reorder(x, me, n, width):
    lanes = n * width
    at = lax.broadcasted_iota(jnp.int32, x.shape, 1) // width
    bit = 1
    while bit < n:
        low = (at & bit) == 0
        other = jnp.where(low, pltpu.roll(x, lanes - bit * width, 1), pltpu.roll(x, bit * width, 1))
        x = jnp.where((me & bit) != 0, other, x)
        bit *= 2
    return x


def gate_up_kernel(n, *refs):
    blocks, (gate_w, up_w, gate, up, sent, x) = refs[:n], refs[n:]
    rows = blocks[0].shape[0]

    @pl.when(pl.program_id(0) == 0)
    def _():
        for k in range(n):
            x[k * rows : (k + 1) * rows, :] = blocks[k][...]

    g = dot(x[...], gate_w[...])
    u = dot(x[...], up_w[...])
    gate[...] = g
    up[...] = u
    sent[0] = g.astype(sent.dtype)
    sent[1] = u.astype(sent.dtype)


def gate_up(blocks, gate_w, up_w, chunk):
    n, (rows, depth) = len(blocks), blocks[0].shape
    width = gate_w.shape[1] // CHUNKS
    tile = min(256, width)
    steps = width // tile
    total = n * rows
    block = pl.BlockSpec((rows, depth), lambda j: (0, 0))
    weight = pl.BlockSpec((depth, tile), lambda j: (0, chunk * steps + j))
    out = pl.BlockSpec((total, tile), lambda j: (0, j))
    return pl.pallas_call(
        functools.partial(gate_up_kernel, n),
        grid=(steps,),
        in_specs=[block] * n + [weight, weight],
        out_specs=[out, out, pl.BlockSpec((2, total, tile), lambda j: (0, 0, j))],
        out_shape=[
            jax.ShapeDtypeStruct((total, width), jnp.float32),
            jax.ShapeDtypeStruct((total, width), jnp.float32),
            jax.ShapeDtypeStruct((2, total, width), jnp.bfloat16),
        ],
        scratch_shapes=[pltpu.VMEM((total, depth), jnp.bfloat16)],
        compiler_params=pltpu.CompilerParams(vmem_limit_bytes=44 * MIB),
        cost_estimate=pl.CostEstimate(
            flops=4 * total * depth * width, bytes_accessed=4 * depth * width, transcendentals=0
        ),
        name="gate_up",
    )(*blocks, gate_w, up_w)


def block_mask(b, ids, adapters, row_adapter, block_first):
    opening = block_first[b]
    adapter = row_adapter[jnp.minimum(opening, row_adapter.shape[0] - 1)]
    inside = (ids >= opening) & (ids < opening + BLOCK) & (adapters == adapter)
    return inside, adapter


def hidden_kernel(n, row_adapter, block_first, adapters, *refs):
    gates, ups, gots = refs[:CHUNKS], refs[CHUNKS : 2 * CHUNKS], refs[2 * CHUNKS : 3 * CHUNKS]
    adapter_down, hidden, shrunk, factors, sems = refs[3 * CHUNKS :]
    count, rank = block_first.shape[0], adapter_down.shape[1]

    def copy(b):
        adapter = row_adapter[jnp.minimum(block_first[b], row_adapter.shape[0] - 1)]
        return pltpu.make_async_copy(adapter_down.at[adapter], factors.at[pl.ds(b * rank, rank)], sems.at[b])

    for b in range(count):
        copy(b).start()
    width = gates[0].shape[1]
    for c in range(CHUNKS):
        g = gates[c][...] + gots[c][0].astype(jnp.float32)
        u = ups[c][...] + gots[c][1].astype(jnp.float32)
        hidden[:, c * width : (c + 1) * width] = (g / (1.0 + jnp.exp(-g)) * u).astype(hidden.dtype)
    for b in range(count):
        copy(b).wait()
    terms = dot(factors[...], hidden[...], ((1,), (1,)))
    total = jnp.zeros((rank, terms.shape[1]), jnp.float32)
    me = lax.axis_index("wide")
    rows = terms.shape[1] // n
    terms = reorder(terms, me, n, rows)
    ids = lax.broadcasted_iota(jnp.int32, (1, terms.shape[1]), 1)
    for b in range(count):
        inside, _ = block_mask(b, ids, adapters[...], row_adapter, block_first)
        total = total + jnp.where(inside, terms[b * rank : (b + 1) * rank], 0.0)
    shrunk[...] = total


def make_hidden(n, row_adapter, block_first, gates, ups, gots, adapter_down):
    total, width = gates[0].shape
    rank, hidden_local = adapter_down.shape[1], adapter_down.shape[2]
    count = block_first.shape[0]
    return pl.pallas_call(
        functools.partial(hidden_kernel, n),
        in_specs=[SMEM, SMEM, VMEM] + [VMEM] * (3 * CHUNKS) + [ANY],
        out_specs=[VMEM, VMEM],
        out_shape=[
            jax.ShapeDtypeStruct((total, hidden_local), jnp.bfloat16),
            jax.ShapeDtypeStruct((rank, total), jnp.float32),
        ],
        scratch_shapes=[
            pltpu.VMEM((count * rank, hidden_local), jnp.bfloat16),
            pltpu.SemaphoreType.DMA((count,)),
        ],
        compiler_params=pltpu.CompilerParams(vmem_limit_bytes=32 * MIB),
        name="hidden_shrink",
    )(row_adapter, block_first, row_adapter.reshape(1, -1), *gates, *ups, *gots, adapter_down)


def down_kernel(hidden, weight, base):
    base[...] = dot(hidden[...], weight[...])


def down(hidden, weight):
    total, depth = hidden.shape
    width = weight.shape[1]
    tile = min(512, width)
    return pl.pallas_call(
        down_kernel,
        grid=(width // tile,),
        in_specs=[pl.BlockSpec((total, depth), lambda j: (0, 0)), pl.BlockSpec((depth, tile), lambda j: (0, j))],
        out_specs=pl.BlockSpec((total, tile), lambda j: (0, j)),
        out_shape=jax.ShapeDtypeStruct((total, width), jnp.float32),
        compiler_params=pltpu.CompilerParams(vmem_limit_bytes=24 * MIB),
        cost_estimate=pl.CostEstimate(
            flops=2 * total * depth * width, bytes_accessed=2 * depth * width, transcendentals=0
        ),
        name="down",
    )(hidden, weight)


def delta_kernel(n, row_adapter, block_first, page_table, adapters, shrunk, adapter_up, base, *refs):
    outs, spread = refs[:n], refs[n]
    me = lax.axis_index("wide")
    slots, rank, _ = adapter_up.shape
    total = shrunk.shape[1]
    rows = total // n
    ids = lax.broadcasted_iota(jnp.int32, (1, total), 1)
    slot_of = jnp.full((1, total), -1, jnp.int32)
    for b in range(block_first.shape[0]):
        inside, adapter = block_mask(b, ids, adapters[...], row_adapter, block_first)
        slot_of = jnp.where(inside, page_table[adapter] - me * slots, slot_of)
    mine = shrunk[...].astype(jnp.bfloat16).astype(jnp.float32)
    for s in range(slots):
        part = reorder(jnp.where(slot_of == s, mine, 0.0), me, n, rows)
        spread[:, s * rank : (s + 1) * rank] = part.T.astype(jnp.bfloat16)
    up = adapter_up[...].reshape(slots * rank, adapter_up.shape[2])
    result = base[...] + dot(spread[...], up)
    for k in range(n):
        outs[k][...] = result[k * rows : (k + 1) * rows].astype(outs[k].dtype)


def add_delta(n, row_adapter, block_first, page_table, shrunk, adapter_up, base):
    total, width = base.shape
    slots, rank, _ = adapter_up.shape
    rows = total // n
    tile = min(1024, width)
    whole = lambda shape: pl.BlockSpec(shape, lambda j: (0,) * len(shape))
    return pl.pallas_call(
        functools.partial(delta_kernel, n),
        grid=(width // tile,),
        in_specs=[
            SMEM,
            SMEM,
            SMEM,
            whole((1, total)),
            whole((rank, total)),
            pl.BlockSpec((slots, rank, tile), lambda j: (0, 0, j)),
            pl.BlockSpec((total, tile), lambda j: (0, j)),
        ],
        out_specs=[pl.BlockSpec((rows, tile), lambda j: (0, j))] * n,
        out_shape=[jax.ShapeDtypeStruct((rows, width), jnp.bfloat16)] * n,
        scratch_shapes=[pltpu.VMEM((total, slots * rank), jnp.bfloat16)],
        compiler_params=pltpu.CompilerParams(vmem_limit_bytes=32 * MIB),
        name="add_delta",
    )(row_adapter, block_first, page_table, row_adapter.reshape(1, -1), shrunk, adapter_up, base)


def sum_kernel(*refs):
    terms, out = refs[:-1], refs[-1]
    total = terms[0][...].astype(jnp.float32)
    for term in terms[1:]:
        total = total + term[...].astype(jnp.float32)
    out[...] = total.astype(out.dtype)


def add_up(terms):
    return pl.pallas_call(
        sum_kernel,
        in_specs=[VMEM] * len(terms),
        out_specs=VMEM,
        out_shape=jax.ShapeDtypeStruct(terms[0].shape, jnp.bfloat16),
        compiler_params=pltpu.CompilerParams(vmem_limit_bytes=24 * MIB),
        name="sum_rows",
    )(*terms)


def local(
    n,
    tokens,
    gate_weight,
    up_weight,
    down_weight,
    adapter_down,
    adapter_up,
    row_adapter,
    block_first,
    page_table,
):
    far_first = list(range(n - 1, 0, -1))
    blocks = [tokens] + [None] * (n - 1)
    for k in far_first:
        blocks[k] = swap(tokens, "wide", n, k)
    gates, ups, gots = [], [], []
    for c in range(CHUNKS):
        gate, up, sent = gate_up(blocks, gate_weight, up_weight, c)
        gates.append(gate)
        ups.append(up)
        gots.append(swap(sent, "tensor", 2, 1))
    hidden, shrunk = make_hidden(n, row_adapter, block_first, gates, ups, gots, adapter_down)
    base = down(hidden, down_weight)
    bit = 1
    while bit < n:
        shrunk = shrunk + swap(shrunk, "wide", n, bit)
        bit *= 2
    parts = add_delta(n, row_adapter, block_first, page_table, shrunk, adapter_up, base)
    terms = [parts[0]] + [swap(parts[k], "wide", n, k) for k in far_first]
    return add_up(terms)


def solution(mesh):
    in_specs = (
        P(("parts", "wide"), "tensor"),
        P("tensor", "wide"),
        P("tensor", "wide"),
        P("wide", "tensor"),
        P("parts", None, "wide"),
        P(("parts", "wide"), None, "tensor"),
        P("parts"),
        P("parts"),
        P("parts"),
    )
    out_specs = P(("parts", "wide"), "tensor")
    body = functools.partial(local, mesh.shape["wide"])
    return jax.shard_map(body, mesh=mesh, in_specs=in_specs, out_specs=out_specs, check_vma=False)
```

time: 257 us -> 105 us (0.41)
  waiting for transfers between devices: 110 us -> 22.8 us
  starting transfers between devices: 0.12 us -> 44.7 us
  loops' own time: 39.4 us -> 0 us
  between operations: 33.4 us -> 0.15 us
  matrix products: 32.5 us -> 0 us
  Pallas kernels: 0 us -> 30 us
  local copies, waits for them, and re-layouts: 26.9 us -> 6.81 us
  other arithmetic: 12.7 us -> 0.01 us
    reduce_scatter x1 -> x0, waiting for transfers between devices: 63.5 us -> none  [local(): lax.psum_scatter(jnp.concatenate([base_term, shrink_terms], axis=1), 'wid...]
    all_gather x1 -> x0, waiting for transfers between devices: 45.1 us -> none  [local(): piece = lax.all_gather(tokens, 'wide', axis=0, tiled=True)]
    ppermute x0 -> x19, starting transfers between devices: none -> 44.7 us  [swap(): return lax.ppermute(x, axis, [(i, i ^ k) for i in range(n)])]
    another operation x1 -> x0, loops' own time: 39.4 us -> none  [block_shrink(): totals = lax.fori_loop(0, block_first.shape[0], one_block, start_totals)]
    dot_general x14 -> x0, matrix products: 32.5 us -> none  [the longest x10 11.2 us: one_block(): lax.dot_general(window, adapter_down[adapter], (((1,), (1,)), ((), ())),...]
    pallas_call x0 -> x6, Pallas kernels: none -> 30 us  [the longest x2 16.6 us: gate_up(): pl.pallas_call(functools.partial(gate_up_kernel, n), grid=(steps,), in_sp...]
    ppermute x0 -> x19, waiting for transfers between devices: none -> 22.8 us  [swap(): return lax.ppermute(x, axis, [(i, i ^ k) for i in range(n)])]
    dynamic_slice x21 -> x0, local copies, waits for them, and re-layouts: 11.7 us -> none  [the longest x10 5.82 us: one_block(): opening = block_first[position]]
  transfers between devices with their start and end apart: 4 -> 19, of which waited for: 3 -> 10; matrix products, arithmetic and copies ran while one was open for 21% -> 0% of each run, Pallas kernels for 0% -> 13%
where the time goes in v1:
time: 105 us; the launch traced here: 104 us
  starting transfers between devices  44.7 us (43%)
  Pallas kernels  30 us (29%)
  waiting for transfers between devices  22.8 us (22%)
  local copies, waits for them, and re-layouts  6.81 us (6%)
    ppermute x19, starting transfers between devices, swap(): return lax.ppermute(x, axis, [(i, i ^ k) for i in range(n)])  44.7 us
    ppermute x19, waiting for transfers between devices, swap(): return lax.ppermute(x, axis, [(i, i ^ k) for i in range(n)])  22.8 us
    pallas_call x2, Pallas kernels, gate_up(): pl.pallas_call(functools.partial(gate_up_kernel, n), grid=(steps,), in_sp...  16.6 us
    unnamed x28, local copies, waits for them, and re-layouts  6.81 us
    pallas_call x1, Pallas kernels, down(): pl.pallas_call(down_kernel, grid=(width // tile,), in_specs=[pl.BlockSpec...  5.38 us
    pallas_call x1, Pallas kernels, add_delta(): pl.pallas_call(functools.partial(delta_kernel, n), grid=(width // tile,),...  4.11 us
    pallas_call x1, Pallas kernels, make_hidden(): pl.pallas_call(functools.partial(hidden_kernel, n), in_specs=[SMEM, SMEM,...  3.04 us
  transfers between devices with their start and end apart: 19, of which 10 were waited for; matrix products, arithmetic and copies ran while one was open for 0% of the time, Pallas kernels for 13%

profile of v1, /device:TPU:0, one launch (start us, length us, event | category | flops | bytes accessed | tf_op | source)
XLA Modules:
  0.0 104.5 jit_solution(13274658358260031498)
XLA Ops:
  0.0 6.0 %collective-permute-start.6 = (bf16[16,4096]{1,0:T(8,128)(2,1)}, bf16[16,4096]{1,0:T(8,128)(2,1)S(1)}, u32[]{:S(2)}, u32[]{:S(2)}) collective-permute-start(bf16[16,4096]{1,0:T(8,128)(2,1)} %refs_0_.3), channel_id=1, source_target_pairs={{0,14},{2,12},{4,10},{6,8},{8,6},{10,4},{12,2},{14,0},{1,15},{3,13... | collective-permute-start | bytes 393224 | tf_op jit(solution)/shard_map/ppermute | solution.py:24
  6.0 0.2 collective-permute-start.5
  6.2 0.8 collective-permute-start.4
  7.0 1.9 %collective-permute-start.3 = (bf16[16,4096]{1,0:T(8,128)(2,1)}, bf16[16,4096]{1,0:T(8,128)(2,1)S(1)}, u32[]{:S(2)}, u32[]{:S(2)}) collective-permute-start(bf16[16,4096]{1,0:T(8,128)(2,1)} %refs_0_.3), channel_id=1, source_target_pairs={{0,8},{2,10},{4,12},{6,14},{8,0},{10,2},{12,4},{14,6},{1,9},{3,11}... | collective-permute-start | bytes 393224 | tf_op jit(solution)/shard_map/ppermute | solution.py:24
  8.9 2.4 %collective-permute-start.2 = (bf16[16,4096]{1,0:T(8,128)(2,1)}, bf16[16,4096]{1,0:T(8,128)(2,1)S(1)}, u32[]{:S(2)}, u32[]{:S(2)}) collective-permute-start(bf16[16,4096]{1,0:T(8,128)(2,1)} %refs_0_.3), channel_id=1, source_target_pairs={{0,6},{2,4},{4,2},{6,0},{8,14},{10,12},{12,10},{14,8},{1,7},{3,5},... | collective-permute-start | bytes 393224 | tf_op jit(solution)/shard_map/ppermute | solution.py:24
  11.3 0.0 collective-permute-done.6.refs_7_
  11.3 10.6 %collective-permute-start.1 = (bf16[16,4096]{1,0:T(8,128)(2,1)}, bf16[16,4096]{1,0:T(8,128)(2,1)S(1)}, u32[]{:S(2)}, u32[]{:S(2)}) collective-permute-start(bf16[16,4096]{1,0:T(8,128)(2,1)} %refs_0_.3), channel_id=1, source_target_pairs={{0,4},{2,6},{4,0},{6,2},{8,12},{10,14},{12,8},{14,10},{1,5},{3,7},... | collective-permute-start | bytes 393224 | tf_op jit(solution)/shard_map/ppermute | solution.py:24
  21.9 0.0 collective-permute-done.5.refs_6_
  21.9 1.4 %collective-permute-start = (bf16[16,4096]{1,0:T(8,128)(2,1)}, bf16[16,4096]{1,0:T(8,128)(2,1)S(1)}, u32[]{:S(2)}, u32[]{:S(2)}) collective-permute-start(bf16[16,4096]{1,0:T(8,128)(2,1)} %refs_0_.3), channel_id=1, source_target_pairs={{0,2},{2,0},{4,6},{6,4},{8,10},{10,8},{12,14},{14,12},{1,3},{3,1},... | collective-permute-start | bytes 393224 | tf_op jit(solution)/shard_map/ppermute | solution.py:24
  23.3 3.5 %collective-permute-done.4.refs_5_ = bf16[16,4096]{1,0:T(8,128)(2,1)S(1)} collective-permute-done((bf16[16,4096]{1,0:T(8,128)(2,1)}, bf16[16,4096]{1,0:T(8,128)(2,1)S(1)}, u32[]{:S(2)}, u32[]{:S(2)}) %collective-permute-start.4) | collective-permute-done | bytes 131104 | tf_op jit(solution)/shard_map/ppermute | solution.py:24
  26.7 1.9 %collective-permute-done.3.refs_4_ = bf16[16,4096]{1,0:T(8,128)(2,1)S(1)} collective-permute-done((bf16[16,4096]{1,0:T(8,128)(2,1)}, bf16[16,4096]{1,0:T(8,128)(2,1)S(1)}, u32[]{:S(2)}, u32[]{:S(2)}) %collective-permute-start.3) | collective-permute-done | bytes 131104 | tf_op jit(solution)/shard_map/ppermute | solution.py:24
  28.6 0.0 collective-permute-done.2.refs_3_
  28.6 1.2 %collective-permute-done.1.refs_2_ = bf16[16,4096]{1,0:T(8,128)(2,1)S(1)} collective-permute-done((bf16[16,4096]{1,0:T(8,128)(2,1)}, bf16[16,4096]{1,0:T(8,128)(2,1)S(1)}, u32[]{:S(2)}, u32[]{:S(2)}) %collective-permute-start.1) | collective-permute-done | bytes 131104 | tf_op jit(solution)/shard_map/ppermute | solution.py:24
  29.8 0.0 collective-permute-done.refs_1_
  29.8 0.0 copy-start.2
  29.8 0.9 copy-done.2
  30.7 8.3 %gate_up.3 = (f32[128,1024]{1,0:T(8,128)S(1)}, f32[128,1024]{1,0:T(8,128)S(1)}, bf16[2,128,1024]{2,1,0:T(8,128)(2,1)}) custom-call(bf16[16,4096]{1,0:T(8,128)(2,1)S(1)} %copy-done.2, bf16[16,4096]{1,0:T(8,128)(2,1)S(1)} %collective-permute-done.refs_1_, bf16[16,4096]{1,0:T(8,128)(2,1)S(1)} %collective-permute-done.1.refs_2_, ...), custom_call_target="tpu_custom_call" | custom-call | flops 2147483648 | bytes 16777216 | tf_op jit(solution)/shard_map/gate_up/pallas_call | solution.py:65
  39.0 0.0 copy-start.3
  39.0 0.8 copy-done.3
  39.8 0.8 copy-done.5
  40.6 0.0 slice-start.2
  40.6 0.0 slice-start.3
  40.6 0.1 collective-permute-start.8
  40.7 0.0 copy-start.1
  40.7 8.4 %gate_up.2 = (f32[128,1024]{1,0:T(8,128)S(1)}, f32[128,1024]{1,0:T(8,128)S(1)}, bf16[2,128,1024]{2,1,0:T(8,128)(2,1)S(1)}) custom-call(bf16[16,4096]{1,0:T(8,128)(2,1)S(1)} %copy-done.2, bf16[16,4096]{1,0:T(8,128)(2,1)S(1)} %collective-permute-done.refs_1_, bf16[16,4096]{1,0:T(8,128)(2,1)S(1)} %collective-permute-done.1.refs_2_, ...), custom_call_target="tpu_custom_call" | custom-call | flops 2147483648 | bytes 16777216 | tf_op jit(solution)/shard_map/gate_up/pallas_call | solution.py:65
  49.1 0.0 copy-start.9
  49.1 1.2 %collective-permute-start.7 = (bf16[2,128,1024]{2,1,0:T(8,128)(2,1)S(1)}, bf16[2,128,1024]{2,1,0:T(8,128)(2,1)S(1)}, u32[]{:S(2)}, u32[]{:S(2)}) collective-permute-start(bf16[2,128,1024]{2,1,0:T(8,128)(2,1)S(1)} %get-tuple-element.25), channel_id=1, source_target_pairs={{0,1},{1,0},{2,3},{3,2},{4,5},{5,4},{6,7},{7,6},{8,9},{9,8},{10,11... | collective-permute-start | bytes 1572872 | tf_op jit(solution)/shard_map/ppermute | solution.py:24
  50.3 0.0 collective-permute-done.8.refs_5_
  50.3 1.5 %collective-permute-done.7.refs_4_ = bf16[2,128,1024]{2,1,0:T(8,128)(2,1)S(1)} collective-permute-done((bf16[2,128,1024]{2,1,0:T(8,128)(2,1)S(1)}, bf16[2,128,1024]{2,1,0:T(8,128)(2,1)S(1)}, u32[]{:S(2)}, u32[]{:S(2)}) %collective-permute-start.7) | collective-permute-done | bytes 524320 | tf_op jit(solution)/shard_map/ppermute | solution.py:24
  51.9 0.0 copy-done.7
  51.9 0.0 copy-done.8
  51.9 2.2 %copy-done = bf16[64,16,2048]{2,1,0:T(8,128)(2,1)S(1)} copy-done((bf16[64,16,2048]{2,1,0:T(8,128)(2,1)S(1)}, bf16[64,16,2048]{2,1,0:T(8,128)(2,1)}, u32[]{:S(2)}) %copy-start) | copy-done | bytes 4194328
  54.0 1.0 copy-done.4
  55.1 1.0 copy-done.6
  56.1 3.0 %hidden_shrink.1 = (bf16[128,2048]{1,0:T(8,128)(2,1)S(1)}, f32[16,128]{1,0:T(8,128)S(1)}) custom-call(s32[128]{0:T(128)S(1)} %copy-done.7, s32[10]{0:T(128)S(1)} %copy-done.8, s32[1,128]{1,0:T(1,128)S(1)} %bitcast.3, f32[128,1024]{1,0:T(8,128)S(1)} %get-tuple-element.21.refs_0_, f32[128,1024]{1,0:T(8,128)S(1)} %copy-done.4, ...), custom_call_target="tpu_custom_call" | custom-call | tf_op jit(solution)/shard_map/hidden_shrink/pallas_call | solution.py:125
  59.2 0.8 collective-permute-start.9
  60.0 2.9 %collective-permute-done.9 = f32[16,128]{1,0:T(8,128)S(1)} collective-permute-done((f32[16,128]{1,0:T(8,128)S(1)}, f32[16,128]{1,0:T(8,128)S(1)}, u32[]{:S(2)}, u32[]{:S(2)}) %collective-permute-start.9) | collective-permute-done | bytes 8224 | tf_op jit(solution)/shard_map/ppermute | solution.py:24
  62.9 0.0 collective-permute-start.10
  62.9 3.6 %collective-permute-done.10 = f32[16,128]{1,0:T(8,128)S(1)} collective-permute-done((f32[16,128]{1,0:T(8,128)S(1)}, f32[16,128]{1,0:T(8,128)S(1)}, u32[]{:S(2)}, u32[]{:S(2)}) %collective-permute-start.10) | collective-permute-done | bytes 8224 | tf_op jit(solution)/shard_map/ppermute | solution.py:24
  66.6 1.0 collective-permute-start.11
  67.6 0.0 slice-done
  67.6 0.0 slice-done.1
  67.6 0.0 slice-done.2
  67.6 0.0 slice-done.3
  67.6 5.4 %down.1.base = f32[128,4096]{1,0:T(8,128)S(1)} custom-call(bf16[128,2048]{1,0:T(8,128)(2,1)S(1)} %get-tuple-element.28.hidden, bf16[2048,4096]{1,0:T(8,128)(2,1)S(1)} %bitcast.2), custom_call_target="tpu_custom_call" | custom-call | flops 2147483648 | bytes 16777216 | tf_op jit(solution)/shard_map/down/pallas_call | solution.py:150
  73.0 0.0 collective-permute-done.11
  73.0 0.0 copy-done.1
  73.0 0.0 copy-done.9
  73.1 4.1 %add_delta.1 = (bf16[16,4096]{1,0:T(8,128)(2,1)S(1)}, bf16[16,4096]{1,0:T(8,128)(2,1)S(1)}, bf16[16,4096]{1,0:T(8,128)(2,1)S(1)}, bf16[16,4096]{1,0:T(8,128)(2,1...) custom-call(s32[128]{0:T(128)S(1)} %copy-done.7, ...), custom_call_target="tpu_custom_call" | custom-call | tf_op jit(solution)/shard_map/add_delta/pallas_call | solution.py:191
  77.2 1.6 %collective-permute-start.12 = (bf16[16,4096]{1,0:T(8,128)(2,1)S(1)}, bf16[16,4096]{1,0:T(8,128)(2,1)S(1)}, u32[]{:S(2)}, u32[]{:S(2)}) collective-permute-start(bf16[16,4096]{1,0:T(8,128)(2,1)S(1)} %get-tuple-element.30), channel_id=1, source_target_pairs={{0,14},{2,12},{4,10},{6,8},{8,6},{10,4},{12,2},{14,0},{1,15},{3,13... | collective-permute-start | bytes 393224 | tf_op jit(solution)/shard_map/ppermute | solution.py:24
  78.8 2.3 %collective-permute-start.13 = (bf16[16,4096]{1,0:T(8,128)(2,1)S(1)}, bf16[16,4096]{1,0:T(8,128)(2,1)S(1)}, u32[]{:S(2)}, u32[]{:S(2)}) collective-permute-start(bf16[16,4096]{1,0:T(8,128)(2,1)S(1)} %get-tuple-element.31), channel_id=1, source_target_pairs={{0,12},{2,14},{4,8},{6,10},{8,4},{10,6},{12,0},{14,2},{1,13},{3,15... | collective-permute-start | bytes 393224 | tf_op jit(solution)/shard_map/ppermute | solution.py:24
  81.1 1.0 collective-permute-start.14
  82.1 2.8 %collective-permute-start.15 = (bf16[16,4096]{1,0:T(8,128)(2,1)S(1)}, bf16[16,4096]{1,0:T(8,128)(2,1)S(1)}, u32[]{:S(2)}, u32[]{:S(2)}) collective-permute-start(bf16[16,4096]{1,0:T(8,128)(2,1)S(1)} %get-tuple-element.33), channel_id=1, source_target_pairs={{0,8},{2,10},{4,12},{6,14},{8,0},{10,2},{12,4},{14,6},{1,9},{3,11}... | collective-permute-start | bytes 393224 | tf_op jit(solution)/shard_map/ppermute | solution.py:24
  84.9 0.3 collective-permute-start.16
  85.1 1.3 %collective-permute-done.12.refs_1_ = bf16[16,4096]{1,0:T(8,128)(2,1)S(1)} collective-permute-done((bf16[16,4096]{1,0:T(8,128)(2,1)S(1)}, bf16[16,4096]{1,0:T(8,128)(2,1)S(1)}, u32[]{:S(2)}, u32[]{:S(2)}) %collective-permute-start.12) | collective-permute-done | bytes 131104 | tf_op jit(solution)/shard_map/ppermute | solution.py:24
  86.4 9.7 %collective-permute-start.17 = (bf16[16,4096]{1,0:T(8,128)(2,1)S(1)}, bf16[16,4096]{1,0:T(8,128)(2,1)S(1)}, u32[]{:S(2)}, u32[]{:S(2)}) collective-permute-start(bf16[16,4096]{1,0:T(8,128)(2,1)S(1)} %get-tuple-element.35), channel_id=1, source_target_pairs={{0,4},{2,6},{4,0},{6,2},{8,12},{10,14},{12,8},{14,10},{1,5},{3,7},... | collective-permute-start | bytes 393224 | tf_op jit(solution)/shard_map/ppermute | solution.py:24
  96.2 0.0 collective-permute-done.13.refs_2_
  96.2 0.6 collective-permute-start.18
  96.8 4.2 %collective-permute-done.14.refs_3_ = bf16[16,4096]{1,0:T(8,128)(2,1)S(1)} collective-permute-done((bf16[16,4096]{1,0:T(8,128)(2,1)S(1)}, bf16[16,4096]{1,0:T(8,128)(2,1)S(1)}, u32[]{:S(2)}, u32[]{:S(2)}) %collective-permute-start.14) | collective-permute-done | bytes 131104 | tf_op jit(solution)/shard_map/ppermute | solution.py:24
  101.0 1.2 %collective-permute-done.15.refs_4_ = bf16[16,4096]{1,0:T(8,128)(2,1)S(1)} collective-permute-done((bf16[16,4096]{1,0:T(8,128)(2,1)S(1)}, bf16[16,4096]{1,0:T(8,128)(2,1)S(1)}, u32[]{:S(2)}, u32[]{:S(2)}) %collective-permute-start.15) | collective-permute-done | bytes 131104 | tf_op jit(solution)/shard_map/ppermute | solution.py:24
  102.2 0.0 collective-permute-done.16.refs_5_
  102.2 1.5 %collective-permute-done.17.refs_6_ = bf16[16,4096]{1,0:T(8,128)(2,1)S(1)} collective-permute-done((bf16[16,4096]{1,0:T(8,128)(2,1)S(1)}, bf16[16,4096]{1,0:T(8,128)(2,1)S(1)}, u32[]{:S(2)}, u32[]{:S(2)}) %collective-permute-start.17) | collective-permute-done | bytes 131104 | tf_op jit(solution)/shard_map/ppermute | solution.py:24
  103.7 0.0 collective-permute-done.18.refs_7_
  103.7 0.8 sum_rows.1
  (12 shorter events, 0.0 us)
Async XLA Ops:
  0.0 11.3 %collective-permute-start.6 = (bf16[16,4096]{1,0:T(8,128)(2,1)}, bf16[16,4096]{1,0:T(8,128)(2,1)S(1)}, u32[]{:S(2)}, u32[]{:S(2)}) collective-permute-start(bf16[16,4096]{1,0:T(8,128)(2,1)} %refs_0_.3), channel_id=1, source_target_pairs={{0,14},{2,12},{4,10},{6,8},{8,6},{10,4},{12,2},{14,0},{1,15},{3,13... | collective-permute-start | bytes 393224 | tf_op jit(solution)/shard_map/ppermute | solution.py:24
  6.0 15.9 %collective-permute-start.5 = (bf16[16,4096]{1,0:T(8,128)(2,1)}, bf16[16,4096]{1,0:T(8,128)(2,1)S(1)}, u32[]{:S(2)}, u32[]{:S(2)}) collective-permute-start(bf16[16,4096]{1,0:T(8,128)(2,1)} %refs_0_.3), channel_id=1, source_target_pairs={{0,12},{2,14},{4,8},{6,10},{8,4},{10,6},{12,0},{14,2},{1,13},{3,15... | collective-permute-start | bytes 393224 | tf_op jit(solution)/shard_map/ppermute | solution.py:24
  6.2 20.5 %collective-permute-start.4 = (bf16[16,4096]{1,0:T(8,128)(2,1)}, bf16[16,4096]{1,0:T(8,128)(2,1)S(1)}, u32[]{:S(2)}, u32[]{:S(2)}) collective-permute-start(bf16[16,4096]{1,0:T(8,128)(2,1)} %refs_0_.3), channel_id=1, source_target_pairs={{0,10},{2,8},{4,14},{6,12},{8,2},{10,0},{12,6},{14,4},{1,11},{3,9}... | collective-permute-start | bytes 393224 | tf_op jit(solution)/shard_map/ppermute | solution.py:24
  7.0 21.6 %collective-permute-start.3 = (bf16[16,4096]{1,0:T(8,128)(2,1)}, bf16[16,4096]{1,0:T(8,128)(2,1)S(1)}, u32[]{:S(2)}, u32[]{:S(2)}) collective-permute-start(bf16[16,4096]{1,0:T(8,128)(2,1)} %refs_0_.3), channel_id=1, source_target_pairs={{0,8},{2,10},{4,12},{6,14},{8,0},{10,2},{12,4},{14,6},{1,9},{3,11}... | collective-permute-start | bytes 393224 | tf_op jit(solution)/shard_map/ppermute | solution.py:24
  8.9 19.7 %collective-permute-start.2 = (bf16[16,4096]{1,0:T(8,128)(2,1)}, bf16[16,4096]{1,0:T(8,128)(2,1)S(1)}, u32[]{:S(2)}, u32[]{:S(2)}) collective-permute-start(bf16[16,4096]{1,0:T(8,128)(2,1)} %refs_0_.3), channel_id=1, source_target_pairs={{0,6},{2,4},{4,2},{6,0},{8,14},{10,12},{12,10},{14,8},{1,7},{3,5},... | collective-permute-start | bytes 393224 | tf_op jit(solution)/shard_map/ppermute | solution.py:24
  11.3 18.6 %collective-permute-start.1 = (bf16[16,4096]{1,0:T(8,128)(2,1)}, bf16[16,4096]{1,0:T(8,128)(2,1)S(1)}, u32[]{:S(2)}, u32[]{:S(2)}) collective-permute-start(bf16[16,4096]{1,0:T(8,128)(2,1)} %refs_0_.3), channel_id=1, source_target_pairs={{0,4},{2,6},{4,0},{6,2},{8,12},{10,14},{12,8},{14,10},{1,5},{3,7},... | collective-permute-start | bytes 393224 | tf_op jit(solution)/shard_map/ppermute | solution.py:24
  21.9 7.9 %collective-permute-start = (bf16[16,4096]{1,0:T(8,128)(2,1)}, bf16[16,4096]{1,0:T(8,128)(2,1)S(1)}, u32[]{:S(2)}, u32[]{:S(2)}) collective-permute-start(bf16[16,4096]{1,0:T(8,128)(2,1)} %refs_0_.3), channel_id=1, source_target_pairs={{0,2},{2,0},{4,6},{6,4},{8,10},{10,8},{12,14},{14,12},{1,3},{3,1},... | collective-permute-start | bytes 393224 | tf_op jit(solution)/shard_map/ppermute | solution.py:24
  29.8 0.9 copy-start.2
  39.0 0.8 copy-start.3
  39.8 0.8 copy-start.5
  40.6 27.0 %slice-start = ((s8[16777216]{0:T(1024)(128)(4,1)}), s8[4194304]{0:T(1024)(128)(4,1)S(1)}, s32[]{:S(2)}) async-start(s8[16777216]{0:T(1024)(128)(4,1)} %bitcast.1), calls=%async_computation | async-start | bytes 8388608
  40.6 11.2 %copy-start.7 = (s32[128]{0:T(128)S(1)}, s32[128]{0:T(128)}, u32[]{:S(2)}) copy-start(s32[128]{0:T(128)} %row_adapter.3) | copy-start | bytes 1540
  40.6 11.2 %copy-start.8 = (s32[10]{0:T(128)S(1)}, s32[10]{0:T(128)}, u32[]{:S(2)}) copy-start(s32[10]{0:T(128)} %block_first.3) | copy-start | bytes 124
  40.6 27.0 %slice-start.1 = ((s8[16777216]{0:T(1024)(128)(4,1)}), s8[4194304]{0:T(1024)(128)(4,1)S(1)}, s32[]{:S(2)}) async-start(s8[16777216]{0:T(1024)(128)(4,1)} %bitcast.1), calls=%async_computation.1 | async-start | bytes 8388608
  40.6 27.0 %slice-start.2 = ((s8[16777216]{0:T(1024)(128)(4,1)}), s8[4194304]{0:T(1024)(128)(4,1)S(1)}, s32[]{:S(2)}) async-start(s8[16777216]{0:T(1024)(128)(4,1)} %bitcast.1), calls=%async_computation.2 | async-start | bytes 8388608
  40.6 27.0 %slice-start.3 = ((s8[16777216]{0:T(1024)(128)(4,1)}), s8[4194304]{0:T(1024)(128)(4,1)S(1)}, s32[]{:S(2)}) async-start(s8[16777216]{0:T(1024)(128)(4,1)} %bitcast.1), calls=%async_computation.3 | async-start | bytes 8388608
  40.6 9.7 %collective-permute-start.8 = (bf16[2,128,1024]{2,1,0:T(8,128)(2,1)}, bf16[2,128,1024]{2,1,0:T(8,128)(2,1)}, u32[]{:S(2)}, u32[]{:S(2)}) collective-permute-start(bf16[2,128,1024]{2,1,0:T(8,128)(2,1)} %get-tuple-element.26), channel_id=1, source_target_pairs={{0,1},{1,0},{2,3},{3,2},{4,5},{5,4},{6,7},{7,6},{8,9},{9,8},{10,11... | collective-permute-start | bytes 1572872 | tf_op jit(solution)/shard_map/ppermute | solution.py:24
  40.7 32.3 %copy-start.1 = (bf16[8,16,4096]{2,1,0:T(8,128)(2,1)S(1)}, bf16[8,16,4096]{2,1,0:T(8,128)(2,1)}, u32[]{:S(2)}) copy-start(bf16[8,16,4096]{2,1,0:T(8,128)(2,1)} %adapter_up.1) | copy-start | bytes 3145732
  49.1 23.9 %copy-start.9 = (s32[64]{0:T(128)S(1)}, s32[64]{0:T(128)}, u32[]{:S(2)}) copy-start(s32[64]{0:T(128)} %page_table.1) | copy-start | bytes 772
  49.1 2.7 %collective-permute-start.7 = (bf16[2,128,1024]{2,1,0:T(8,128)(2,1)S(1)}, bf16[2,128,1024]{2,1,0:T(8,128)(2,1)S(1)}, u32[]{:S(2)}, u32[]{:S(2)}) collective-permute-start(bf16[2,128,1024]{2,1,0:T(8,128)(2,1)S(1)} %get-tuple-element.25), channel_id=1, source_target_pairs={{0,1},{1,0},{2,3},{3,2},{4,5},{5,4},{6,7},{7,6},{8,9},{9,8},{10,11... | collective-permute-start | bytes 1572872 | tf_op jit(solution)/shard_map/ppermute | solution.py:24
  51.9 2.2 %copy-start = (bf16[64,16,2048]{2,1,0:T(8,128)(2,1)S(1)}, bf16[64,16,2048]{2,1,0:T(8,128)(2,1)}, u32[]{:S(2)}) copy-start(bf16[64,16,2048]{2,1,0:T(8,128)(2,1)} %refs_6_.1) | copy-start | bytes 12582916
  54.0 1.0 copy-start.4
  55.1 1.0 copy-start.6
  59.2 3.7 %collective-permute-start.9 = (f32[16,128]{1,0:T(8,128)S(1)}, f32[16,128]{1,0:T(8,128)S(1)}, u32[]{:S(2)}, u32[]{:S(2)}) collective-permute-start(f32[16,128]{1,0:T(8,128)S(1)} %get-tuple-element.27), channel_id=1, source_target_pairs={{0,2},{2,0},{4,6},{6,4},{8,10},{10,8},{12,14},{14,12},{1,3},{3,1},... | collective-permute-start | bytes 24584 | tf_op jit(solution)/shard_map/ppermute | solution.py:24
  62.9 3.7 %collective-permute-start.10 = (f32[16,128]{1,0:T(8,128)S(1)}, f32[16,128]{1,0:T(8,128)S(1)}, u32[]{:S(2)}, u32[]{:S(2)}) collective-permute-start(f32[16,128]{1,0:T(8,128)S(1)} %add.9), channel_id=1, source_target_pairs={{0,4},{2,6},{4,0},{6,2},{8,12},{10,14},{12,8},{14,10},{1,5},{3,7},... | collective-permute-start | bytes 24584 | tf_op jit(solution)/shard_map/ppermute | solution.py:24
  66.6 6.4 %collective-permute-start.11 = (f32[16,128]{1,0:T(8,128)S(1)}, f32[16,128]{1,0:T(8,128)S(1)}, u32[]{:S(2)}, u32[]{:S(2)}) collective-permute-start(f32[16,128]{1,0:T(8,128)S(1)} %add.10), channel_id=1, source_target_pairs={{0,8},{2,10},{4,12},{6,14},{8,0},{10,2},{12,4},{14,6},{1,9},{3,11}... | collective-permute-start | bytes 24584 | tf_op jit(solution)/shard_map/ppermute | solution.py:24
  77.2 9.3 %collective-permute-start.12 = (bf16[16,4096]{1,0:T(8,128)(2,1)S(1)}, bf16[16,4096]{1,0:T(8,128)(2,1)S(1)}, u32[]{:S(2)}, u32[]{:S(2)}) collective-permute-start(bf16[16,4096]{1,0:T(8,128)(2,1)S(1)} %get-tuple-element.30), channel_id=1, source_target_pairs={{0,14},{2,12},{4,10},{6,8},{8,6},{10,4},{12,2},{14,0},{1,15},{3,13... | collective-permute-start | bytes 393224 | tf_op jit(solution)/shard_map/ppermute | solution.py:24
  78.8 17.4 %collective-permute-start.13 = (bf16[16,4096]{1,0:T(8,128)(2,1)S(1)}, bf16[16,4096]{1,0:T(8,128)(2,1)S(1)}, u32[]{:S(2)}, u32[]{:S(2)}) collective-permute-start(bf16[16,4096]{1,0:T(8,128)(2,1)S(1)} %get-tuple-element.31), channel_id=1, source_target_pairs={{0,12},{2,14},{4,8},{6,10},{8,4},{10,6},{12,0},{14,2},{1,13},{3,15... | collective-permute-start | bytes 393224 | tf_op jit(solution)/shard_map/ppermute | solution.py:24
  81.1 19.9 %collective-permute-start.14 = (bf16[16,4096]{1,0:T(8,128)(2,1)S(1)}, bf16[16,4096]{1,0:T(8,128)(2,1)S(1)}, u32[]{:S(2)}, u32[]{:S(2)}) collective-permute-start(bf16[16,4096]{1,0:T(8,128)(2,1)S(1)} %get-tuple-element.32), channel_id=1, source_target_pairs={{0,10},{2,8},{4,14},{6,12},{8,2},{10,0},{12,6},{14,4},{1,11},{3,9}... | collective-permute-start | bytes 393224 | tf_op jit(solution)/shard_map/ppermute | solution.py:24
  82.1 20.1 %collective-permute-start.15 = (bf16[16,4096]{1,0:T(8,128)(2,1)S(1)}, bf16[16,4096]{1,0:T(8,128)(2,1)S(1)}, u32[]{:S(2)}, u32[]{:S(2)}) collective-permute-start(bf16[16,4096]{1,0:T(8,128)(2,1)S(1)} %get-tuple-element.33), channel_id=1, source_target_pairs={{0,8},{2,10},{4,12},{6,14},{8,0},{10,2},{12,4},{14,6},{1,9},{3,11}... | collective-permute-start | bytes 393224 | tf_op jit(solution)/shard_map/ppermute | solution.py:24
  84.9 17.3 %collective-permute-start.16 = (bf16[16,4096]{1,0:T(8,128)(2,1)S(1)}, bf16[16,4096]{1,0:T(8,128)(2,1)S(1)}, u32[]{:S(2)}, u32[]{:S(2)}) collective-permute-start(bf16[16,4096]{1,0:T(8,128)(2,1)S(1)} %get-tuple-element.34), channel_id=1, source_target_pairs={{0,6},{2,4},{4,2},{6,0},{8,14},{10,12},{12,10},{14,8},{1,7},{3,5},... | collective-permute-start | bytes 393224 | tf_op jit(solution)/shard_map/ppermute | solution.py:24
  86.4 17.2 %collective-permute-start.17 = (bf16[16,4096]{1,0:T(8,128)(2,1)S(1)}, bf16[16,4096]{1,0:T(8,128)(2,1)S(1)}, u32[]{:S(2)}, u32[]{:S(2)}) collective-permute-start(bf16[16,4096]{1,0:T(8,128)(2,1)S(1)} %get-tuple-element.35), channel_id=1, source_target_pairs={{0,4},{2,6},{4,0},{6,2},{8,12},{10,14},{12,8},{14,10},{1,5},{3,7},... | collective-permute-start | bytes 393224 | tf_op jit(solution)/shard_map/ppermute | solution.py:24
  96.2 7.5 %collective-permute-start.18 = (bf16[16,4096]{1,0:T(8,128)(2,1)S(1)}, bf16[16,4096]{1,0:T(8,128)(2,1)S(1)}, u32[]{:S(2)}, u32[]{:S(2)}) collective-permute-start(bf16[16,4096]{1,0:T(8,128)(2,1)S(1)} %get-tuple-element.36), channel_id=1, source_target_pairs={{0,2},{2,0},{4,6},{6,4},{8,10},{10,8},{12,14},{14,12},{1,3},{3,1},... | collective-permute-start | bytes 393224 | tf_op jit(solution)/shard_map/ppermute | solution.py:24

commit v2 on v0

v2 whole, which is shorter than its diff:
```python
import functools

import jax
import jax.numpy as jnp
from jax import lax
from jax.experimental import pallas as pl
from jax.experimental.pallas import tpu as pltpu
from jax.sharding import PartitionSpec as P

BLOCK = 128
LIMIT = 6
MIB = 1 << 20

SMEM = pl.BlockSpec(memory_space=pltpu.SMEM)
VMEM = pl.BlockSpec(memory_space=pltpu.VMEM)
ANY = pl.BlockSpec(memory_space=pl.ANY)
HBM = pl.BlockSpec(memory_space=pltpu.HBM)


def dot(a, b, dims=((1,), (0,))):
    return lax.dot_general(a, b, (dims, ((), ())), preferred_element_type=jnp.float32)


def swap(x, axis, n, k):
    return lax.ppermute(x, axis, [(i, i ^ k) for i in range(n)])


def reorder(x, me, n, width):
    lanes = n * width
    at = lax.broadcasted_iota(jnp.int32, x.shape, 1) // width
    bit = 1
    while bit < n:
        low = (at & bit) == 0
        other = jnp.where(low, pltpu.roll(x, lanes - bit * width, 1), pltpu.roll(x, bit * width, 1))
        x = jnp.where((me & bit) != 0, other, x)
        bit *= 2
    return x


def stay(x):
    return pltpu.with_memory_space_constraint(x, pltpu.HBM)


def half_columns(width, other):
    half = lax.axis_index("tensor")
    start = ((1 - half) if other else half) * width
    return pl.ds(pl.multiple_of(start, 128), width)


def copies(source, out, columns, sems, steps=4):
    rows = out.shape[0] // steps
    parts = [pl.ds(i * rows, rows) for i in range(steps)]
    return [
        pltpu.make_async_copy(source.at[part, columns], out.at[part], sems.at[i]) for i, part in enumerate(parts)
    ]


def weight_moves(weight, sent, kept, sems):
    width = sent.shape[1]
    return copies(weight, sent, half_columns(width, True), sems.at[0]) + copies(
        weight, kept, half_columns(width, False), sems.at[1]
    )


def gate_fetch_kernel(weight, adapter_up, sent, kept, up_x, up_z, sems, up_sems):
    width = up_x.shape[2]
    moves = weight_moves(weight, sent, kept, sems)
    for h, out in enumerate((up_x, up_z)):
        moves.append(pltpu.make_async_copy(adapter_up.at[:, :, pl.ds(h * width, width)], out, up_sems.at[h]))
    for move in moves:
        move.start()
    for move in moves:
        move.wait()


def fetch_gate(weight, adapter_up):
    depth, width = weight.shape
    half = jax.ShapeDtypeStruct((depth, width // 2), weight.dtype)
    slots, rank, out_width = adapter_up.shape
    pages = jax.ShapeDtypeStruct((slots, rank, out_width // 2), adapter_up.dtype)
    return pl.pallas_call(
        gate_fetch_kernel,
        in_specs=[HBM, HBM],
        out_specs=[VMEM] * 4,
        out_shape=[half, half, pages, pages],
        scratch_shapes=[pltpu.SemaphoreType.DMA((2, 4)), pltpu.SemaphoreType.DMA((2,))],
        compiler_params=pltpu.CompilerParams(vmem_limit_bytes=LIMIT * MIB),
        cost_estimate=pl.CostEstimate(flops=0, bytes_accessed=2 * weight.size, transcendentals=0),
        name="fetch_gate",
    )(stay(weight), stay(adapter_up))


def up_fetch_kernel(row_adapter, block_first, after, weight, adapter_down, sent, kept, factors, sems, block_sems):
    count, rank = block_first.shape[0], adapter_down.shape[1]
    moves = weight_moves(weight, sent, kept, sems)
    for b in range(count):
        adapter = row_adapter[jnp.minimum(block_first[b], row_adapter.shape[0] - 1)]
        place = factors.at[pl.ds(b * rank, rank)]
        moves.append(pltpu.make_async_copy(adapter_down.at[adapter], place, block_sems.at[b]))
    for move in moves:
        move.start()
    for move in moves:
        move.wait()


def fetch_up(row_adapter, block_first, after, weight, adapter_down):
    depth, width = weight.shape
    half = jax.ShapeDtypeStruct((depth, width // 2), weight.dtype)
    count, (_, rank, hidden_local) = block_first.shape[0], adapter_down.shape
    return pl.pallas_call(
        up_fetch_kernel,
        in_specs=[SMEM, SMEM, ANY, HBM, HBM],
        out_specs=[VMEM] * 3,
        out_shape=[half, half, jax.ShapeDtypeStruct((count * rank, hidden_local), adapter_down.dtype)],
        scratch_shapes=[pltpu.SemaphoreType.DMA((2, 4)), pltpu.SemaphoreType.DMA((count,))],
        compiler_params=pltpu.CompilerParams(vmem_limit_bytes=LIMIT * MIB),
        cost_estimate=pl.CostEstimate(flops=0, bytes_accessed=0, transcendentals=0),
        name="fetch_up",
    )(row_adapter, block_first, after, stay(weight), stay(adapter_down))


def multiply(x, gate, up, out):
    width = out.shape[2]
    tile = min(256, width)
    for j in range(0, width, tile):
        out[0, :, j : j + tile] = dot(x[...], gate[:, j : j + tile])
        out[1, :, j : j + tile] = dot(x[...], up[:, j : j + tile])


def gate_up_kernel(n, *refs):
    xs, (gate, up, out, *rest) = refs[:n], refs[n:]
    x = xs[0]
    if rest:
        (x,) = rest
        rows = xs[0].shape[0]
        for k in range(n):
            x[k * rows : (k + 1) * rows, :] = xs[k][...]
    multiply(x, gate, up, out)


def gate_up(xs, gate, up):
    total, (depth, width) = sum(x.shape[0] for x in xs), gate.shape
    out = [jax.ShapeDtypeStruct((2, total, width), jnp.float32)]
    if len(xs) > 1:
        out.append(jax.ShapeDtypeStruct((total, depth), jnp.bfloat16))
    return pl.pallas_call(
        functools.partial(gate_up_kernel, len(xs)),
        in_specs=[VMEM] * (len(xs) + 2),
        out_specs=[VMEM] * len(out),
        out_shape=out,
        compiler_params=pltpu.CompilerParams(vmem_limit_bytes=LIMIT * MIB),
        cost_estimate=pl.CostEstimate(flops=0, bytes_accessed=0, transcendentals=0),
        name="gate_up",
    )(*xs, gate, up)


def silu_kernel(kept, got, hidden):
    step = 16

    @pl.loop(0, hidden.shape[0] // step)
    def _(i):
        rows = pl.ds(pl.multiple_of(i * step, step), step)
        g = kept[0, rows] + got[0, rows]
        u = kept[1, rows] + got[1, rows]
        hidden[rows] = (g / (1.0 + jnp.exp(-g)) * u).astype(hidden.dtype)


def silu(kept, got):
    return pl.pallas_call(
        silu_kernel,
        in_specs=[VMEM, VMEM],
        out_specs=VMEM,
        out_shape=jax.ShapeDtypeStruct(kept.shape[1:], jnp.bfloat16),
        compiler_params=pltpu.CompilerParams(vmem_limit_bytes=LIMIT * MIB),
        cost_estimate=pl.CostEstimate(flops=0, bytes_accessed=0, transcendentals=0),
        name="silu",
    )(kept, got)


def block_mask(b, ids, adapters, row_adapter, block_first):
    opening = block_first[b]
    adapter = row_adapter[jnp.minimum(opening, row_adapter.shape[0] - 1)]
    inside = (ids >= opening) & (ids < opening + BLOCK) & (adapters == adapter)
    return inside, adapter


def shrink_kernel(n, row_adapter, block_first, adapters, mine, other, factors, shrunk):
    count = block_first.shape[0]
    rank = factors.shape[0] // count
    width = mine.shape[1]
    half = lax.axis_index("tensor")
    first = pl.ds(pl.multiple_of(half * width, 128), width)
    second = pl.ds(pl.multiple_of((1 - half) * width, 128), width)
    terms = dot(factors[:, first], mine[...], ((1,), (1,))) + dot(factors[:, second], other[...], ((1,), (1,)))
    total = jnp.zeros((rank, terms.shape[1]), jnp.float32)
    me = lax.axis_index("wide")
    rows = terms.shape[1] // n
    terms = reorder(terms, me, n, rows)
    ids = lax.broadcasted_iota(jnp.int32, (1, terms.shape[1]), 1)
    for b in range(count):
        inside, _ = block_mask(b, ids, adapters[...], row_adapter, block_first)
        total = total + jnp.where(inside, terms[b * rank : (b + 1) * rank], 0.0)
    shrunk[...] = total


def shrink(n, row_adapter, block_first, mine, other, factors):
    total = mine.shape[0]
    count = block_first.shape[0]
    return pl.pallas_call(
        functools.partial(shrink_kernel, n),
        in_specs=[SMEM, SMEM, VMEM, VMEM, VMEM, VMEM],
        out_specs=VMEM,
        out_shape=jax.ShapeDtypeStruct((factors.shape[0] // count, total), jnp.float32),
        compiler_params=pltpu.CompilerParams(vmem_limit_bytes=LIMIT * MIB),
        cost_estimate=pl.CostEstimate(flops=0, bytes_accessed=0, transcendentals=0),
        name="shrink",
    )(row_adapter, block_first, row_adapter.reshape(1, -1), mine, other, factors)


def relays(n):
    plan = []
    for mask in (1, 2):
        plan.append((mask, [k for k in range(1, n) if k & mask and k != mask], [k for k in range(1, n) if not k & mask]))
    return plan


def down_kernel(n, h, mine, other, weight, base, raw, tiles, sems):
    total, depth = mine.shape
    rows = total // n
    half = lax.axis_index("tensor")
    first = pl.ds(pl.multiple_of(half * depth, 128), depth)
    second = pl.ds(pl.multiple_of((1 - half) * depth, 128), depth)
    count, _, tile = tiles.shape
    width = count * tile

    def copy(j):
        return pltpu.make_async_copy(weight.at[:, pl.ds(h * width + j * tile, tile)], tiles.at[j], sems.at[j])

    for j in range(count):
        copy(j).start()
    for j in range(count):
        copy(j).wait()
        columns = slice(j * tile, (j + 1) * tile)
        result = dot(mine[...], tiles[j, first]) + dot(other[...], tiles[j, second])
        base[:, columns] = result
        for i, k in enumerate(relays(n)[h][1]):
            raw[i * rows : (i + 1) * rows, columns] = result[k * rows : (k + 1) * rows].astype(raw.dtype)


def down(n, h, mine, other, weight):
    total, depth = mine.shape
    width = weight.shape[1] // 2
    tile = min(512, width)
    sent = relays(n)[h][1]
    return pl.pallas_call(
        functools.partial(down_kernel, n, h),
        in_specs=[VMEM, VMEM, HBM],
        out_specs=[VMEM] * 2,
        out_shape=[
            jax.ShapeDtypeStruct((total, width), jnp.float32),
            jax.ShapeDtypeStruct((len(sent) * total // n, width), jnp.bfloat16),
        ],
        scratch_shapes=[
            pltpu.VMEM((width // tile, 2 * depth, tile), weight.dtype),
            pltpu.SemaphoreType.DMA((width // tile,)),
        ],
        compiler_params=pltpu.CompilerParams(vmem_limit_bytes=(LIMIT + 8) * MIB),
        cost_estimate=pl.CostEstimate(flops=0, bytes_accessed=0, transcendentals=0),
        name="down",
    )(mine, other, stay(weight))


def kept_blocks(n):
    (_, _, one), (_, _, two) = relays(n)
    whole = [k for k in range(n) if k < 3 or (k in one and k in two)]
    halves = [[k for k in kept if k not in whole] for kept in (one, two)]
    return whole, halves


def delta_kernel(n, row_adapter, block_first, page_table, adapters, shrunk, up_x, up_z, next_x, next_z, base_x, base_z, *refs):
    refs = list(refs)
    plan = relays(n)
    whole, halves = kept_blocks(n)
    raws = [refs.pop(0) for _ in plan]
    places = [{k ^ mask: i for i, k in enumerate(sent)} for mask, sent, _ in plan]
    full = {k: refs.pop(0) for k in whole}
    part = [{k: refs.pop(0) for k in ks} for ks in halves]
    (spread,) = refs
    me = lax.axis_index("wide")
    slots, rank, _ = up_x.shape
    width = 2 * base_x.shape[1]
    total = shrunk.shape[1]
    rows = total // n
    ids = lax.broadcasted_iota(jnp.int32, (1, total), 1)
    page = jnp.full((1, total), -1, jnp.int32)
    for b in range(block_first.shape[0]):
        inside, adapter = block_mask(b, ids, adapters[...], row_adapter, block_first)
        page = jnp.where(inside, page_table[adapter], page)
    page = reorder(page, me, n, rows)
    mine = reorder(shrunk[...].astype(jnp.bfloat16).astype(jnp.float32), me, n, rows)
    block = ids // rows
    size = slots * rank
    for s in range(slots):
        own = page == me * slots + s
        spread[s * rank : (s + 1) * rank] = jnp.where(own, mine, 0.0)
        for h, (mask, _, _) in enumerate(plan):
            near = (page == (me ^ mask) * slots + s) & (block > 0) & ((block & mask) == 0)
            at = (h + 1) * size + s * rank
            spread[at : at + rank] = jnp.where(near, mine, 0.0)
    factor = spread[...].T.astype(jnp.bfloat16)
    tile = min(1024, width // 2)
    for h, (base, ups, near) in enumerate(((base_x, up_x, next_x), (base_z, up_z, next_z))):
        for j in range(0, width // 2, tile):
            local = slice(j, j + tile)
            columns = slice(h * (width // 2) + j, h * (width // 2) + j + tile)
            result = base[:, local] + dot(factor[:, :size], ups[:, :, local].reshape(size, tile))
            result = result + dot(factor[:, (h + 1) * size : (h + 2) * size], near[:, :, local].reshape(size, tile))
            for k in whole + halves[h]:
                term = result[k * rows : (k + 1) * rows]
                if k in places[h]:
                    at = places[h][k] * rows
                    term = term + raws[h][at : at + rows, local].astype(jnp.float32)
                if k in full:
                    full[k][:, columns] = term.astype(jnp.bfloat16)
                else:
                    part[h][k][:, local] = term.astype(jnp.bfloat16)


def add_delta(n, row_adapter, block_first, page_table, shrunk, ups, nears, bases, raws):
    total, width = bases[0].shape[0], 2 * bases[0].shape[1]
    slots, rank, _ = ups[0].shape
    rows = total // n
    whole, halves = kept_blocks(n)
    block = lambda columns: jax.ShapeDtypeStruct((rows, columns), jnp.bfloat16)
    outs = pl.pallas_call(
        functools.partial(delta_kernel, n),
        in_specs=[SMEM, SMEM, SMEM] + [VMEM] * (8 + len(raws)),
        out_specs=[VMEM] * (len(whole) + len(halves[0]) + len(halves[1])),
        out_shape=[block(width)] * len(whole) + [block(width // 2)] * (len(halves[0]) + len(halves[1])),
        scratch_shapes=[pltpu.VMEM((3 * slots * rank, total), jnp.float32)],
        compiler_params=pltpu.CompilerParams(vmem_limit_bytes=LIMIT * MIB),
        name="add_delta",
    )(
        row_adapter, block_first, page_table, row_adapter.reshape(1, -1), shrunk, *ups, *nears, *bases, *raws,
    )
    return outs[: len(whole)], outs[len(whole) : len(whole) + len(halves[0])], outs[len(whole) + len(halves[0]) :]


def sum_kernel(count, *refs):
    wholes, parts, out = refs[: count[0]], refs[count[0] : -1], refs[-1]
    width = out.shape[1] // 2
    for h in range(2):
        columns = slice(h * width, (h + 1) * width)
        total = wholes[0][:, columns].astype(jnp.float32)
        for term in wholes[1:]:
            total = total + term[:, columns].astype(jnp.float32)
        for term in parts[: count[1]] if h == 0 else parts[count[1] :]:
            total = total + term[...].astype(jnp.float32)
        out[:, columns] = total.astype(out.dtype)


def add_up(wholes, firsts, seconds):
    return pl.pallas_call(
        functools.partial(sum_kernel, (len(wholes), len(firsts))),
        in_specs=[VMEM] * (len(wholes) + len(firsts) + len(seconds)),
        out_specs=VMEM,
        out_shape=jax.ShapeDtypeStruct(wholes[0].shape, jnp.bfloat16),
        compiler_params=pltpu.CompilerParams(vmem_limit_bytes=LIMIT * MIB),
        name="sum_rows",
    )(*wholes, *firsts, *seconds)


def plus_kernel(a, b, out):
    out[...] = a[...] + b[...]


def plus(a, b):
    return pl.pallas_call(
        plus_kernel,
        in_specs=[VMEM, VMEM],
        out_specs=VMEM,
        out_shape=jax.ShapeDtypeStruct(a.shape, a.dtype),
        compiler_params=pltpu.CompilerParams(vmem_limit_bytes=LIMIT * MIB),
        cost_estimate=pl.CostEstimate(flops=0, bytes_accessed=0, transcendentals=0),
        name="plus",
    )(a, b)


def local(
    n,
    tokens,
    gate_weight,
    up_weight,
    down_weight,
    adapter_down,
    adapter_up,
    row_adapter,
    block_first,
    page_table,
):
    blocks = [tokens] + [None] * (n - 1)
    far = [k for k in range(4, n) if k % 2 == 0]
    for k in far + [1, 2, 3]:
        blocks[k] = swap(tokens, "wide", n, k)
    gate_sent, gate_kept, *ups = fetch_gate(gate_weight, adapter_up)
    last = far[-1]
    blocks[last], *ups = lax.optimization_barrier((blocks[last], *ups))
    for k in far:
        blocks[k ^ 1] = swap(blocks[k], "wide", n, 1)
    blocks[last], *blocks[1:4] = lax.optimization_barrier((blocks[last], *blocks[1:4]))
    up_sent, up_kept, factors = fetch_up(row_adapter, block_first, blocks[last], up_weight, adapter_down)
    sent, x = gate_up(blocks, gate_sent, up_sent)
    got = swap(sent, "tensor", 2, 1)
    nears = [swap(piece, "wide", n, mask) for piece, (mask, _, _) in zip(ups, relays(n))]
    (kept,) = gate_up([x], gate_kept, up_kept)
    mine = silu(kept, got)
    other = swap(mine, "tensor", 2, 1)
    shrunk = shrink(n, row_adapter, block_first, mine, other, factors)
    arrived = swap(shrunk, "wide", n, 1)
    shrunk, mine = lax.optimization_barrier((shrunk, mine))
    bases, raws = [], []
    for h in range(2):
        base, raw = down(n, h, mine, other, down_weight)
        mine, base, raw = lax.optimization_barrier((mine, base, raw))
        bases.append(base)
        raws.append(raw)
    arrived, *rest = lax.optimization_barrier((arrived, *bases, *raws, *nears))
    bases, raws, nears = rest[:2], rest[2:4], rest[4:]
    shrunk = plus(shrunk, arrived)
    raws = [swap(raw, "wide", n, mask) for raw, (mask, _, _) in zip(raws, relays(n))]
    bit = 2
    while bit < n:
        shrunk = plus(shrunk, swap(shrunk, "wide", n, bit))
        bit *= 2
    parts = add_delta(n, row_adapter, block_first, page_table, shrunk, ups, nears, bases, raws)
    whole, halves = kept_blocks(n)
    arrived = {}
    for ks, xs in reversed(list(zip([whole] + halves, parts))):
        for k, block in reversed(list(zip(ks, xs))):
            arrived[k] = block if k == 0 else swap(block, "wide", n, k)
    arrived = [[arrived[k] for k in ks] for ks in [whole] + halves]
    return add_up(*arrived)


def solution(mesh):
    in_specs = (
        P(("parts", "wide"), "tensor"),
        P("tensor", "wide"),
        P("tensor", "wide"),
        P("wide", "tensor"),
        P("parts", None, "wide"),
        P(("parts", "wide"), None, "tensor"),
        P("parts"),
        P("parts"),
        P("parts"),
    )
    out_specs = P(("parts", "wide"), "tensor")
    body = functools.partial(local, mesh.shape["wide"])
    return jax.shard_map(body, mesh=mesh, in_specs=in_specs, out_specs=out_specs, check_vma=False)
```

time: 257 us -> 73.5 us (0.29)
  waiting for transfers between devices: 110 us -> 16 us
  loops' own time: 39.4 us -> 0 us
  between operations: 33.4 us -> 0.2 us
  matrix products: 32.5 us -> 0 us
  Pallas kernels: 0 us -> 29.5 us
  starting transfers between devices: 0.12 us -> 27.7 us
  local copies, waits for them, and re-layouts: 26.9 us -> 0.02 us
  other arithmetic: 12.7 us -> 0 us
    reduce_scatter x1 -> x0, waiting for transfers between devices: 63.5 us -> none  [local(): lax.psum_scatter(jnp.concatenate([base_term, shrink_terms], axis=1), 'wid...]
    all_gather x1 -> x0, waiting for transfers between devices: 45.1 us -> none  [local(): piece = lax.all_gather(tokens, 'wide', axis=0, tiled=True)]
    another operation x1 -> x0, loops' own time: 39.4 us -> none  [block_shrink(): totals = lax.fori_loop(0, block_first.shape[0], one_block, start_totals)]
    dot_general x14 -> x0, matrix products: 32.5 us -> none  [the longest x10 11.2 us: one_block(): lax.dot_general(window, adapter_down[adapter], (((1,), (1,)), ((), ())),...]
    pallas_call x0 -> x13, Pallas kernels: none -> 29.5 us  [the longest x2 8 us: down(): pl.pallas_call(functools.partial(down_kernel, n, h), in_specs=[VMEM, VMEM...]
    ppermute x0 -> x21, starting transfers between devices: none -> 27.7 us  [swap(): return lax.ppermute(x, axis, [(i, i ^ k) for i in range(n)])]
    ppermute x0 -> x21, waiting for transfers between devices: none -> 16 us  [swap(): return lax.ppermute(x, axis, [(i, i ^ k) for i in range(n)])]
    dynamic_slice x21 -> x0, local copies, waits for them, and re-layouts: 11.7 us -> none  [the longest x10 5.82 us: one_block(): opening = block_first[position]]
  transfers between devices with their start and end apart: 4 -> 21, of which waited for: 3 -> 7; matrix products, arithmetic and copies ran while one was open for 21% -> 0% of each run, Pallas kernels for 0% -> 34%
where the time goes in v2:
time: 73.5 us; the launch traced here: 73.4 us
  Pallas kernels  29.5 us (40%)
  starting transfers between devices  27.7 us (38%)
  waiting for transfers between devices  16 us (22%)
    ppermute x21, starting transfers between devices, swap(): return lax.ppermute(x, axis, [(i, i ^ k) for i in range(n)])  27.7 us
    ppermute x21, waiting for transfers between devices, swap(): return lax.ppermute(x, axis, [(i, i ^ k) for i in range(n)])  16 us
    pallas_call x2, Pallas kernels, down(): pl.pallas_call(functools.partial(down_kernel, n, h), in_specs=[VMEM, VMEM...  8 us
    pallas_call x1, Pallas kernels, fetch_up(): pl.pallas_call(up_fetch_kernel, in_specs=[SMEM, SMEM, ANY, HBM, HBM], out...  6.74 us
    pallas_call x1, Pallas kernels, fetch_gate(): pl.pallas_call(gate_fetch_kernel, in_specs=[HBM, HBM], out_specs=[VMEM] *...  6.13 us
    pallas_call x2, Pallas kernels, gate_up(): pl.pallas_call(functools.partial(gate_up_kernel, len(xs)), in_specs=[VMEM...  4.92 us
    pallas_call x1, Pallas kernels, add_delta(): pl.pallas_call(functools.partial(delta_kernel, n), in_specs=[SMEM, SMEM,...  1.54 us
  transfers between devices with their start and end apart: 21, of which 7 were waited for; matrix products, arithmetic and copies ran while one was open for 0% of the time, Pallas kernels for 34%

profile of v2, /device:TPU:0, one launch (start us, length us, event | category | flops | bytes accessed | tf_op | source)
XLA Modules:
  0.0 73.4 jit_solution(9074559920350889120)
XLA Ops:
  0.0 0.0 copy-start.1
  0.0 0.0 copy-start.2
  0.0 5.0 %collective-permute-start = (bf16[16,4096]{1,0:T(8,128)(2,1)}, bf16[16,4096]{1,0:T(8,128)(2,1)S(1)}, u32[]{:S(2)}, u32[]{:S(2)}) collective-permute-start(bf16[16,4096]{1,0:T(8,128)(2,1)} %refs_0_.1), channel_id=1, source_target_pairs={{0,12},{2,14},{4,8},{6,10},{8,4},{10,6},{12,0},{14,2},{1,13},{3,15... | collective-permute-start | bytes 393224 | tf_op jit(solution)/shard_map/ppermute | solution.py:25
  5.1 0.0 collective-permute-start.4
  5.1 1.5 %collective-permute-start.1 = (bf16[16,4096]{1,0:T(8,128)(2,1)}, bf16[16,4096]{1,0:T(8,128)(2,1)S(1)}, u32[]{:S(2)}, u32[]{:S(2)}) collective-permute-start(bf16[16,4096]{1,0:T(8,128)(2,1)} %refs_0_.1), channel_id=1, source_target_pairs={{0,2},{2,0},{4,6},{6,4},{8,10},{10,8},{12,14},{14,12},{1,3},{3,1},... | collective-permute-start | bytes 393224 | tf_op jit(solution)/shard_map/ppermute | solution.py:25
  6.5 0.8 %collective-permute-start.2 = (bf16[16,4096]{1,0:T(8,128)(2,1)}, bf16[16,4096]{1,0:T(8,128)(2,1)S(1)}, u32[]{:S(2)}, u32[]{:S(2)}) collective-permute-start(bf16[16,4096]{1,0:T(8,128)(2,1)} %refs_0_.1), channel_id=1, source_target_pairs={{0,4},{2,6},{4,0},{6,2},{8,12},{10,14},{12,8},{14,10},{1,5},{3,7},... | collective-permute-start | bytes 393224 | tf_op jit(solution)/shard_map/ppermute | solution.py:25
  7.3 1.2 %collective-permute-start.3 = (bf16[16,4096]{1,0:T(8,128)(2,1)}, bf16[16,4096]{1,0:T(8,128)(2,1)S(1)}, u32[]{:S(2)}, u32[]{:S(2)}) collective-permute-start(bf16[16,4096]{1,0:T(8,128)(2,1)} %refs_0_.1), channel_id=1, source_target_pairs={{0,6},{2,4},{4,2},{6,0},{8,14},{10,12},{12,10},{14,8},{1,7},{3,5},... | collective-permute-start | bytes 393224 | tf_op jit(solution)/shard_map/ppermute | solution.py:25
  8.5 6.1 %fetch_gate.1 = (bf16[4096,1024]{1,0:T(8,128)(2,1)S(1)}, bf16[4096,1024]{1,0:T(8,128)(2,1)S(1)}, bf16[8,16,2048]{2,1,0:T(8,128)(2,1)S(1)}, bf16[8,16,2048]{2,1,0:T(8,128)(2,1)S(1)}) custom-call(bf16[4096,2048]{1,0:T(8,128)(2,1)} %weight.4, bf16[8,16,4096]{2,1,0:T(8,128)(2,1)} %adapter_up.1), custom_call_target="tpu_custom_call" | custom-call | bytes 16777216 | tf_op jit(solution)/shard_map/fetch_gate/pallas_call | solution.py:81
  14.7 0.0 collective-permute-done.after.refs_6_
  14.7 0.0 copy-start
  14.7 1.6 %collective-permute-start.6 = (bf16[16,4096]{1,0:T(8,128)(2,1)S(1)}, bf16[16,4096]{1,0:T(8,128)(2,1)S(1)}, u32[]{:S(2)}, u32[]{:S(2)}) collective-permute-start(bf16[16,4096]{1,0:T(8,128)(2,1)S(1)} %collective-permute-done.after.refs_6_), channel_id=1, source_target_pairs={{0,2},{2,0},{4,6},{6,4},{8,10},{10,8},{12,14},{14,12},{1,3},{3,1},... | collective-permute-start | bytes 393224 | tf_op jit(solution)/shard_map/ppermute | solution.py:25
  16.3 0.2 collective-permute-done.4.refs_4_
  16.4 1.5 %collective-permute-start.5 = (bf16[16,4096]{1,0:T(8,128)(2,1)S(1)}, bf16[16,4096]{1,0:T(8,128)(2,1)S(1)}, u32[]{:S(2)}, u32[]{:S(2)}) collective-permute-start(bf16[16,4096]{1,0:T(8,128)(2,1)S(1)} %collective-permute-done.4.refs_4_), channel_id=1, source_target_pairs={{0,2},{2,0},{4,6},{6,4},{8,10},{10,8},{12,14},{14,12},{1,3},{3,1},... | collective-permute-start | bytes 393224 | tf_op jit(solution)/shard_map/ppermute | solution.py:25
  17.9 0.0 collective-permute-done.1.refs_1_
  17.9 0.0 collective-permute-done.2.refs_2_
  17.9 0.4 collective-permute-done.3.refs_3_
  18.3 0.0 copy-done.1
  18.3 0.0 copy-done.2
  18.3 6.7 %fetch_up.1 = (bf16[4096,1024]{1,0:T(8,128)(2,1)S(1)}, bf16[4096,1024]{1,0:T(8,128)(2,1)S(1)}, bf16[160,2048]{1,0:T(8,128)(2,1)S(1)}) custom-call(s32[128]{0:T(128)S(1)} %copy-done.1, s32[10]{0:T(128)S(1)} %copy-done.2, bf16[16,4096]{1,0:T(8,128)(2,1)S(1)} %collective-permute-done.after.refs_6_, bf16[4096,2048]{1,0:T(8,128)(2,1)} %weight.5, ...), custom_call_target="tpu_custom_call" | custom-call | tf_op jit(solution)/shard_map/fetch_up/pallas_call | solution.py:110
  25.1 0.0 collective-permute-done.6.refs_7_
  25.1 0.0 collective-permute-done.5.refs_5_
  25.1 0.0 copy-done
  25.1 2.4 %gate_up.2 = (f32[2,128,1024]{2,1,0:T(8,128)S(1)}, bf16[128,4096]{1,0:T(8,128)(2,1)S(1)}) custom-call(bf16[16,4096]{1,0:T(8,128)(2,1)S(1)} %copy-done, bf16[16,4096]{1,0:T(8,128)(2,1)S(1)} %collective-permute-done.1.refs_1_, bf16[16,4096]{1,0:T(8,128)(2,1)S(1)} %collective-permute-done.2.refs_2_, bf16[16,4096]{1,0:T(8,128)(2,1)S(1)} %collective-permute-done.3.refs_3_, ...), custom_call_target="tpu_custom_call" | custom-call | tf_op jit(solution)/shard_map/gate_up/pallas_call | solution.py:146
  27.6 0.1 collective-permute-start.7
  27.6 0.9 %collective-permute-start.10 = (bf16[8,16,2048]{2,1,0:T(8,128)(2,1)S(1)}, bf16[8,16,2048]{2,1,0:T(8,128)(2,1)S(1)}, u32[]{:S(2)}, u32[]{:S(2)}) collective-permute-start(bf16[8,16,2048]{2,1,0:T(8,128)(2,1)S(1)} %get-tuple-element.70.up_x), channel_id=1, source_target_pairs={{0,2},{2,0},{4,6},{6,4},{8,10},{10,8},{12,14},{14,12},{1,3},{3,1},... | collective-permute-start | bytes 1572872 | tf_op jit(solution)/shard_map/ppermute | solution.py:25
  28.5 1.4 %collective-permute-start.11 = (bf16[8,16,2048]{2,1,0:T(8,128)(2,1)S(1)}, bf16[8,16,2048]{2,1,0:T(8,128)(2,1)S(1)}, u32[]{:S(2)}, u32[]{:S(2)}) collective-permute-start(bf16[8,16,2048]{2,1,0:T(8,128)(2,1)S(1)} %get-tuple-element.71.up_z), channel_id=1, source_target_pairs={{0,4},{2,6},{4,0},{6,2},{8,12},{10,14},{12,8},{14,10},{1,5},{3,7},... | collective-permute-start | bytes 1572872 | tf_op jit(solution)/shard_map/ppermute | solution.py:25
  29.9 2.5 %gate_up.3.kept = f32[2,128,1024]{2,1,0:T(8,128)S(1)} custom-call(bf16[128,4096]{1,0:T(8,128)(2,1)S(1)} %get-tuple-element.54.refs_0_, bf16[4096,1024]{1,0:T(8,128)(2,1)S(1)} %get-tuple-element.55.refs_1_, bf16[4096,1024]{1,0:T(8,128)(2,1)S(1)} %get-tuple-element.56.refs_2_), custom_call_target="tpu_custom_call" | custom-call | tf_op jit(solution)/shard_map/gate_up/pallas_call | solution.py:146
  32.4 0.0 collective-permute-done.7.got
  32.4 0.3 silu.1.mine
  32.7 0.1 collective-permute-start.8
  32.8 1.5 %collective-permute-done.8.other = bf16[128,1024]{1,0:T(8,128)(2,1)S(1)} collective-permute-done((bf16[128,1024]{1,0:T(8,128)(2,1)S(1)}, bf16[128,1024]{1,0:T(8,128)(2,1)S(1)}, u32[]{:S(2)}, u32[]{:S(2)}) %collective-permute-start.8) | collective-permute-done | bytes 262176 | tf_op jit(solution)/shard_map/ppermute | solution.py:25
  34.3 1.1 %shrink.1.a = f32[16,128]{1,0:T(8,128)S(1)} custom-call(s32[128]{0:T(128)S(1)} %copy-done.1, s32[10]{0:T(128)S(1)} %copy-done.2, s32[1,128]{1,0:T(1,128)S(1)} %bitcast.1, bf16[128,1024]{1,0:T(8,128)(2,1)S(1)} %silu.1.mine, bf16[128,1024]{1,0:T(8,128)(2,1)S(1)} %collective-permute-done.8.other, bf16[160,2048]{1,0:T(8,128)(2,1)S(1)} %get-tuple-element.58.factors), custom_call_target="tpu_custom_call" | custom-call | tf_op jit(solution)/shard_map/shrink/pallas_call | solution.py:209
  35.4 1.6 %collective-permute-start.9 = (f32[16,128]{1,0:T(8,128)S(1)}, f32[16,128]{1,0:T(8,128)S(1)}, u32[]{:S(2)}, u32[]{:S(2)}) collective-permute-start(f32[16,128]{1,0:T(8,128)S(1)} %shrink.1.a), channel_id=1, source_target_pairs={{0,2},{2,0},{4,6},{6,4},{8,10},{10,8},{12,14},{14,12},{1,3},{3,1},... | collective-permute-start | bytes 24584 | tf_op jit(solution)/shard_map/ppermute | solution.py:25
  37.0 4.0 %down.2 = (f32[128,2048]{1,0:T(8,128)S(1)}, bf16[48,2048]{1,0:T(8,128)(2,1)S(1)}) custom-call(bf16[128,1024]{1,0:T(8,128)(2,1)S(1)} %silu.1.mine, bf16[128,1024]{1,0:T(8,128)(2,1)S(1)} %collective-permute-done.8.other, bf16[2048,4096]{1,0:T(8,128)(2,1)} %weight.7), custom_call_target="tpu_custom_call" | custom-call | tf_op jit(solution)/shard_map/down/pallas_call | solution.py:255
  41.0 0.0 copy-start.3
  41.0 4.0 %down.3 = (f32[128,2048]{1,0:T(8,128)S(1)}, bf16[48,2048]{1,0:T(8,128)(2,1)S(1)}) custom-call(bf16[128,1024]{1,0:T(8,128)(2,1)S(1)} %silu.1.mine, bf16[128,1024]{1,0:T(8,128)(2,1)S(1)} %collective-permute-done.8.other, bf16[2048,4096]{1,0:T(8,128)(2,1)} %weight.7), custom_call_target="tpu_custom_call" | custom-call | tf_op jit(solution)/shard_map/down/pallas_call | solution.py:255
  45.0 0.0 collective-permute-done.10.next_x
  45.0 0.0 collective-permute-done.11.next_z
  45.0 0.0 collective-permute-done.9.b
  45.0 0.6 collective-permute-start.14
  45.6 0.6 collective-permute-start.15
  46.3 1.4 %collective-permute-start.12 = (f32[16,128]{1,0:T(8,128)S(1)}, f32[16,128]{1,0:T(8,128)S(1)}, u32[]{:S(2)}, u32[]{:S(2)}) collective-permute-start(f32[16,128]{1,0:T(8,128)S(1)} %plus.3.a), channel_id=1, source_target_pairs={{0,4},{2,6},{4,0},{6,2},{8,12},{10,14},{12,8},{14,10},{1,5},{3,7},... | collective-permute-start | bytes 24584 | tf_op jit(solution)/shard_map/ppermute | solution.py:25
  47.7 4.5 %collective-permute-done.12.b = f32[16,128]{1,0:T(8,128)S(1)} collective-permute-done((f32[16,128]{1,0:T(8,128)S(1)}, f32[16,128]{1,0:T(8,128)S(1)}, u32[]{:S(2)}, u32[]{:S(2)}) %collective-permute-start.12) | collective-permute-done | bytes 8224 | tf_op jit(solution)/shard_map/ppermute | solution.py:25
  52.2 2.2 %collective-permute-start.13 = (f32[16,128]{1,0:T(8,128)S(1)}, f32[16,128]{1,0:T(8,128)S(1)}, u32[]{:S(2)}, u32[]{:S(2)}) collective-permute-start(f32[16,128]{1,0:T(8,128)S(1)} %plus.4.a), channel_id=1, source_target_pairs={{0,8},{2,10},{4,12},{6,14},{8,0},{10,2},{12,4},{14,6},{1,9},{3,11}... | collective-permute-start | bytes 24584 | tf_op jit(solution)/shard_map/ppermute | solution.py:25
  54.4 2.3 %collective-permute-done.13.b = f32[16,128]{1,0:T(8,128)S(1)} collective-permute-done((f32[16,128]{1,0:T(8,128)S(1)}, f32[16,128]{1,0:T(8,128)S(1)}, u32[]{:S(2)}, u32[]{:S(2)}) %collective-permute-start.13) | collective-permute-done | bytes 8224 | tf_op jit(solution)/shard_map/ppermute | solution.py:25
  56.8 0.0 collective-permute-done.14.refs_0_
  56.8 0.0 collective-permute-done.15.refs_1_
  56.8 0.0 copy-done.3
  56.8 1.5 %add_delta.1 = (bf16[16,4096]{1,0:T(8,128)(2,1)S(1)}, bf16[16,4096]{1,0:T(8,128)(2,1)S(1)}, bf16[16,4096]{1,0:T(8,128)(2,1)S(1)}, bf16[16,4096]{1,0:T(8,128)(2,1...) custom-call(s32[128]{0:T(128)S(1)} %copy-done.1, s32[10]{0:T(128)S(1)} %copy-done.2, s32[64]{0:T(128)S(1)} %copy-done.3, ...), custom_call_target="tpu_custom_call" | custom-call | tf_op jit(solution)/shard_map/add_delta/pallas_call | solution.py:335
  58.3 1.6 %collective-permute-start.16 = (bf16[16,4096]{1,0:T(8,128)(2,1)S(1)}, bf16[16,4096]{1,0:T(8,128)(2,1)S(1)}, u32[]{:S(2)}, u32[]{:S(2)}) collective-permute-start(bf16[16,4096]{1,0:T(8,128)(2,1)S(1)} %get-tuple-element.80), channel_id=1, source_target_pairs={{0,2},{2,0},{4,6},{6,4},{8,10},{10,8},{12,14},{14,12},{1,3},{3,1},... | collective-permute-start | bytes 393224 | tf_op jit(solution)/shard_map/ppermute | solution.py:25
  59.9 0.3 collective-permute-start.17
  60.2 2.2 %collective-permute-start.18 = (bf16[16,4096]{1,0:T(8,128)(2,1)S(1)}, bf16[16,4096]{1,0:T(8,128)(2,1)S(1)}, u32[]{:S(2)}, u32[]{:S(2)}) collective-permute-start(bf16[16,4096]{1,0:T(8,128)(2,1)S(1)} %get-tuple-element.82), channel_id=1, source_target_pairs={{0,8},{2,10},{4,12},{6,14},{8,0},{10,2},{12,4},{14,6},{1,9},{3,11}... | collective-permute-start | bytes 393224 | tf_op jit(solution)/shard_map/ppermute | solution.py:25
  62.4 1.9 %collective-permute-start.19 = (bf16[16,2048]{1,0:T(8,128)(2,1)S(1)}, bf16[16,2048]{1,0:T(8,128)(2,1)S(1)}, u32[]{:S(2)}, u32[]{:S(2)}) collective-permute-start(bf16[16,2048]{1,0:T(8,128)(2,1)S(1)} %get-tuple-element.83), channel_id=1, source_target_pairs={{0,12},{2,14},{4,8},{6,10},{8,4},{10,6},{12,0},{14,2},{1,13},{3,15... | collective-permute-start | bytes 196616 | tf_op jit(solution)/shard_map/ppermute | solution.py:25
  64.3 1.3 %collective-permute-start.20 = (bf16[16,2048]{1,0:T(8,128)(2,1)S(1)}, bf16[16,2048]{1,0:T(8,128)(2,1)S(1)}, u32[]{:S(2)}, u32[]{:S(2)}) collective-permute-start(bf16[16,2048]{1,0:T(8,128)(2,1)S(1)} %get-tuple-element.84), channel_id=1, source_target_pairs={{0,10},{2,8},{4,14},{6,12},{8,2},{10,0},{12,6},{14,4},{1,11},{3,9}... | collective-permute-start | bytes 196616 | tf_op jit(solution)/shard_map/ppermute | solution.py:25
  65.6 3.7 %collective-permute-done.19.refs_4_ = bf16[16,2048]{1,0:T(8,128)(2,1)S(1)} collective-permute-done((bf16[16,2048]{1,0:T(8,128)(2,1)S(1)}, bf16[16,2048]{1,0:T(8,128)(2,1)S(1)}, u32[]{:S(2)}, u32[]{:S(2)}) %collective-permute-start.19) | collective-permute-done | bytes 65568 | tf_op jit(solution)/shard_map/ppermute | solution.py:25
  69.3 3.3 %collective-permute-done.20.refs_5_ = bf16[16,2048]{1,0:T(8,128)(2,1)S(1)} collective-permute-done((bf16[16,2048]{1,0:T(8,128)(2,1)S(1)}, bf16[16,2048]{1,0:T(8,128)(2,1)S(1)}, u32[]{:S(2)}, u32[]{:S(2)}) %collective-permute-start.20) | collective-permute-done | bytes 65568 | tf_op jit(solution)/shard_map/ppermute | solution.py:25
  72.6 0.0 collective-permute-done.16.refs_1_
  72.6 0.0 collective-permute-done.17.refs_2_
  72.6 0.0 collective-permute-done.18.refs_3_
  72.6 0.7 %sum_rows.1 = bf16[16,4096]{1,0:T(8,128)(2,1)} custom-call(bf16[16,4096]{1,0:T(8,128)(2,1)S(1)} %get-tuple-element.79.refs_0_, bf16[16,4096]{1,0:T(8,128)(2,1)S(1)} %collective-permute-done.16.refs_1_, bf16[16,4096]{1,0:T(8,128)(2,1)S(1)} %collective-permute-done.17.refs_2_, bf16[16,4096]{1,0:T(8,128)(2,1)S(1)} %collective-permute-done.18.refs_3_, ...), custom_call_target="tpu_custom_call" | custom-call | tf_op jit(solution)/shard_map/sum_rows/pallas_call | solution.py:363
  (3 shorter events, 0.0 us)
Async XLA Ops:
  0.0 18.3 %copy-start.1 = (s32[128]{0:T(128)S(1)}, s32[128]{0:T(128)}, u32[]{:S(2)}) copy-start(s32[128]{0:T(128)} %row_adapter.5) | copy-start | bytes 1540
  0.0 18.3 %copy-start.2 = (s32[10]{0:T(128)S(1)}, s32[10]{0:T(128)}, u32[]{:S(2)}) copy-start(s32[10]{0:T(128)} %block_first.5) | copy-start | bytes 124
  0.0 14.7 %collective-permute-start = (bf16[16,4096]{1,0:T(8,128)(2,1)}, bf16[16,4096]{1,0:T(8,128)(2,1)S(1)}, u32[]{:S(2)}, u32[]{:S(2)}) collective-permute-start(bf16[16,4096]{1,0:T(8,128)(2,1)} %refs_0_.1), channel_id=1, source_target_pairs={{0,12},{2,14},{4,8},{6,10},{8,4},{10,6},{12,0},{14,2},{1,13},{3,15... | collective-permute-start | bytes 393224 | tf_op jit(solution)/shard_map/ppermute | solution.py:25
  5.1 11.4 %collective-permute-start.4 = (bf16[16,4096]{1,0:T(8,128)(2,1)}, bf16[16,4096]{1,0:T(8,128)(2,1)S(1)}, u32[]{:S(2)}, u32[]{:S(2)}) collective-permute-start(bf16[16,4096]{1,0:T(8,128)(2,1)} %refs_0_.1), channel_id=1, source_target_pairs={{0,8},{2,10},{4,12},{6,14},{8,0},{10,2},{12,4},{14,6},{1,9},{3,11}... | collective-permute-start | bytes 393224 | tf_op jit(solution)/shard_map/ppermute | solution.py:25
  5.1 12.9 %collective-permute-start.1 = (bf16[16,4096]{1,0:T(8,128)(2,1)}, bf16[16,4096]{1,0:T(8,128)(2,1)S(1)}, u32[]{:S(2)}, u32[]{:S(2)}) collective-permute-start(bf16[16,4096]{1,0:T(8,128)(2,1)} %refs_0_.1), channel_id=1, source_target_pairs={{0,2},{2,0},{4,6},{6,4},{8,10},{10,8},{12,14},{14,12},{1,3},{3,1},... | collective-permute-start | bytes 393224 | tf_op jit(solution)/shard_map/ppermute | solution.py:25
  6.5 11.4 %collective-permute-start.2 = (bf16[16,4096]{1,0:T(8,128)(2,1)}, bf16[16,4096]{1,0:T(8,128)(2,1)S(1)}, u32[]{:S(2)}, u32[]{:S(2)}) collective-permute-start(bf16[16,4096]{1,0:T(8,128)(2,1)} %refs_0_.1), channel_id=1, source_target_pairs={{0,4},{2,6},{4,0},{6,2},{8,12},{10,14},{12,8},{14,10},{1,5},{3,7},... | collective-permute-start | bytes 393224 | tf_op jit(solution)/shard_map/ppermute | solution.py:25
  7.3 11.0 %collective-permute-start.3 = (bf16[16,4096]{1,0:T(8,128)(2,1)}, bf16[16,4096]{1,0:T(8,128)(2,1)S(1)}, u32[]{:S(2)}, u32[]{:S(2)}) collective-permute-start(bf16[16,4096]{1,0:T(8,128)(2,1)} %refs_0_.1), channel_id=1, source_target_pairs={{0,6},{2,4},{4,2},{6,0},{8,14},{10,12},{12,10},{14,8},{1,7},{3,5},... | collective-permute-start | bytes 393224 | tf_op jit(solution)/shard_map/ppermute | solution.py:25
  14.7 10.4 %copy-start = (bf16[16,4096]{1,0:T(8,128)(2,1)S(1)}, bf16[16,4096]{1,0:T(8,128)(2,1)}, u32[]{:S(2)}) copy-start(bf16[16,4096]{1,0:T(8,128)(2,1)} %refs_0_.1) | copy-start | bytes 393220
  14.7 10.4 %collective-permute-start.6 = (bf16[16,4096]{1,0:T(8,128)(2,1)S(1)}, bf16[16,4096]{1,0:T(8,128)(2,1)S(1)}, u32[]{:S(2)}, u32[]{:S(2)}) collective-permute-start(bf16[16,4096]{1,0:T(8,128)(2,1)S(1)} %collective-permute-done.after.refs_6_), channel_id=1, source_target_pairs={{0,2},{2,0},{4,6},{6,4},{8,10},{10,8},{12,14},{14,12},{1,3},{3,1},... | collective-permute-start | bytes 393224 | tf_op jit(solution)/shard_map/ppermute | solution.py:25
  16.4 8.6 %collective-permute-start.5 = (bf16[16,4096]{1,0:T(8,128)(2,1)S(1)}, bf16[16,4096]{1,0:T(8,128)(2,1)S(1)}, u32[]{:S(2)}, u32[]{:S(2)}) collective-permute-start(bf16[16,4096]{1,0:T(8,128)(2,1)S(1)} %collective-permute-done.4.refs_4_), channel_id=1, source_target_pairs={{0,2},{2,0},{4,6},{6,4},{8,10},{10,8},{12,14},{14,12},{1,3},{3,1},... | collective-permute-start | bytes 393224 | tf_op jit(solution)/shard_map/ppermute | solution.py:25
  27.6 4.9 %collective-permute-start.7 = (f32[2,128,1024]{2,1,0:T(8,128)S(1)}, f32[2,128,1024]{2,1,0:T(8,128)S(1)}, u32[]{:S(2)}, u32[]{:S(2)}) collective-permute-start(f32[2,128,1024]{2,1,0:T(8,128)S(1)} %get-tuple-element.57), channel_id=1, source_target_pairs={{0,1},{1,0},{2,3},{3,2},{4,5},{5,4},{6,7},{7,6},{8,9},{9,8},{10,11... | collective-permute-start | bytes 3145736 | tf_op jit(solution)/shard_map/ppermute | solution.py:25
  27.6 17.4 %collective-permute-start.10 = (bf16[8,16,2048]{2,1,0:T(8,128)(2,1)S(1)}, bf16[8,16,2048]{2,1,0:T(8,128)(2,1)S(1)}, u32[]{:S(2)}, u32[]{:S(2)}) collective-permute-start(bf16[8,16,2048]{2,1,0:T(8,128)(2,1)S(1)} %get-tuple-element.70.up_x), channel_id=1, source_target_pairs={{0,2},{2,0},{4,6},{6,4},{8,10},{10,8},{12,14},{14,12},{1,3},{3,1},... | collective-permute-start | bytes 1572872 | tf_op jit(solution)/shard_map/ppermute | solution.py:25
  28.5 16.5 %collective-permute-start.11 = (bf16[8,16,2048]{2,1,0:T(8,128)(2,1)S(1)}, bf16[8,16,2048]{2,1,0:T(8,128)(2,1)S(1)}, u32[]{:S(2)}, u32[]{:S(2)}) collective-permute-start(bf16[8,16,2048]{2,1,0:T(8,128)(2,1)S(1)} %get-tuple-element.71.up_z), channel_id=1, source_target_pairs={{0,4},{2,6},{4,0},{6,2},{8,12},{10,14},{12,8},{14,10},{1,5},{3,7},... | collective-permute-start | bytes 1572872 | tf_op jit(solution)/shard_map/ppermute | solution.py:25
  32.7 1.6 %collective-permute-start.8 = (bf16[128,1024]{1,0:T(8,128)(2,1)S(1)}, bf16[128,1024]{1,0:T(8,128)(2,1)S(1)}, u32[]{:S(2)}, u32[]{:S(2)}) collective-permute-start(bf16[128,1024]{1,0:T(8,128)(2,1)S(1)} %silu.1.mine), channel_id=1, source_target_pairs={{0,1},{1,0},{2,3},{3,2},{4,5},{5,4},{6,7},{7,6},{8,9},{9,8},{10,11... | collective-permute-start | bytes 786440 | tf_op jit(solution)/shard_map/ppermute | solution.py:25
  35.4 9.6 %collective-permute-start.9 = (f32[16,128]{1,0:T(8,128)S(1)}, f32[16,128]{1,0:T(8,128)S(1)}, u32[]{:S(2)}, u32[]{:S(2)}) collective-permute-start(f32[16,128]{1,0:T(8,128)S(1)} %shrink.1.a), channel_id=1, source_target_pairs={{0,2},{2,0},{4,6},{6,4},{8,10},{10,8},{12,14},{14,12},{1,3},{3,1},... | collective-permute-start | bytes 24584 | tf_op jit(solution)/shard_map/ppermute | solution.py:25
  41.0 15.8 %copy-start.3 = (s32[64]{0:T(128)S(1)}, s32[64]{0:T(128)}, u32[]{:S(2)}) copy-start(s32[64]{0:T(128)} %page_table.1) | copy-start | bytes 772
  45.0 11.7 %collective-permute-start.14 = (bf16[48,2048]{1,0:T(8,128)(2,1)S(1)}, bf16[48,2048]{1,0:T(8,128)(2,1)S(1)}, u32[]{:S(2)}, u32[]{:S(2)}) collective-permute-start(bf16[48,2048]{1,0:T(8,128)(2,1)S(1)} %get-tuple-element.77), channel_id=1, source_target_pairs={{0,2},{2,0},{4,6},{6,4},{8,10},{10,8},{12,14},{14,12},{1,3},{3,1},... | collective-permute-start | bytes 589832 | tf_op jit(solution)/shard_map/ppermute | solution.py:25
  45.6 11.1 %collective-permute-start.15 = (bf16[48,2048]{1,0:T(8,128)(2,1)S(1)}, bf16[48,2048]{1,0:T(8,128)(2,1)S(1)}, u32[]{:S(2)}, u32[]{:S(2)}) collective-permute-start(bf16[48,2048]{1,0:T(8,128)(2,1)S(1)} %get-tuple-element.78), channel_id=1, source_target_pairs={{0,4},{2,6},{4,0},{6,2},{8,12},{10,14},{12,8},{14,10},{1,5},{3,7},... | collective-permute-start | bytes 589832 | tf_op jit(solution)/shard_map/ppermute | solution.py:25
  46.3 5.9 %collective-permute-start.12 = (f32[16,128]{1,0:T(8,128)S(1)}, f32[16,128]{1,0:T(8,128)S(1)}, u32[]{:S(2)}, u32[]{:S(2)}) collective-permute-start(f32[16,128]{1,0:T(8,128)S(1)} %plus.3.a), channel_id=1, source_target_pairs={{0,4},{2,6},{4,0},{6,2},{8,12},{10,14},{12,8},{14,10},{1,5},{3,7},... | collective-permute-start | bytes 24584 | tf_op jit(solution)/shard_map/ppermute | solution.py:25
  52.2 4.6 %collective-permute-start.13 = (f32[16,128]{1,0:T(8,128)S(1)}, f32[16,128]{1,0:T(8,128)S(1)}, u32[]{:S(2)}, u32[]{:S(2)}) collective-permute-start(f32[16,128]{1,0:T(8,128)S(1)} %plus.4.a), channel_id=1, source_target_pairs={{0,8},{2,10},{4,12},{6,14},{8,0},{10,2},{12,4},{14,6},{1,9},{3,11}... | collective-permute-start | bytes 24584 | tf_op jit(solution)/shard_map/ppermute | solution.py:25
  58.3 14.3 %collective-permute-start.16 = (bf16[16,4096]{1,0:T(8,128)(2,1)S(1)}, bf16[16,4096]{1,0:T(8,128)(2,1)S(1)}, u32[]{:S(2)}, u32[]{:S(2)}) collective-permute-start(bf16[16,4096]{1,0:T(8,128)(2,1)S(1)} %get-tuple-element.80), channel_id=1, source_target_pairs={{0,2},{2,0},{4,6},{6,4},{8,10},{10,8},{12,14},{14,12},{1,3},{3,1},... | collective-permute-start | bytes 393224 | tf_op jit(solution)/shard_map/ppermute | solution.py:25
  59.9 12.7 %collective-permute-start.17 = (bf16[16,4096]{1,0:T(8,128)(2,1)S(1)}, bf16[16,4096]{1,0:T(8,128)(2,1)S(1)}, u32[]{:S(2)}, u32[]{:S(2)}) collective-permute-start(bf16[16,4096]{1,0:T(8,128)(2,1)S(1)} %get-tuple-element.81), channel_id=1, source_target_pairs={{0,4},{2,6},{4,0},{6,2},{8,12},{10,14},{12,8},{14,10},{1,5},{3,7},... | collective-permute-start | bytes 393224 | tf_op jit(solution)/shard_map/ppermute | solution.py:25
  60.2 12.4 %collective-permute-start.18 = (bf16[16,4096]{1,0:T(8,128)(2,1)S(1)}, bf16[16,4096]{1,0:T(8,128)(2,1)S(1)}, u32[]{:S(2)}, u32[]{:S(2)}) collective-permute-start(bf16[16,4096]{1,0:T(8,128)(2,1)S(1)} %get-tuple-element.82), channel_id=1, source_target_pairs={{0,8},{2,10},{4,12},{6,14},{8,0},{10,2},{12,4},{14,6},{1,9},{3,11}... | collective-permute-start | bytes 393224 | tf_op jit(solution)/shard_map/ppermute | solution.py:25
  62.4 6.8 %collective-permute-start.19 = (bf16[16,2048]{1,0:T(8,128)(2,1)S(1)}, bf16[16,2048]{1,0:T(8,128)(2,1)S(1)}, u32[]{:S(2)}, u32[]{:S(2)}) collective-permute-start(bf16[16,2048]{1,0:T(8,128)(2,1)S(1)} %get-tuple-element.83), channel_id=1, source_target_pairs={{0,12},{2,14},{4,8},{6,10},{8,4},{10,6},{12,0},{14,2},{1,13},{3,15... | collective-permute-start | bytes 196616 | tf_op jit(solution)/shard_map/ppermute | solution.py:25
  64.3 8.3 %collective-permute-start.20 = (bf16[16,2048]{1,0:T(8,128)(2,1)S(1)}, bf16[16,2048]{1,0:T(8,128)(2,1)S(1)}, u32[]{:S(2)}, u32[]{:S(2)}) collective-permute-start(bf16[16,2048]{1,0:T(8,128)(2,1)S(1)} %get-tuple-element.84), channel_id=1, source_target_pairs={{0,10},{2,8},{4,14},{6,12},{8,2},{10,0},{12,6},{14,4},{1,11},{3,9}... | collective-permute-start | bytes 196616 | tf_op jit(solution)/shard_map/ppermute | solution.py:25

commit v3 on v2

--- a/solution.py
+++ b/solution.py
@@ -224,47 +224,46 @@
     return plan
 
 
-def down_kernel(n, h, mine, other, weight, base, raw, tiles, sems):
+def down_kernel(n, mine, other, weight, base_x, base_z, raw_x, raw_z, tiles, sems):
     total, depth = mine.shape
     rows = total // n
     half = lax.axis_index("tensor")
     first = pl.ds(pl.multiple_of(half * depth, 128), depth)
     second = pl.ds(pl.multiple_of((1 - half) * depth, 128), depth)
     count, _, tile = tiles.shape
-    width = count * tile
 
     def copy(j):
-        return pltpu.make_async_copy(weight.at[:, pl.ds(h * width + j * tile, tile)], tiles.at[j], sems.at[j])
+        return pltpu.make_async_copy(weight.at[:, pl.ds(j * tile, tile)], tiles.at[j], sems.at[j])
 
     for j in range(count):
         copy(j).start()
     for j in range(count):
         copy(j).wait()
-        columns = slice(j * tile, (j + 1) * tile)
+        h, at = divmod(j, count // 2)
+        base, raw = ((base_x, raw_x), (base_z, raw_z))[h]
+        columns = slice(at * tile, (at + 1) * tile)
         result = dot(mine[...], tiles[j, first]) + dot(other[...], tiles[j, second])
         base[:, columns] = result
         for i, k in enumerate(relays(n)[h][1]):
             raw[i * rows : (i + 1) * rows, columns] = result[k * rows : (k + 1) * rows].astype(raw.dtype)
 
 
-def down(n, h, mine, other, weight):
+def down(n, mine, other, weight):
     total, depth = mine.shape
     width = weight.shape[1] // 2
     tile = min(512, width)
-    sent = relays(n)[h][1]
-    return pl.pallas_call(
-        functools.partial(down_kernel, n, h),
+    base = jax.ShapeDtypeStruct((total, width), jnp.float32)
+    raws = [jax.ShapeDtypeStruct((len(sent) * total // n, width), jnp.bfloat16) for _, sent, _ in relays(n)]
+    return pl.pallas_call(
+        functools.partial(down_kernel, n),
         in_specs=[VMEM, VMEM, HBM],
-        out_specs=[VMEM] * 2,
-        out_shape=[
-            jax.ShapeDtypeStruct((total, width), jnp.float32),
-            jax.ShapeDtypeStruct((len(sent) * total // n, width), jnp.bfloat16),
+        out_specs=[VMEM] * 4,
+        out_shape=[base, base, *raws],
+        scratch_shapes=[
+            pltpu.VMEM((2 * width // tile, 2 * depth, tile), weight.dtype),
+            pltpu.SemaphoreType.DMA((2 * width // tile,)),
         ],
-        scratch_shapes=[
-            pltpu.VMEM((width // tile, 2 * depth, tile), weight.dtype),
-            pltpu.SemaphoreType.DMA((width // tile,)),
-        ],
-        compiler_params=pltpu.CompilerParams(vmem_limit_bytes=(LIMIT + 8) * MIB),
+        compiler_params=pltpu.CompilerParams(vmem_limit_bytes=(LIMIT + 16) * MIB),
         cost_estimate=pl.CostEstimate(flops=0, bytes_accessed=0, transcendentals=0),
         name="down",
     )(mine, other, stay(weight))
@@ -418,19 +417,17 @@
     shrunk = shrink(n, row_adapter, block_first, mine, other, factors)
     arrived = swap(shrunk, "wide", n, 1)
     shrunk, mine = lax.optimization_barrier((shrunk, mine))
-    bases, raws = [], []
-    for h in range(2):
-        base, raw = down(n, h, mine, other, down_weight)
-        mine, base, raw = lax.optimization_barrier((mine, base, raw))
-        bases.append(base)
-        raws.append(raw)
-    arrived, *rest = lax.optimization_barrier((arrived, *bases, *raws, *nears))
+    *sums, raw_x, raw_z = down(n, mine, other, down_weight)
+    arrived, *rest = lax.optimization_barrier((arrived, *sums, raw_x, raw_z, *nears))
     bases, raws, nears = rest[:2], rest[2:4], rest[4:]
     shrunk = plus(shrunk, arrived)
-    raws = [swap(raw, "wide", n, mask) for raw, (mask, _, _) in zip(raws, relays(n))]
+    raws[0] = swap(raws[0], "wide", n, 1)
     bit = 2
     while bit < n:
         shrunk = plus(shrunk, swap(shrunk, "wide", n, bit))
+        if bit == 2:
+            shrunk, raws[1] = lax.optimization_barrier((shrunk, raws[1]))
+            raws[1] = swap(raws[1], "wide", n, 2)
         bit *= 2
     parts = add_delta(n, row_adapter, block_first, page_table, shrunk, ups, nears, bases, raws)
     whole, halves = kept_blocks(n)
@@ -438,6 +435,8 @@
     for ks, xs in reversed(list(zip([whole] + halves, parts))):
         for k, block in reversed(list(zip(ks, xs))):
             arrived[k] = block if k == 0 else swap(block, "wide", n, k)
+    last = [k for k in arrived if k > 2]
+    arrived.update(zip(last, lax.optimization_barrier([arrived[k] for k in last])))
     arrived = [[arrived[k] for k in ks] for ks in [whole] + halves]
     return add_up(*arrived)
 

time: 73.5 us -> 68.4 us (0.931)
  waiting for transfers between devices: 16 us -> 11.9 us
  Pallas kernels: 29.5 us -> 27.9 us
    ppermute x21, waiting for transfers between devices: 16 us -> 11.9 us  [swap(): return lax.ppermute(x, axis, [(i, i ^ k) for i in range(n)])]
    pallas_call x2 -> x1, Pallas kernels: 8 us -> 6.48 us  [down(): pl.pallas_call(functools.partial(down_kernel, n), in_specs=[VMEM, VMEM, H...]
  transfers between devices with their start and end apart: 21 -> 21, of which waited for: 7 -> 8; matrix products, arithmetic and copies ran while one was open for 0% -> 0% of each run, Pallas kernels for 34% -> 34%
where the time goes in v3:
time: 68.4 us; the launch traced here: 68.2 us
  starting transfers between devices  28.1 us (41%)
  Pallas kernels  27.9 us (41%)
  waiting for transfers between devices  11.9 us (17%)
    ppermute x21, starting transfers between devices, swap(): return lax.ppermute(x, axis, [(i, i ^ k) for i in range(n)])  28.1 us
    ppermute x21, waiting for transfers between devices, swap(): return lax.ppermute(x, axis, [(i, i ^ k) for i in range(n)])  11.9 us
    pallas_call x1, Pallas kernels, fetch_up(): pl.pallas_call(up_fetch_kernel, in_specs=[SMEM, SMEM, ANY, HBM, HBM], out...  6.74 us
    pallas_call x1, Pallas kernels, down(): pl.pallas_call(functools.partial(down_kernel, n), in_specs=[VMEM, VMEM, H...  6.48 us
    pallas_call x1, Pallas kernels, fetch_gate(): pl.pallas_call(gate_fetch_kernel, in_specs=[HBM, HBM], out_specs=[VMEM] *...  6.13 us
    pallas_call x2, Pallas kernels, gate_up(): pl.pallas_call(functools.partial(gate_up_kernel, len(xs)), in_specs=[VMEM...  4.92 us
    pallas_call x1, Pallas kernels, add_delta(): pl.pallas_call(functools.partial(delta_kernel, n), in_specs=[SMEM, SMEM,...  1.54 us
  transfers between devices with their start and end apart: 21, of which 8 were waited for; matrix products, arithmetic and copies ran while one was open for 0% of the time, Pallas kernels for 34%

profile of v3, /device:TPU:0, one launch (start us, length us, event | category | flops | bytes accessed | tf_op | source)
XLA Modules:
  0.0 68.2 jit_solution(13533552236291498106)
XLA Ops:
  0.0 0.0 copy-start.1
  0.0 0.0 copy-start.2
  0.0 5.0 %collective-permute-start = (bf16[16,4096]{1,0:T(8,128)(2,1)}, bf16[16,4096]{1,0:T(8,128)(2,1)S(1)}, u32[]{:S(2)}, u32[]{:S(2)}) collective-permute-start(bf16[16,4096]{1,0:T(8,128)(2,1)} %refs_0_.1), channel_id=1, source_target_pairs={{0,12},{2,14},{4,8},{6,10},{8,4},{10,6},{12,0},{14,2},{1,13},{3,15... | collective-permute-start | bytes 393224 | tf_op jit(solution)/shard_map/ppermute | solution.py:25
  5.1 0.0 collective-permute-start.4
  5.1 1.5 %collective-permute-start.1 = (bf16[16,4096]{1,0:T(8,128)(2,1)}, bf16[16,4096]{1,0:T(8,128)(2,1)S(1)}, u32[]{:S(2)}, u32[]{:S(2)}) collective-permute-start(bf16[16,4096]{1,0:T(8,128)(2,1)} %refs_0_.1), channel_id=1, source_target_pairs={{0,2},{2,0},{4,6},{6,4},{8,10},{10,8},{12,14},{14,12},{1,3},{3,1},... | collective-permute-start | bytes 393224 | tf_op jit(solution)/shard_map/ppermute | solution.py:25
  6.5 0.8 %collective-permute-start.2 = (bf16[16,4096]{1,0:T(8,128)(2,1)}, bf16[16,4096]{1,0:T(8,128)(2,1)S(1)}, u32[]{:S(2)}, u32[]{:S(2)}) collective-permute-start(bf16[16,4096]{1,0:T(8,128)(2,1)} %refs_0_.1), channel_id=1, source_target_pairs={{0,4},{2,6},{4,0},{6,2},{8,12},{10,14},{12,8},{14,10},{1,5},{3,7},... | collective-permute-start | bytes 393224 | tf_op jit(solution)/shard_map/ppermute | solution.py:25
  7.3 1.2 %collective-permute-start.3 = (bf16[16,4096]{1,0:T(8,128)(2,1)}, bf16[16,4096]{1,0:T(8,128)(2,1)S(1)}, u32[]{:S(2)}, u32[]{:S(2)}) collective-permute-start(bf16[16,4096]{1,0:T(8,128)(2,1)} %refs_0_.1), channel_id=1, source_target_pairs={{0,6},{2,4},{4,2},{6,0},{8,14},{10,12},{12,10},{14,8},{1,7},{3,5},... | collective-permute-start | bytes 393224 | tf_op jit(solution)/shard_map/ppermute | solution.py:25
  8.5 6.1 %fetch_gate.1 = (bf16[4096,1024]{1,0:T(8,128)(2,1)S(1)}, bf16[4096,1024]{1,0:T(8,128)(2,1)S(1)}, bf16[8,16,2048]{2,1,0:T(8,128)(2,1)S(1)}, bf16[8,16,2048]{2,1,0:T(8,128)(2,1)S(1)}) custom-call(bf16[4096,2048]{1,0:T(8,128)(2,1)} %weight.3, bf16[8,16,4096]{2,1,0:T(8,128)(2,1)} %adapter_up.1), custom_call_target="tpu_custom_call" | custom-call | bytes 16777216 | tf_op jit(solution)/shard_map/fetch_gate/pallas_call | solution.py:81
  14.7 0.0 collective-permute-done.after.refs_6_
  14.7 0.0 copy-start
  14.7 1.6 %collective-permute-start.6 = (bf16[16,4096]{1,0:T(8,128)(2,1)S(1)}, bf16[16,4096]{1,0:T(8,128)(2,1)S(1)}, u32[]{:S(2)}, u32[]{:S(2)}) collective-permute-start(bf16[16,4096]{1,0:T(8,128)(2,1)S(1)} %collective-permute-done.after.refs_6_), channel_id=1, source_target_pairs={{0,2},{2,0},{4,6},{6,4},{8,10},{10,8},{12,14},{14,12},{1,3},{3,1},... | collective-permute-start | bytes 393224 | tf_op jit(solution)/shard_map/ppermute | solution.py:25
  16.3 0.2 collective-permute-done.4.refs_4_
  16.4 1.5 %collective-permute-start.5 = (bf16[16,4096]{1,0:T(8,128)(2,1)S(1)}, bf16[16,4096]{1,0:T(8,128)(2,1)S(1)}, u32[]{:S(2)}, u32[]{:S(2)}) collective-permute-start(bf16[16,4096]{1,0:T(8,128)(2,1)S(1)} %collective-permute-done.4.refs_4_), channel_id=1, source_target_pairs={{0,2},{2,0},{4,6},{6,4},{8,10},{10,8},{12,14},{14,12},{1,3},{3,1},... | collective-permute-start | bytes 393224 | tf_op jit(solution)/shard_map/ppermute | solution.py:25
  17.9 0.0 collective-permute-done.1.refs_1_
  17.9 0.0 collective-permute-done.2.refs_2_
  17.9 0.4 collective-permute-done.3.refs_3_
  18.3 0.0 copy-done.1
  18.3 0.0 copy-done.2
  18.3 6.7 %fetch_up.1 = (bf16[4096,1024]{1,0:T(8,128)(2,1)S(1)}, bf16[4096,1024]{1,0:T(8,128)(2,1)S(1)}, bf16[160,2048]{1,0:T(8,128)(2,1)S(1)}) custom-call(s32[128]{0:T(128)S(1)} %copy-done.1, s32[10]{0:T(128)S(1)} %copy-done.2, bf16[16,4096]{1,0:T(8,128)(2,1)S(1)} %collective-permute-done.after.refs_6_, bf16[4096,2048]{1,0:T(8,128)(2,1)} %weight.4, ...), custom_call_target="tpu_custom_call" | custom-call | tf_op jit(solution)/shard_map/fetch_up/pallas_call | solution.py:110
  25.1 0.0 collective-permute-done.6.refs_7_
  25.1 0.0 collective-permute-done.5.refs_5_
  25.1 0.0 copy-done
  25.1 2.4 %gate_up.2 = (f32[2,128,1024]{2,1,0:T(8,128)S(1)}, bf16[128,4096]{1,0:T(8,128)(2,1)S(1)}) custom-call(bf16[16,4096]{1,0:T(8,128)(2,1)S(1)} %copy-done, bf16[16,4096]{1,0:T(8,128)(2,1)S(1)} %collective-permute-done.1.refs_1_, bf16[16,4096]{1,0:T(8,128)(2,1)S(1)} %collective-permute-done.2.refs_2_, bf16[16,4096]{1,0:T(8,128)(2,1)S(1)} %collective-permute-done.3.refs_3_, ...), custom_call_target="tpu_custom_call" | custom-call | tf_op jit(solution)/shard_map/gate_up/pallas_call | solution.py:146
  27.6 0.1 collective-permute-start.7
  27.6 0.9 %collective-permute-start.10 = (bf16[8,16,2048]{2,1,0:T(8,128)(2,1)S(1)}, bf16[8,16,2048]{2,1,0:T(8,128)(2,1)S(1)}, u32[]{:S(2)}, u32[]{:S(2)}) collective-permute-start(bf16[8,16,2048]{2,1,0:T(8,128)(2,1)S(1)} %get-tuple-element.65.up_x), channel_id=1, source_target_pairs={{0,2},{2,0},{4,6},{6,4},{8,10},{10,8},{12,14},{14,12},{1,3},{3,1},... | collective-permute-start | bytes 1572872 | tf_op jit(solution)/shard_map/ppermute | solution.py:25
  28.5 1.4 %collective-permute-start.11 = (bf16[8,16,2048]{2,1,0:T(8,128)(2,1)S(1)}, bf16[8,16,2048]{2,1,0:T(8,128)(2,1)S(1)}, u32[]{:S(2)}, u32[]{:S(2)}) collective-permute-start(bf16[8,16,2048]{2,1,0:T(8,128)(2,1)S(1)} %get-tuple-element.66.up_z), channel_id=1, source_target_pairs={{0,4},{2,6},{4,0},{6,2},{8,12},{10,14},{12,8},{14,10},{1,5},{3,7},... | collective-permute-start | bytes 1572872 | tf_op jit(solution)/shard_map/ppermute | solution.py:25
  29.9 2.5 %gate_up.3.kept = f32[2,128,1024]{2,1,0:T(8,128)S(1)} custom-call(bf16[128,4096]{1,0:T(8,128)(2,1)S(1)} %get-tuple-element.54.refs_0_, bf16[4096,1024]{1,0:T(8,128)(2,1)S(1)} %get-tuple-element.55.refs_1_, bf16[4096,1024]{1,0:T(8,128)(2,1)S(1)} %get-tuple-element.56.refs_2_), custom_call_target="tpu_custom_call" | custom-call | tf_op jit(solution)/shard_map/gate_up/pallas_call | solution.py:146
  32.4 0.0 collective-permute-done.7.got
  32.4 0.3 silu.1.mine
  32.7 0.1 collective-permute-start.8
  32.8 1.5 %collective-permute-done.8.other = bf16[128,1024]{1,0:T(8,128)(2,1)S(1)} collective-permute-done((bf16[128,1024]{1,0:T(8,128)(2,1)S(1)}, bf16[128,1024]{1,0:T(8,128)(2,1)S(1)}, u32[]{:S(2)}, u32[]{:S(2)}) %collective-permute-start.8) | collective-permute-done | bytes 262176 | tf_op jit(solution)/shard_map/ppermute | solution.py:25
  34.3 1.1 %shrink.1.a = f32[16,128]{1,0:T(8,128)S(1)} custom-call(s32[128]{0:T(128)S(1)} %copy-done.1, s32[10]{0:T(128)S(1)} %copy-done.2, s32[1,128]{1,0:T(1,128)S(1)} %bitcast.1, bf16[128,1024]{1,0:T(8,128)(2,1)S(1)} %silu.1.mine, bf16[128,1024]{1,0:T(8,128)(2,1)S(1)} %collective-permute-done.8.other, bf16[160,2048]{1,0:T(8,128)(2,1)S(1)} %get-tuple-element.58.factors), custom_call_target="tpu_custom_call" | custom-call | tf_op jit(solution)/shard_map/shrink/pallas_call | solution.py:209
  35.4 0.0 copy-start.3
  35.4 1.6 %collective-permute-start.9 = (f32[16,128]{1,0:T(8,128)S(1)}, f32[16,128]{1,0:T(8,128)S(1)}, u32[]{:S(2)}, u32[]{:S(2)}) collective-permute-start(f32[16,128]{1,0:T(8,128)S(1)} %shrink.1.a), channel_id=1, source_target_pairs={{0,2},{2,0},{4,6},{6,4},{8,10},{10,8},{12,14},{14,12},{1,3},{3,1},... | collective-permute-start | bytes 24584 | tf_op jit(solution)/shard_map/ppermute | solution.py:25
  37.0 6.5 %down.1 = (f32[128,2048]{1,0:T(8,128)S(1)}, f32[128,2048]{1,0:T(8,128)S(1)}, bf16[48,2048]{1,0:T(8,128)(2,1)S(1)}, bf16[48,2048]{1,0:T(8,128)(2,1)S(1)}) custom-call(bf16[128,1024]{1,0:T(8,128)(2,1)S(1)} %silu.1.mine, bf16[128,1024]{1,0:T(8,128)(2,1)S(1)} %collective-permute-done.8.other, bf16[2048,4096]{1,0:T(8,128)(2,1)} %weight.5), custom_call_target="tpu_custom_call" | custom-call | tf_op jit(solution)/shard_map/down/pallas_call | solution.py:257
  43.5 0.0 collective-permute-done.10.next_x
  43.5 0.0 collective-permute-done.11.next_z
  43.5 0.0 collective-permute-done.9.b
  43.5 0.4 collective-permute-start.12
  44.0 1.5 %collective-permute-start.14 = (bf16[48,2048]{1,0:T(8,128)(2,1)S(1)}, bf16[48,2048]{1,0:T(8,128)(2,1)S(1)}, u32[]{:S(2)}, u32[]{:S(2)}) collective-permute-start(bf16[48,2048]{1,0:T(8,128)(2,1)S(1)} %get-tuple-element.74), channel_id=1, source_target_pairs={{0,2},{2,0},{4,6},{6,4},{8,10},{10,8},{12,14},{14,12},{1,3},{3,1},... | collective-permute-start | bytes 589832 | tf_op jit(solution)/shard_map/ppermute | solution.py:25
  45.4 1.8 %collective-permute-done.12.b = f32[16,128]{1,0:T(8,128)S(1)} collective-permute-done((f32[16,128]{1,0:T(8,128)S(1)}, f32[16,128]{1,0:T(8,128)S(1)}, u32[]{:S(2)}, u32[]{:S(2)}) %collective-permute-start.12) | collective-permute-done | bytes 8224 | tf_op jit(solution)/shard_map/ppermute | solution.py:25
  47.3 0.4 collective-permute-start.15
  47.6 2.2 %collective-permute-start.13 = (f32[16,128]{1,0:T(8,128)S(1)}, f32[16,128]{1,0:T(8,128)S(1)}, u32[]{:S(2)}, u32[]{:S(2)}) collective-permute-start(f32[16,128]{1,0:T(8,128)S(1)} %plus.4.a), channel_id=1, source_target_pairs={{0,8},{2,10},{4,12},{6,14},{8,0},{10,2},{12,4},{14,6},{1,9},{3,11}... | collective-permute-start | bytes 24584 | tf_op jit(solution)/shard_map/ppermute | solution.py:25
  49.8 2.4 %collective-permute-done.13.b = f32[16,128]{1,0:T(8,128)S(1)} collective-permute-done((f32[16,128]{1,0:T(8,128)S(1)}, f32[16,128]{1,0:T(8,128)S(1)}, u32[]{:S(2)}, u32[]{:S(2)}) %collective-permute-start.13) | collective-permute-done | bytes 8224 | tf_op jit(solution)/shard_map/ppermute | solution.py:25
  52.3 0.0 collective-permute-done.14.refs_0_
  52.3 0.7 %collective-permute-done.15.refs_1_ = bf16[48,2048]{1,0:T(8,128)(2,1)S(1)} collective-permute-done((bf16[48,2048]{1,0:T(8,128)(2,1)S(1)}, bf16[48,2048]{1,0:T(8,128)(2,1)S(1)}, u32[]{:S(2)}, u32[]{:S(2)}) %collective-permute-start.15) | collective-permute-done | bytes 196640 | tf_op jit(solution)/shard_map/ppermute | solution.py:25
  53.0 0.0 copy-done.3
  53.0 1.5 %add_delta.1 = (bf16[16,4096]{1,0:T(8,128)(2,1)S(1)}, bf16[16,4096]{1,0:T(8,128)(2,1)S(1)}, bf16[16,4096]{1,0:T(8,128)(2,1)S(1)}, bf16[16,4096]{1,0:T(8,128)(2,1...) custom-call(s32[128]{0:T(128)S(1)} %copy-done.1, s32[10]{0:T(128)S(1)} %copy-done.2, s32[64]{0:T(128)S(1)} %copy-done.3, ...), custom_call_target="tpu_custom_call" | custom-call | tf_op jit(solution)/shard_map/add_delta/pallas_call | solution.py:334
  54.6 2.2 %collective-permute-start.20 = (bf16[16,4096]{1,0:T(8,128)(2,1)S(1)}, bf16[16,4096]{1,0:T(8,128)(2,1)S(1)}, u32[]{:S(2)}, u32[]{:S(2)}) collective-permute-start(bf16[16,4096]{1,0:T(8,128)(2,1)S(1)} %get-tuple-element.81), channel_id=1, source_target_pairs={{0,8},{2,10},{4,12},{6,14},{8,0},{10,2},{12,4},{14,6},{1,9},{3,11}... | collective-permute-start | bytes 393224 | tf_op jit(solution)/shard_map/ppermute | solution.py:25
  56.8 0.7 %collective-permute-start.16 = (bf16[16,4096]{1,0:T(8,128)(2,1)S(1)}, bf16[16,4096]{1,0:T(8,128)(2,1)S(1)}, u32[]{:S(2)}, u32[]{:S(2)}) collective-permute-start(bf16[16,4096]{1,0:T(8,128)(2,1)S(1)} %get-tuple-element.77), channel_id=1, source_target_pairs={{0,2},{2,0},{4,6},{6,4},{8,10},{10,8},{12,14},{14,12},{1,3},{3,1},... | collective-permute-start | bytes 393224 | tf_op jit(solution)/shard_map/ppermute | solution.py:25
  57.5 1.2 %collective-permute-start.17 = (bf16[16,4096]{1,0:T(8,128)(2,1)S(1)}, bf16[16,4096]{1,0:T(8,128)(2,1)S(1)}, u32[]{:S(2)}, u32[]{:S(2)}) collective-permute-start(bf16[16,4096]{1,0:T(8,128)(2,1)S(1)} %get-tuple-element.78), channel_id=1, source_target_pairs={{0,4},{2,6},{4,0},{6,2},{8,12},{10,14},{12,8},{14,10},{1,5},{3,7},... | collective-permute-start | bytes 393224 | tf_op jit(solution)/shard_map/ppermute | solution.py:25
  58.7 2.6 %collective-permute-start.18 = (bf16[16,2048]{1,0:T(8,128)(2,1)S(1)}, bf16[16,2048]{1,0:T(8,128)(2,1)S(1)}, u32[]{:S(2)}, u32[]{:S(2)}) collective-permute-start(bf16[16,2048]{1,0:T(8,128)(2,1)S(1)} %get-tuple-element.79), channel_id=1, source_target_pairs={{0,10},{2,8},{4,14},{6,12},{8,2},{10,0},{12,6},{14,4},{1,11},{3,9}... | collective-permute-start | bytes 196616 | tf_op jit(solution)/shard_map/ppermute | solution.py:25
  61.3 1.4 %collective-permute-start.19 = (bf16[16,2048]{1,0:T(8,128)(2,1)S(1)}, bf16[16,2048]{1,0:T(8,128)(2,1)S(1)}, u32[]{:S(2)}, u32[]{:S(2)}) collective-permute-start(bf16[16,2048]{1,0:T(8,128)(2,1)S(1)} %get-tuple-element.80), channel_id=1, source_target_pairs={{0,12},{2,14},{4,8},{6,10},{8,4},{10,6},{12,0},{14,2},{1,13},{3,15... | collective-permute-start | bytes 196616 | tf_op jit(solution)/shard_map/ppermute | solution.py:25
  62.7 3.6 %collective-permute-done.18.refs_5_ = bf16[16,2048]{1,0:T(8,128)(2,1)S(1)} collective-permute-done((bf16[16,2048]{1,0:T(8,128)(2,1)S(1)}, bf16[16,2048]{1,0:T(8,128)(2,1)S(1)}, u32[]{:S(2)}, u32[]{:S(2)}) %collective-permute-start.18) | collective-permute-done | bytes 65568 | tf_op jit(solution)/shard_map/ppermute | solution.py:25
  66.3 1.2 %collective-permute-done.19.refs_4_ = bf16[16,2048]{1,0:T(8,128)(2,1)S(1)} collective-permute-done((bf16[16,2048]{1,0:T(8,128)(2,1)S(1)}, bf16[16,2048]{1,0:T(8,128)(2,1)S(1)}, u32[]{:S(2)}, u32[]{:S(2)}) %collective-permute-start.19) | collective-permute-done | bytes 65568 | tf_op jit(solution)/shard_map/ppermute | solution.py:25
  67.5 0.0 collective-permute-done.20.refs_3_
  67.5 0.0 collective-permute-done.16.refs_1_
  67.5 0.0 collective-permute-done.17.refs_2_
  67.5 0.7 %sum_rows.1 = bf16[16,4096]{1,0:T(8,128)(2,1)} custom-call(bf16[16,4096]{1,0:T(8,128)(2,1)S(1)} %get-tuple-element.76.refs_0_, bf16[16,4096]{1,0:T(8,128)(2,1)S(1)} %collective-permute-done.16.refs_1_, bf16[16,4096]{1,0:T(8,128)(2,1)S(1)} %collective-permute-done.17.refs_2_, bf16[16,4096]{1,0:T(8,128)(2,1)S(1)} %collective-permute-done.20.refs_3_, ...), custom_call_target="tpu_custom_call" | custom-call | tf_op jit(solution)/shard_map/sum_rows/pallas_call | solution.py:362
  (3 shorter events, 0.0 us)
Async XLA Ops:
  0.0 18.3 %copy-start.1 = (s32[128]{0:T(128)S(1)}, s32[128]{0:T(128)}, u32[]{:S(2)}) copy-start(s32[128]{0:T(128)} %row_adapter.5) | copy-start | bytes 1540
  0.0 18.3 %copy-start.2 = (s32[10]{0:T(128)S(1)}, s32[10]{0:T(128)}, u32[]{:S(2)}) copy-start(s32[10]{0:T(128)} %block_first.5) | copy-start | bytes 124
  0.0 14.7 %collective-permute-start = (bf16[16,4096]{1,0:T(8,128)(2,1)}, bf16[16,4096]{1,0:T(8,128)(2,1)S(1)}, u32[]{:S(2)}, u32[]{:S(2)}) collective-permute-start(bf16[16,4096]{1,0:T(8,128)(2,1)} %refs_0_.1), channel_id=1, source_target_pairs={{0,12},{2,14},{4,8},{6,10},{8,4},{10,6},{12,0},{14,2},{1,13},{3,15... | collective-permute-start | bytes 393224 | tf_op jit(solution)/shard_map/ppermute | solution.py:25
  5.1 11.4 %collective-permute-start.4 = (bf16[16,4096]{1,0:T(8,128)(2,1)}, bf16[16,4096]{1,0:T(8,128)(2,1)S(1)}, u32[]{:S(2)}, u32[]{:S(2)}) collective-permute-start(bf16[16,4096]{1,0:T(8,128)(2,1)} %refs_0_.1), channel_id=1, source_target_pairs={{0,8},{2,10},{4,12},{6,14},{8,0},{10,2},{12,4},{14,6},{1,9},{3,11}... | collective-permute-start | bytes 393224 | tf_op jit(solution)/shard_map/ppermute | solution.py:25
  5.1 12.9 %collective-permute-start.1 = (bf16[16,4096]{1,0:T(8,128)(2,1)}, bf16[16,4096]{1,0:T(8,128)(2,1)S(1)}, u32[]{:S(2)}, u32[]{:S(2)}) collective-permute-start(bf16[16,4096]{1,0:T(8,128)(2,1)} %refs_0_.1), channel_id=1, source_target_pairs={{0,2},{2,0},{4,6},{6,4},{8,10},{10,8},{12,14},{14,12},{1,3},{3,1},... | collective-permute-start | bytes 393224 | tf_op jit(solution)/shard_map/ppermute | solution.py:25
  6.5 11.4 %collective-permute-start.2 = (bf16[16,4096]{1,0:T(8,128)(2,1)}, bf16[16,4096]{1,0:T(8,128)(2,1)S(1)}, u32[]{:S(2)}, u32[]{:S(2)}) collective-permute-start(bf16[16,4096]{1,0:T(8,128)(2,1)} %refs_0_.1), channel_id=1, source_target_pairs={{0,4},{2,6},{4,0},{6,2},{8,12},{10,14},{12,8},{14,10},{1,5},{3,7},... | collective-permute-start | bytes 393224 | tf_op jit(solution)/shard_map/ppermute | solution.py:25
  7.3 11.0 %collective-permute-start.3 = (bf16[16,4096]{1,0:T(8,128)(2,1)}, bf16[16,4096]{1,0:T(8,128)(2,1)S(1)}, u32[]{:S(2)}, u32[]{:S(2)}) collective-permute-start(bf16[16,4096]{1,0:T(8,128)(2,1)} %refs_0_.1), channel_id=1, source_target_pairs={{0,6},{2,4},{4,2},{6,0},{8,14},{10,12},{12,10},{14,8},{1,7},{3,5},... | collective-permute-start | bytes 393224 | tf_op jit(solution)/shard_map/ppermute | solution.py:25
  14.7 10.4 %copy-start = (bf16[16,4096]{1,0:T(8,128)(2,1)S(1)}, bf16[16,4096]{1,0:T(8,128)(2,1)}, u32[]{:S(2)}) copy-start(bf16[16,4096]{1,0:T(8,128)(2,1)} %refs_0_.1) | copy-start | bytes 393220
  14.7 10.4 %collective-permute-start.6 = (bf16[16,4096]{1,0:T(8,128)(2,1)S(1)}, bf16[16,4096]{1,0:T(8,128)(2,1)S(1)}, u32[]{:S(2)}, u32[]{:S(2)}) collective-permute-start(bf16[16,4096]{1,0:T(8,128)(2,1)S(1)} %collective-permute-done.after.refs_6_), channel_id=1, source_target_pairs={{0,2},{2,0},{4,6},{6,4},{8,10},{10,8},{12,14},{14,12},{1,3},{3,1},... | collective-permute-start | bytes 393224 | tf_op jit(solution)/shard_map/ppermute | solution.py:25
  16.4 8.6 %collective-permute-start.5 = (bf16[16,4096]{1,0:T(8,128)(2,1)S(1)}, bf16[16,4096]{1,0:T(8,128)(2,1)S(1)}, u32[]{:S(2)}, u32[]{:S(2)}) collective-permute-start(bf16[16,4096]{1,0:T(8,128)(2,1)S(1)} %collective-permute-done.4.refs_4_), channel_id=1, source_target_pairs={{0,2},{2,0},{4,6},{6,4},{8,10},{10,8},{12,14},{14,12},{1,3},{3,1},... | collective-permute-start | bytes 393224 | tf_op jit(solution)/shard_map/ppermute | solution.py:25
  27.6 4.9 %collective-permute-start.7 = (f32[2,128,1024]{2,1,0:T(8,128)S(1)}, f32[2,128,1024]{2,1,0:T(8,128)S(1)}, u32[]{:S(2)}, u32[]{:S(2)}) collective-permute-start(f32[2,128,1024]{2,1,0:T(8,128)S(1)} %get-tuple-element.57), channel_id=1, source_target_pairs={{0,1},{1,0},{2,3},{3,2},{4,5},{5,4},{6,7},{7,6},{8,9},{9,8},{10,11... | collective-permute-start | bytes 3145736 | tf_op jit(solution)/shard_map/ppermute | solution.py:25
  27.6 15.9 %collective-permute-start.10 = (bf16[8,16,2048]{2,1,0:T(8,128)(2,1)S(1)}, bf16[8,16,2048]{2,1,0:T(8,128)(2,1)S(1)}, u32[]{:S(2)}, u32[]{:S(2)}) collective-permute-start(bf16[8,16,2048]{2,1,0:T(8,128)(2,1)S(1)} %get-tuple-element.65.up_x), channel_id=1, source_target_pairs={{0,2},{2,0},{4,6},{6,4},{8,10},{10,8},{12,14},{14,12},{1,3},{3,1},... | collective-permute-start | bytes 1572872 | tf_op jit(solution)/shard_map/ppermute | solution.py:25
  28.5 15.0 %collective-permute-start.11 = (bf16[8,16,2048]{2,1,0:T(8,128)(2,1)S(1)}, bf16[8,16,2048]{2,1,0:T(8,128)(2,1)S(1)}, u32[]{:S(2)}, u32[]{:S(2)}) collective-permute-start(bf16[8,16,2048]{2,1,0:T(8,128)(2,1)S(1)} %get-tuple-element.66.up_z), channel_id=1, source_target_pairs={{0,4},{2,6},{4,0},{6,2},{8,12},{10,14},{12,8},{14,10},{1,5},{3,7},... | collective-permute-start | bytes 1572872 | tf_op jit(solution)/shard_map/ppermute | solution.py:25
  32.7 1.6 %collective-permute-start.8 = (bf16[128,1024]{1,0:T(8,128)(2,1)S(1)}, bf16[128,1024]{1,0:T(8,128)(2,1)S(1)}, u32[]{:S(2)}, u32[]{:S(2)}) collective-permute-start(bf16[128,1024]{1,0:T(8,128)(2,1)S(1)} %silu.1.mine), channel_id=1, source_target_pairs={{0,1},{1,0},{2,3},{3,2},{4,5},{5,4},{6,7},{7,6},{8,9},{9,8},{10,11... | collective-permute-start | bytes 786440 | tf_op jit(solution)/shard_map/ppermute | solution.py:25
  35.4 17.6 %copy-start.3 = (s32[64]{0:T(128)S(1)}, s32[64]{0:T(128)}, u32[]{:S(2)}) copy-start(s32[64]{0:T(128)} %page_table.1) | copy-start | bytes 772
  35.4 8.1 %collective-permute-start.9 = (f32[16,128]{1,0:T(8,128)S(1)}, f32[16,128]{1,0:T(8,128)S(1)}, u32[]{:S(2)}, u32[]{:S(2)}) collective-permute-start(f32[16,128]{1,0:T(8,128)S(1)} %shrink.1.a), channel_id=1, source_target_pairs={{0,2},{2,0},{4,6},{6,4},{8,10},{10,8},{12,14},{14,12},{1,3},{3,1},... | collective-permute-start | bytes 24584 | tf_op jit(solution)/shard_map/ppermute | solution.py:25
  43.5 3.7 %collective-permute-start.12 = (f32[16,128]{1,0:T(8,128)S(1)}, f32[16,128]{1,0:T(8,128)S(1)}, u32[]{:S(2)}, u32[]{:S(2)}) collective-permute-start(f32[16,128]{1,0:T(8,128)S(1)} %plus.3.a), channel_id=1, source_target_pairs={{0,4},{2,6},{4,0},{6,2},{8,12},{10,14},{12,8},{14,10},{1,5},{3,7},... | collective-permute-start | bytes 24584 | tf_op jit(solution)/shard_map/ppermute | solution.py:25
  44.0 8.3 %collective-permute-start.14 = (bf16[48,2048]{1,0:T(8,128)(2,1)S(1)}, bf16[48,2048]{1,0:T(8,128)(2,1)S(1)}, u32[]{:S(2)}, u32[]{:S(2)}) collective-permute-start(bf16[48,2048]{1,0:T(8,128)(2,1)S(1)} %get-tuple-element.74), channel_id=1, source_target_pairs={{0,2},{2,0},{4,6},{6,4},{8,10},{10,8},{12,14},{14,12},{1,3},{3,1},... | collective-permute-start | bytes 589832 | tf_op jit(solution)/shard_map/ppermute | solution.py:25
  47.3 5.8 %collective-permute-start.15 = (bf16[48,2048]{1,0:T(8,128)(2,1)S(1)}, bf16[48,2048]{1,0:T(8,128)(2,1)S(1)}, u32[]{:S(2)}, u32[]{:S(2)}) collective-permute-start(bf16[48,2048]{1,0:T(8,128)(2,1)S(1)} %get-tuple-element.75), channel_id=1, source_target_pairs={{0,4},{2,6},{4,0},{6,2},{8,12},{10,14},{12,8},{14,10},{1,5},{3,7},... | collective-permute-start | bytes 589832 | tf_op jit(solution)/shard_map/ppermute | solution.py:25
  47.6 4.7 %collective-permute-start.13 = (f32[16,128]{1,0:T(8,128)S(1)}, f32[16,128]{1,0:T(8,128)S(1)}, u32[]{:S(2)}, u32[]{:S(2)}) collective-permute-start(f32[16,128]{1,0:T(8,128)S(1)} %plus.4.a), channel_id=1, source_target_pairs={{0,8},{2,10},{4,12},{6,14},{8,0},{10,2},{12,4},{14,6},{1,9},{3,11}... | collective-permute-start | bytes 24584 | tf_op jit(solution)/shard_map/ppermute | solution.py:25
  54.6 12.9 %collective-permute-start.20 = (bf16[16,4096]{1,0:T(8,128)(2,1)S(1)}, bf16[16,4096]{1,0:T(8,128)(2,1)S(1)}, u32[]{:S(2)}, u32[]{:S(2)}) collective-permute-start(bf16[16,4096]{1,0:T(8,128)(2,1)S(1)} %get-tuple-element.81), channel_id=1, source_target_pairs={{0,8},{2,10},{4,12},{6,14},{8,0},{10,2},{12,4},{14,6},{1,9},{3,11}... | collective-permute-start | bytes 393224 | tf_op jit(solution)/shard_map/ppermute | solution.py:25
  56.8 10.7 %collective-permute-start.16 = (bf16[16,4096]{1,0:T(8,128)(2,1)S(1)}, bf16[16,4096]{1,0:T(8,128)(2,1)S(1)}, u32[]{:S(2)}, u32[]{:S(2)}) collective-permute-start(bf16[16,4096]{1,0:T(8,128)(2,1)S(1)} %get-tuple-element.77), channel_id=1, source_target_pairs={{0,2},{2,0},{4,6},{6,4},{8,10},{10,8},{12,14},{14,12},{1,3},{3,1},... | collective-permute-start | bytes 393224 | tf_op jit(solution)/shard_map/ppermute | solution.py:25
  57.5 10.0 %collective-permute-start.17 = (bf16[16,4096]{1,0:T(8,128)(2,1)S(1)}, bf16[16,4096]{1,0:T(8,128)(2,1)S(1)}, u32[]{:S(2)}, u32[]{:S(2)}) collective-permute-start(bf16[16,4096]{1,0:T(8,128)(2,1)S(1)} %get-tuple-element.78), channel_id=1, source_target_pairs={{0,4},{2,6},{4,0},{6,2},{8,12},{10,14},{12,8},{14,10},{1,5},{3,7},... | collective-permute-start | bytes 393224 | tf_op jit(solution)/shard_map/ppermute | solution.py:25
  58.7 7.6 %collective-permute-start.18 = (bf16[16,2048]{1,0:T(8,128)(2,1)S(1)}, bf16[16,2048]{1,0:T(8,128)(2,1)S(1)}, u32[]{:S(2)}, u32[]{:S(2)}) collective-permute-start(bf16[16,2048]{1,0:T(8,128)(2,1)S(1)} %get-tuple-element.79), channel_id=1, source_target_pairs={{0,10},{2,8},{4,14},{6,12},{8,2},{10,0},{12,6},{14,4},{1,11},{3,9}... | collective-permute-start | bytes 196616 | tf_op jit(solution)/shard_map/ppermute | solution.py:25
  61.3 6.2 %collective-permute-start.19 = (bf16[16,2048]{1,0:T(8,128)(2,1)S(1)}, bf16[16,2048]{1,0:T(8,128)(2,1)S(1)}, u32[]{:S(2)}, u32[]{:S(2)}) collective-permute-start(bf16[16,2048]{1,0:T(8,128)(2,1)S(1)} %get-tuple-element.80), channel_id=1, source_target_pairs={{0,12},{2,14},{4,8},{6,10},{8,4},{10,6},{12,0},{14,2},{1,13},{3,15... | collective-permute-start | bytes 196616 | tf_op jit(solution)/shard_map/ppermute | solution.py:25

commit v4 on v3

--- a/solution.py
+++ b/solution.py
@@ -62,9 +62,20 @@
     )
 
 
-def gate_fetch_kernel(weight, adapter_up, sent, kept, up_x, up_z, sems, up_sems):
+def kept_parts(width):
+    half = width // 2
+    return [half // 2] * 2 if half % 256 == 0 else [half]
+
+
+def kept_columns(part, width, total):
+    start = lax.axis_index("tensor") * (total // 2) + part * width
+    return pl.ds(pl.multiple_of(start, 128), width)
+
+
+def gate_fetch_kernel(weight, up, adapter_up, sent, kept, up_first, up_x, up_z, sems, up_sems):
     width = up_x.shape[2]
     moves = weight_moves(weight, sent, kept, sems)
+    moves += copies(up, up_first, kept_columns(0, up_first.shape[1], up.shape[1]), sems.at[2])
     for h, out in enumerate((up_x, up_z)):
         moves.append(pltpu.make_async_copy(adapter_up.at[:, :, pl.ds(h * width, width)], out, up_sems.at[h]))
     for move in moves:
@@ -73,26 +84,30 @@
         move.wait()
 
 
-def fetch_gate(weight, adapter_up):
+def fetch_gate(weight, up, adapter_up):
     depth, width = weight.shape
     half = jax.ShapeDtypeStruct((depth, width // 2), weight.dtype)
+    first = jax.ShapeDtypeStruct((depth, kept_parts(width)[0]), weight.dtype)
     slots, rank, out_width = adapter_up.shape
     pages = jax.ShapeDtypeStruct((slots, rank, out_width // 2), adapter_up.dtype)
     return pl.pallas_call(
         gate_fetch_kernel,
-        in_specs=[HBM, HBM],
-        out_specs=[VMEM] * 4,
-        out_shape=[half, half, pages, pages],
-        scratch_shapes=[pltpu.SemaphoreType.DMA((2, 4)), pltpu.SemaphoreType.DMA((2,))],
+        in_specs=[HBM, HBM, HBM],
+        out_specs=[VMEM] * 5,
+        out_shape=[half, half, first, pages, pages],
+        scratch_shapes=[pltpu.SemaphoreType.DMA((3, 4)), pltpu.SemaphoreType.DMA((2,))],
         compiler_params=pltpu.CompilerParams(vmem_limit_bytes=LIMIT * MIB),
         cost_estimate=pl.CostEstimate(flops=0, bytes_accessed=2 * weight.size, transcendentals=0),
         name="fetch_gate",
-    )(stay(weight), stay(adapter_up))
-
-
-def up_fetch_kernel(row_adapter, block_first, after, weight, adapter_down, sent, kept, factors, sems, block_sems):
+    )(stay(weight), stay(up), stay(adapter_up))
+
+
+def up_fetch_kernel(row_adapter, block_first, after, weight, adapter_down, sent, factors, *refs):
+    more, (sems, block_sems) = refs[:-2], refs[-2:]
     count, rank = block_first.shape[0], adapter_down.shape[1]
-    moves = weight_moves(weight, sent, kept, sems)
+    moves = copies(weight, sent, half_columns(sent.shape[1], True), sems.at[0])
+    for part, out in enumerate(more, 1):
+        moves += copies(weight, out, kept_columns(part, out.shape[1], weight.shape[1]), sems.at[part])
     for b in range(count):
         adapter = row_adapter[jnp.minimum(block_first[b], row_adapter.shape[0] - 1)]
         place = factors.at[pl.ds(b * rank, rank)]
@@ -106,12 +121,13 @@
 def fetch_up(row_adapter, block_first, after, weight, adapter_down):
     depth, width = weight.shape
     half = jax.ShapeDtypeStruct((depth, width // 2), weight.dtype)
+    more = [jax.ShapeDtypeStruct((depth, part), weight.dtype) for part in kept_parts(width)[1:]]
     count, (_, rank, hidden_local) = block_first.shape[0], adapter_down.shape
     return pl.pallas_call(
         up_fetch_kernel,
         in_specs=[SMEM, SMEM, ANY, HBM, HBM],
-        out_specs=[VMEM] * 3,
-        out_shape=[half, half, jax.ShapeDtypeStruct((count * rank, hidden_local), adapter_down.dtype)],
+        out_specs=[VMEM] * (2 + len(more)),
+        out_shape=[half, jax.ShapeDtypeStruct((count * rank, hidden_local), adapter_down.dtype), *more],
         scratch_shapes=[pltpu.SemaphoreType.DMA((2, 4)), pltpu.SemaphoreType.DMA((count,))],
         compiler_params=pltpu.CompilerParams(vmem_limit_bytes=LIMIT * MIB),
         cost_estimate=pl.CostEstimate(flops=0, bytes_accessed=0, transcendentals=0),
@@ -119,39 +135,40 @@
     )(row_adapter, block_first, after, stay(weight), stay(adapter_down))
 
 
-def multiply(x, gate, up, out):
+def multiply(x, gate, ups, out):
     width = out.shape[2]
+    part = ups[0].shape[1]
     tile = min(256, width)
     for j in range(0, width, tile):
         out[0, :, j : j + tile] = dot(x[...], gate[:, j : j + tile])
-        out[1, :, j : j + tile] = dot(x[...], up[:, j : j + tile])
-
-
-def gate_up_kernel(n, *refs):
-    xs, (gate, up, out, *rest) = refs[:n], refs[n:]
+        out[1, :, j : j + tile] = dot(x[...], ups[j // part][:, j % part : j % part + tile])
+
+
+def gate_up_kernel(n, parts, *refs):
+    xs, gate, ups, (out, *rest) = refs[:n], refs[n], refs[n + 1 : n + 1 + parts], refs[n + 1 + parts :]
     x = xs[0]
     if rest:
         (x,) = rest
         rows = xs[0].shape[0]
         for k in range(n):
             x[k * rows : (k + 1) * rows, :] = xs[k][...]
-    multiply(x, gate, up, out)
-
-
-def gate_up(xs, gate, up):
+    multiply(x, gate, ups, out)
+
+
+def gate_up(xs, gate, ups):
     total, (depth, width) = sum(x.shape[0] for x in xs), gate.shape
     out = [jax.ShapeDtypeStruct((2, total, width), jnp.float32)]
     if len(xs) > 1:
         out.append(jax.ShapeDtypeStruct((total, depth), jnp.bfloat16))
     return pl.pallas_call(
-        functools.partial(gate_up_kernel, len(xs)),
-        in_specs=[VMEM] * (len(xs) + 2),
+        functools.partial(gate_up_kernel, len(xs), len(ups)),
+        in_specs=[VMEM] * (len(xs) + 1 + len(ups)),
         out_specs=[VMEM] * len(out),
         out_shape=out,
         compiler_params=pltpu.CompilerParams(vmem_limit_bytes=LIMIT * MIB),
         cost_estimate=pl.CostEstimate(flops=0, bytes_accessed=0, transcendentals=0),
         name="gate_up",
-    )(*xs, gate, up)
+    )(*xs, gate, *ups)
 
 
 def silu_kernel(kept, got, hidden):
@@ -401,17 +418,17 @@
     far = [k for k in range(4, n) if k % 2 == 0]
     for k in far + [1, 2, 3]:
         blocks[k] = swap(tokens, "wide", n, k)
-    gate_sent, gate_kept, *ups = fetch_gate(gate_weight, adapter_up)
+    gate_sent, gate_kept, up_first, *ups = fetch_gate(gate_weight, up_weight, adapter_up)
     last = far[-1]
     blocks[last], *ups = lax.optimization_barrier((blocks[last], *ups))
     for k in far:
         blocks[k ^ 1] = swap(blocks[k], "wide", n, 1)
     blocks[last], *blocks[1:4] = lax.optimization_barrier((blocks[last], *blocks[1:4]))
-    up_sent, up_kept, factors = fetch_up(row_adapter, block_first, blocks[last], up_weight, adapter_down)
-    sent, x = gate_up(blocks, gate_sent, up_sent)
+    up_sent, factors, *up_more = fetch_up(row_adapter, block_first, blocks[last], up_weight, adapter_down)
+    sent, x = gate_up(blocks, gate_sent, [up_sent])
     got = swap(sent, "tensor", 2, 1)
     nears = [swap(piece, "wide", n, mask) for piece, (mask, _, _) in zip(ups, relays(n))]
-    (kept,) = gate_up([x], gate_kept, up_kept)
+    (kept,) = gate_up([x], gate_kept, [up_first, *up_more])
     mine = silu(kept, got)
     other = swap(mine, "tensor", 2, 1)
     shrunk = shrink(n, row_adapter, block_first, mine, other, factors)

time: 68.4 us -> 67.1 us (0.981)
  waiting for transfers between devices: 11.9 us -> 11 us
    pallas_call x1, Pallas kernels: 6.74 us -> 5.52 us  [fetch_up(): pl.pallas_call(up_fetch_kernel, in_specs=[SMEM, SMEM, ANY, HBM, HBM], out...]
    pallas_call x3, Pallas kernels: 11 us -> 12.2 us  [the longest x1 7.39 us: fetch_gate(): pl.pallas_call(gate_fetch_kernel, in_specs=[HBM, HBM, HBM], out_specs=[VM...]
    ppermute x21, waiting for transfers between devices: 11.9 us -> 11 us  [swap(): return lax.ppermute(x, axis, [(i, i ^ k) for i in range(n)])]
  transfers between devices with their start and end apart: 21 -> 21, of which waited for: 8 -> 7; matrix products, arithmetic and copies ran while one was open for 0% -> 0% of each run, Pallas kernels for 34% -> 35%
where the time goes in v4:
time: 67.1 us; the launch traced here: 67 us
  starting transfers between devices  27.9 us (42%)
  Pallas kernels  27.9 us (42%)
  waiting for transfers between devices  11 us (16%)
    ppermute x21, starting transfers between devices, swap(): return lax.ppermute(x, axis, [(i, i ^ k) for i in range(n)])  27.9 us
    ppermute x21, waiting for transfers between devices, swap(): return lax.ppermute(x, axis, [(i, i ^ k) for i in range(n)])  11 us
    pallas_call x1, Pallas kernels, fetch_gate(): pl.pallas_call(gate_fetch_kernel, in_specs=[HBM, HBM, HBM], out_specs=[VM...  7.39 us
    pallas_call x1, Pallas kernels, down(): pl.pallas_call(functools.partial(down_kernel, n), in_specs=[VMEM, VMEM, H...  6.48 us
    pallas_call x1, Pallas kernels, fetch_up(): pl.pallas_call(up_fetch_kernel, in_specs=[SMEM, SMEM, ANY, HBM, HBM], out...  5.52 us
    pallas_call x2, Pallas kernels, gate_up(): pl.pallas_call(functools.partial(gate_up_kernel, len(xs), len(ups)), in_s...  4.8 us
    pallas_call x1, Pallas kernels, add_delta(): pl.pallas_call(functools.partial(delta_kernel, n), in_specs=[SMEM, SMEM,...  1.53 us
  transfers between devices with their start and end apart: 21, of which 7 were waited for; matrix products, arithmetic and copies ran while one was open for 0% of the time, Pallas kernels for 35%

profile of v4, /device:TPU:0, one launch (start us, length us, event | category | flops | bytes accessed | tf_op | source)
XLA Modules:
  0.0 67.0 jit_solution(8293730929834201969)
XLA Ops:
  0.0 0.0 copy-start.1
  0.0 0.0 copy-start.2
  0.0 5.0 %collective-permute-start = (bf16[16,4096]{1,0:T(8,128)(2,1)}, bf16[16,4096]{1,0:T(8,128)(2,1)S(1)}, u32[]{:S(2)}, u32[]{:S(2)}) collective-permute-start(bf16[16,4096]{1,0:T(8,128)(2,1)} %refs_0_.1), channel_id=1, source_target_pairs={{0,12},{2,14},{4,8},{6,10},{8,4},{10,6},{12,0},{14,2},{1,13},{3,15... | collective-permute-start | bytes 393224 | tf_op jit(solution)/shard_map/ppermute | solution.py:25
  5.1 0.0 collective-permute-start.4
  5.1 1.5 %collective-permute-start.1 = (bf16[16,4096]{1,0:T(8,128)(2,1)}, bf16[16,4096]{1,0:T(8,128)(2,1)S(1)}, u32[]{:S(2)}, u32[]{:S(2)}) collective-permute-start(bf16[16,4096]{1,0:T(8,128)(2,1)} %refs_0_.1), channel_id=1, source_target_pairs={{0,2},{2,0},{4,6},{6,4},{8,10},{10,8},{12,14},{14,12},{1,3},{3,1},... | collective-permute-start | bytes 393224 | tf_op jit(solution)/shard_map/ppermute | solution.py:25
  6.5 0.8 %collective-permute-start.2 = (bf16[16,4096]{1,0:T(8,128)(2,1)}, bf16[16,4096]{1,0:T(8,128)(2,1)S(1)}, u32[]{:S(2)}, u32[]{:S(2)}) collective-permute-start(bf16[16,4096]{1,0:T(8,128)(2,1)} %refs_0_.1), channel_id=1, source_target_pairs={{0,4},{2,6},{4,0},{6,2},{8,12},{10,14},{12,8},{14,10},{1,5},{3,7},... | collective-permute-start | bytes 393224 | tf_op jit(solution)/shard_map/ppermute | solution.py:25
  7.3 1.2 %collective-permute-start.3 = (bf16[16,4096]{1,0:T(8,128)(2,1)}, bf16[16,4096]{1,0:T(8,128)(2,1)S(1)}, u32[]{:S(2)}, u32[]{:S(2)}) collective-permute-start(bf16[16,4096]{1,0:T(8,128)(2,1)} %refs_0_.1), channel_id=1, source_target_pairs={{0,6},{2,4},{4,2},{6,0},{8,14},{10,12},{12,10},{14,8},{1,7},{3,5},... | collective-permute-start | bytes 393224 | tf_op jit(solution)/shard_map/ppermute | solution.py:25
  8.5 7.4 %fetch_gate.1 = (bf16[4096,1024]{1,0:T(8,128)(2,1)S(1)}, bf16[4096,1024]{1,0:T(8,128)(2,1)S(1)}, bf16[4096,512]{1,0:T(8,128)(2,1)S(1)}, bf16[8,16,2048]{2,1,0:T(8,128)(2,1)S(1)}, bf16[8,16,2048]{2,1,0:T(8,128)(2,1)S(1)}) custom-call(bf16[4096,2048]{1,0:T(8,128)(2,1)} %weight.3, bf16[4096,2048]{1,0:T(8,128)(2,1)} %weight.4, bf16[8,16,4096]{2,1,0:T(8,128)(2,1)} %adapter_up.1), custom_call_target="tpu_custom_call" | custom-call | bytes 16777216 | tf_op jit(solution)/shard_map/fetch_gate/pallas_call | solution.py:93
  15.9 0.0 collective-permute-done.after.refs_6_
  16.0 0.0 copy-start
  16.0 1.6 %collective-permute-start.6 = (bf16[16,4096]{1,0:T(8,128)(2,1)S(1)}, bf16[16,4096]{1,0:T(8,128)(2,1)S(1)}, u32[]{:S(2)}, u32[]{:S(2)}) collective-permute-start(bf16[16,4096]{1,0:T(8,128)(2,1)S(1)} %collective-permute-done.after.refs_6_), channel_id=1, source_target_pairs={{0,2},{2,0},{4,6},{6,4},{8,10},{10,8},{12,14},{14,12},{1,3},{3,1},... | collective-permute-start | bytes 393224 | tf_op jit(solution)/shard_map/ppermute | solution.py:25
  17.5 0.0 collective-permute-done.4.refs_4_
  17.5 0.5 collective-permute-start.5
  18.1 0.0 collective-permute-done.1.refs_1_
  18.1 0.0 collective-permute-done.2.refs_2_
  18.1 0.3 collective-permute-done.3.refs_3_
  18.3 0.0 copy-done.1
  18.3 0.0 copy-done.2
  18.3 5.5 %fetch_up.1 = (bf16[4096,1024]{1,0:T(8,128)(2,1)S(1)}, bf16[160,2048]{1,0:T(8,128)(2,1)S(1)}, bf16[4096,512]{1,0:T(8,128)(2,1)S(1)}) custom-call(s32[128]{0:T(128)S(1)} %copy-done.1, s32[10]{0:T(128)S(1)} %copy-done.2, bf16[16,4096]{1,0:T(8,128)(2,1)S(1)} %collective-permute-done.after.refs_6_, bf16[4096,2048]{1,0:T(8,128)(2,1)} %weight.4, ...), custom_call_target="tpu_custom_call" | custom-call | tf_op jit(solution)/shard_map/fetch_up/pallas_call | solution.py:126
  23.9 0.0 collective-permute-done.6.refs_7_
  23.9 0.0 collective-permute-done.5.refs_5_
  23.9 0.0 copy-done
  23.9 2.4 %gate_up.2 = (f32[2,128,1024]{2,1,0:T(8,128)S(1)}, bf16[128,4096]{1,0:T(8,128)(2,1)S(1)}) custom-call(bf16[16,4096]{1,0:T(8,128)(2,1)S(1)} %copy-done, bf16[16,4096]{1,0:T(8,128)(2,1)S(1)} %collective-permute-done.1.refs_1_, bf16[16,4096]{1,0:T(8,128)(2,1)S(1)} %collective-permute-done.2.refs_2_, bf16[16,4096]{1,0:T(8,128)(2,1)S(1)} %collective-permute-done.3.refs_3_, ...), custom_call_target="tpu_custom_call" | custom-call | tf_op jit(solution)/shard_map/gate_up/pallas_call | solution.py:163
  26.3 0.1 collective-permute-start.7
  26.4 1.3 %collective-permute-start.10 = (bf16[8,16,2048]{2,1,0:T(8,128)(2,1)S(1)}, bf16[8,16,2048]{2,1,0:T(8,128)(2,1)S(1)}, u32[]{:S(2)}, u32[]{:S(2)}) collective-permute-start(bf16[8,16,2048]{2,1,0:T(8,128)(2,1)S(1)} %get-tuple-element.67.up_x), channel_id=1, source_target_pairs={{0,2},{2,0},{4,6},{6,4},{8,10},{10,8},{12,14},{14,12},{1,3},{3,1},... | collective-permute-start | bytes 1572872 | tf_op jit(solution)/shard_map/ppermute | solution.py:25
  27.7 1.0 %collective-permute-start.11 = (bf16[8,16,2048]{2,1,0:T(8,128)(2,1)S(1)}, bf16[8,16,2048]{2,1,0:T(8,128)(2,1)S(1)}, u32[]{:S(2)}, u32[]{:S(2)}) collective-permute-start(bf16[8,16,2048]{2,1,0:T(8,128)(2,1)S(1)} %get-tuple-element.68.up_z), channel_id=1, source_target_pairs={{0,4},{2,6},{4,0},{6,2},{8,12},{10,14},{12,8},{14,10},{1,5},{3,7},... | collective-permute-start | bytes 1572872 | tf_op jit(solution)/shard_map/ppermute | solution.py:25
  28.7 2.3 %gate_up.3.kept = f32[2,128,1024]{2,1,0:T(8,128)S(1)} custom-call(bf16[128,4096]{1,0:T(8,128)(2,1)S(1)} %get-tuple-element.55.refs_0_, bf16[4096,1024]{1,0:T(8,128)(2,1)S(1)} %get-tuple-element.56.refs_1_, bf16[4096,512]{1,0:T(8,128)(2,1)S(1)} %get-tuple-element.57.refs_2_, bf16[4096,512]{1,0:T(8,128)(2,1)S(1)} %get-tuple-element.58.refs_3_), custom_call_target="tpu_custom_call" | custom-call | tf_op jit(solution)/shard_map/gate_up/pallas_call | solution.py:163
  31.1 0.0 collective-permute-done.7.got
  31.1 0.3 silu.1.mine
  31.4 0.1 collective-permute-start.8
  31.5 1.5 %collective-permute-done.8.other = bf16[128,1024]{1,0:T(8,128)(2,1)S(1)} collective-permute-done((bf16[128,1024]{1,0:T(8,128)(2,1)S(1)}, bf16[128,1024]{1,0:T(8,128)(2,1)S(1)}, u32[]{:S(2)}, u32[]{:S(2)}) %collective-permute-start.8) | collective-permute-done | bytes 262176 | tf_op jit(solution)/shard_map/ppermute | solution.py:25
  33.0 1.1 %shrink.1.a = f32[16,128]{1,0:T(8,128)S(1)} custom-call(s32[128]{0:T(128)S(1)} %copy-done.1, s32[10]{0:T(128)S(1)} %copy-done.2, s32[1,128]{1,0:T(1,128)S(1)} %bitcast.1, bf16[128,1024]{1,0:T(8,128)(2,1)S(1)} %silu.1.mine, bf16[128,1024]{1,0:T(8,128)(2,1)S(1)} %collective-permute-done.8.other, bf16[160,2048]{1,0:T(8,128)(2,1)S(1)} %get-tuple-element.60.factors), custom_call_target="tpu_custom_call" | custom-call | tf_op jit(solution)/shard_map/shrink/pallas_call | solution.py:226
  34.1 0.0 copy-start.3
  34.1 1.6 %collective-permute-start.9 = (f32[16,128]{1,0:T(8,128)S(1)}, f32[16,128]{1,0:T(8,128)S(1)}, u32[]{:S(2)}, u32[]{:S(2)}) collective-permute-start(f32[16,128]{1,0:T(8,128)S(1)} %shrink.1.a), channel_id=1, source_target_pairs={{0,2},{2,0},{4,6},{6,4},{8,10},{10,8},{12,14},{14,12},{1,3},{3,1},... | collective-permute-start | bytes 24584 | tf_op jit(solution)/shard_map/ppermute | solution.py:25
  35.6 6.5 %down.1 = (f32[128,2048]{1,0:T(8,128)S(1)}, f32[128,2048]{1,0:T(8,128)S(1)}, bf16[48,2048]{1,0:T(8,128)(2,1)S(1)}, bf16[48,2048]{1,0:T(8,128)(2,1)S(1)}) custom-call(bf16[128,1024]{1,0:T(8,128)(2,1)S(1)} %silu.1.mine, bf16[128,1024]{1,0:T(8,128)(2,1)S(1)} %collective-permute-done.8.other, bf16[2048,4096]{1,0:T(8,128)(2,1)} %weight.5), custom_call_target="tpu_custom_call" | custom-call | tf_op jit(solution)/shard_map/down/pallas_call | solution.py:274
  42.1 0.0 collective-permute-done.10.next_x
  42.1 0.0 collective-permute-done.11.next_z
  42.2 0.0 collective-permute-done.9.b
  42.2 0.5 collective-permute-start.12
  42.7 1.5 %collective-permute-start.14 = (bf16[48,2048]{1,0:T(8,128)(2,1)S(1)}, bf16[48,2048]{1,0:T(8,128)(2,1)S(1)}, u32[]{:S(2)}, u32[]{:S(2)}) collective-permute-start(bf16[48,2048]{1,0:T(8,128)(2,1)S(1)} %get-tuple-element.76), channel_id=1, source_target_pairs={{0,2},{2,0},{4,6},{6,4},{8,10},{10,8},{12,14},{14,12},{1,3},{3,1},... | collective-permute-start | bytes 589832 | tf_op jit(solution)/shard_map/ppermute | solution.py:25
  44.2 1.7 %collective-permute-done.12.b = f32[16,128]{1,0:T(8,128)S(1)} collective-permute-done((f32[16,128]{1,0:T(8,128)S(1)}, f32[16,128]{1,0:T(8,128)S(1)}, u32[]{:S(2)}, u32[]{:S(2)}) %collective-permute-start.12) | collective-permute-done | bytes 8224 | tf_op jit(solution)/shard_map/ppermute | solution.py:25
  45.9 0.5 collective-permute-start.15
  46.4 2.6 %collective-permute-start.13 = (f32[16,128]{1,0:T(8,128)S(1)}, f32[16,128]{1,0:T(8,128)S(1)}, u32[]{:S(2)}, u32[]{:S(2)}) collective-permute-start(f32[16,128]{1,0:T(8,128)S(1)} %plus.4.a), channel_id=1, source_target_pairs={{0,8},{2,10},{4,12},{6,14},{8,0},{10,2},{12,4},{14,6},{1,9},{3,11}... | collective-permute-start | bytes 24584 | tf_op jit(solution)/shard_map/ppermute | solution.py:25
  48.9 2.1 %collective-permute-done.13.b = f32[16,128]{1,0:T(8,128)S(1)} collective-permute-done((f32[16,128]{1,0:T(8,128)S(1)}, f32[16,128]{1,0:T(8,128)S(1)}, u32[]{:S(2)}, u32[]{:S(2)}) %collective-permute-start.13) | collective-permute-done | bytes 8224 | tf_op jit(solution)/shard_map/ppermute | solution.py:25
  51.0 0.0 collective-permute-done.14.refs_0_
  51.0 0.6 collective-permute-done.15.refs_1_
  51.7 0.0 copy-done.3
  51.7 1.5 %add_delta.1 = (bf16[16,4096]{1,0:T(8,128)(2,1)S(1)}, bf16[16,4096]{1,0:T(8,128)(2,1)S(1)}, bf16[16,4096]{1,0:T(8,128)(2,1)S(1)}, bf16[16,4096]{1,0:T(8,128)(2,1...) custom-call(s32[128]{0:T(128)S(1)} %copy-done.1, s32[10]{0:T(128)S(1)} %copy-done.2, s32[64]{0:T(128)S(1)} %copy-done.3, ...), custom_call_target="tpu_custom_call" | custom-call | tf_op jit(solution)/shard_map/add_delta/pallas_call | solution.py:351
  53.2 2.4 %collective-permute-start.20 = (bf16[16,4096]{1,0:T(8,128)(2,1)S(1)}, bf16[16,4096]{1,0:T(8,128)(2,1)S(1)}, u32[]{:S(2)}, u32[]{:S(2)}) collective-permute-start(bf16[16,4096]{1,0:T(8,128)(2,1)S(1)} %get-tuple-element.83), channel_id=1, source_target_pairs={{0,8},{2,10},{4,12},{6,14},{8,0},{10,2},{12,4},{14,6},{1,9},{3,11}... | collective-permute-start | bytes 393224 | tf_op jit(solution)/shard_map/ppermute | solution.py:25
  55.6 1.0 %collective-permute-start.16 = (bf16[16,4096]{1,0:T(8,128)(2,1)S(1)}, bf16[16,4096]{1,0:T(8,128)(2,1)S(1)}, u32[]{:S(2)}, u32[]{:S(2)}) collective-permute-start(bf16[16,4096]{1,0:T(8,128)(2,1)S(1)} %get-tuple-element.79), channel_id=1, source_target_pairs={{0,2},{2,0},{4,6},{6,4},{8,10},{10,8},{12,14},{14,12},{1,3},{3,1},... | collective-permute-start | bytes 393224 | tf_op jit(solution)/shard_map/ppermute | solution.py:25
  56.6 1.2 %collective-permute-start.17 = (bf16[16,4096]{1,0:T(8,128)(2,1)S(1)}, bf16[16,4096]{1,0:T(8,128)(2,1)S(1)}, u32[]{:S(2)}, u32[]{:S(2)}) collective-permute-start(bf16[16,4096]{1,0:T(8,128)(2,1)S(1)} %get-tuple-element.80), channel_id=1, source_target_pairs={{0,4},{2,6},{4,0},{6,2},{8,12},{10,14},{12,8},{14,10},{1,5},{3,7},... | collective-permute-start | bytes 393224 | tf_op jit(solution)/shard_map/ppermute | solution.py:25
  57.8 2.3 %collective-permute-start.18 = (bf16[16,2048]{1,0:T(8,128)(2,1)S(1)}, bf16[16,2048]{1,0:T(8,128)(2,1)S(1)}, u32[]{:S(2)}, u32[]{:S(2)}) collective-permute-start(bf16[16,2048]{1,0:T(8,128)(2,1)S(1)} %get-tuple-element.81), channel_id=1, source_target_pairs={{0,10},{2,8},{4,14},{6,12},{8,2},{10,0},{12,6},{14,4},{1,11},{3,9}... | collective-permute-start | bytes 196616 | tf_op jit(solution)/shard_map/ppermute | solution.py:25
  60.1 1.3 %collective-permute-start.19 = (bf16[16,2048]{1,0:T(8,128)(2,1)S(1)}, bf16[16,2048]{1,0:T(8,128)(2,1)S(1)}, u32[]{:S(2)}, u32[]{:S(2)}) collective-permute-start(bf16[16,2048]{1,0:T(8,128)(2,1)S(1)} %get-tuple-element.82), channel_id=1, source_target_pairs={{0,12},{2,14},{4,8},{6,10},{8,4},{10,6},{12,0},{14,2},{1,13},{3,15... | collective-permute-start | bytes 196616 | tf_op jit(solution)/shard_map/ppermute | solution.py:25
  61.5 3.6 %collective-permute-done.18.refs_5_ = bf16[16,2048]{1,0:T(8,128)(2,1)S(1)} collective-permute-done((bf16[16,2048]{1,0:T(8,128)(2,1)S(1)}, bf16[16,2048]{1,0:T(8,128)(2,1)S(1)}, u32[]{:S(2)}, u32[]{:S(2)}) %collective-permute-start.18) | collective-permute-done | bytes 65568 | tf_op jit(solution)/shard_map/ppermute | solution.py:25
  65.1 1.1 %collective-permute-done.19.refs_4_ = bf16[16,2048]{1,0:T(8,128)(2,1)S(1)} collective-permute-done((bf16[16,2048]{1,0:T(8,128)(2,1)S(1)}, bf16[16,2048]{1,0:T(8,128)(2,1)S(1)}, u32[]{:S(2)}, u32[]{:S(2)}) %collective-permute-start.19) | collective-permute-done | bytes 65568 | tf_op jit(solution)/shard_map/ppermute | solution.py:25
  66.2 0.0 collective-permute-done.20.refs_3_
  66.2 0.0 collective-permute-done.16.refs_1_
  66.2 0.0 collective-permute-done.17.refs_2_
  66.2 0.7 %sum_rows.1 = bf16[16,4096]{1,0:T(8,128)(2,1)} custom-call(bf16[16,4096]{1,0:T(8,128)(2,1)S(1)} %get-tuple-element.78.refs_0_, bf16[16,4096]{1,0:T(8,128)(2,1)S(1)} %collective-permute-done.16.refs_1_, bf16[16,4096]{1,0:T(8,128)(2,1)S(1)} %collective-permute-done.17.refs_2_, bf16[16,4096]{1,0:T(8,128)(2,1)S(1)} %collective-permute-done.20.refs_3_, ...), custom_call_target="tpu_custom_call" | custom-call | tf_op jit(solution)/shard_map/sum_rows/pallas_call | solution.py:379
  (3 shorter events, 0.0 us)
Async XLA Ops:
  0.0 18.3 %copy-start.1 = (s32[128]{0:T(128)S(1)}, s32[128]{0:T(128)}, u32[]{:S(2)}) copy-start(s32[128]{0:T(128)} %row_adapter.5) | copy-start | bytes 1540
  0.0 18.3 %copy-start.2 = (s32[10]{0:T(128)S(1)}, s32[10]{0:T(128)}, u32[]{:S(2)}) copy-start(s32[10]{0:T(128)} %block_first.5) | copy-start | bytes 124
  0.0 15.9 %collective-permute-start = (bf16[16,4096]{1,0:T(8,128)(2,1)}, bf16[16,4096]{1,0:T(8,128)(2,1)S(1)}, u32[]{:S(2)}, u32[]{:S(2)}) collective-permute-start(bf16[16,4096]{1,0:T(8,128)(2,1)} %refs_0_.1), channel_id=1, source_target_pairs={{0,12},{2,14},{4,8},{6,10},{8,4},{10,6},{12,0},{14,2},{1,13},{3,15... | collective-permute-start | bytes 393224 | tf_op jit(solution)/shard_map/ppermute | solution.py:25
  5.1 12.5 %collective-permute-start.4 = (bf16[16,4096]{1,0:T(8,128)(2,1)}, bf16[16,4096]{1,0:T(8,128)(2,1)S(1)}, u32[]{:S(2)}, u32[]{:S(2)}) collective-permute-start(bf16[16,4096]{1,0:T(8,128)(2,1)} %refs_0_.1), channel_id=1, source_target_pairs={{0,8},{2,10},{4,12},{6,14},{8,0},{10,2},{12,4},{14,6},{1,9},{3,11}... | collective-permute-start | bytes 393224 | tf_op jit(solution)/shard_map/ppermute | solution.py:25
  5.1 13.0 %collective-permute-start.1 = (bf16[16,4096]{1,0:T(8,128)(2,1)}, bf16[16,4096]{1,0:T(8,128)(2,1)S(1)}, u32[]{:S(2)}, u32[]{:S(2)}) collective-permute-start(bf16[16,4096]{1,0:T(8,128)(2,1)} %refs_0_.1), channel_id=1, source_target_pairs={{0,2},{2,0},{4,6},{6,4},{8,10},{10,8},{12,14},{14,12},{1,3},{3,1},... | collective-permute-start | bytes 393224 | tf_op jit(solution)/shard_map/ppermute | solution.py:25
  6.5 11.5 %collective-permute-start.2 = (bf16[16,4096]{1,0:T(8,128)(2,1)}, bf16[16,4096]{1,0:T(8,128)(2,1)S(1)}, u32[]{:S(2)}, u32[]{:S(2)}) collective-permute-start(bf16[16,4096]{1,0:T(8,128)(2,1)} %refs_0_.1), channel_id=1, source_target_pairs={{0,4},{2,6},{4,0},{6,2},{8,12},{10,14},{12,8},{14,10},{1,5},{3,7},... | collective-permute-start | bytes 393224 | tf_op jit(solution)/shard_map/ppermute | solution.py:25
  7.3 11.0 %collective-permute-start.3 = (bf16[16,4096]{1,0:T(8,128)(2,1)}, bf16[16,4096]{1,0:T(8,128)(2,1)S(1)}, u32[]{:S(2)}, u32[]{:S(2)}) collective-permute-start(bf16[16,4096]{1,0:T(8,128)(2,1)} %refs_0_.1), channel_id=1, source_target_pairs={{0,6},{2,4},{4,2},{6,0},{8,14},{10,12},{12,10},{14,8},{1,7},{3,5},... | collective-permute-start | bytes 393224 | tf_op jit(solution)/shard_map/ppermute | solution.py:25
  16.0 7.9 %copy-start = (bf16[16,4096]{1,0:T(8,128)(2,1)S(1)}, bf16[16,4096]{1,0:T(8,128)(2,1)}, u32[]{:S(2)}) copy-start(bf16[16,4096]{1,0:T(8,128)(2,1)} %refs_0_.1) | copy-start | bytes 393220
  16.0 7.9 %collective-permute-start.6 = (bf16[16,4096]{1,0:T(8,128)(2,1)S(1)}, bf16[16,4096]{1,0:T(8,128)(2,1)S(1)}, u32[]{:S(2)}, u32[]{:S(2)}) collective-permute-start(bf16[16,4096]{1,0:T(8,128)(2,1)S(1)} %collective-permute-done.after.refs_6_), channel_id=1, source_target_pairs={{0,2},{2,0},{4,6},{6,4},{8,10},{10,8},{12,14},{14,12},{1,3},{3,1},... | collective-permute-start | bytes 393224 | tf_op jit(solution)/shard_map/ppermute | solution.py:25
  17.5 6.3 %collective-permute-start.5 = (bf16[16,4096]{1,0:T(8,128)(2,1)S(1)}, bf16[16,4096]{1,0:T(8,128)(2,1)S(1)}, u32[]{:S(2)}, u32[]{:S(2)}) collective-permute-start(bf16[16,4096]{1,0:T(8,128)(2,1)S(1)} %collective-permute-done.4.refs_4_), channel_id=1, source_target_pairs={{0,2},{2,0},{4,6},{6,4},{8,10},{10,8},{12,14},{14,12},{1,3},{3,1},... | collective-permute-start | bytes 393224 | tf_op jit(solution)/shard_map/ppermute | solution.py:25
  26.3 4.7 %collective-permute-start.7 = (f32[2,128,1024]{2,1,0:T(8,128)S(1)}, f32[2,128,1024]{2,1,0:T(8,128)S(1)}, u32[]{:S(2)}, u32[]{:S(2)}) collective-permute-start(f32[2,128,1024]{2,1,0:T(8,128)S(1)} %get-tuple-element.59), channel_id=1, source_target_pairs={{0,1},{1,0},{2,3},{3,2},{4,5},{5,4},{6,7},{7,6},{8,9},{9,8},{10,11... | collective-permute-start | bytes 3145736 | tf_op jit(solution)/shard_map/ppermute | solution.py:25
  26.4 15.7 %collective-permute-start.10 = (bf16[8,16,2048]{2,1,0:T(8,128)(2,1)S(1)}, bf16[8,16,2048]{2,1,0:T(8,128)(2,1)S(1)}, u32[]{:S(2)}, u32[]{:S(2)}) collective-permute-start(bf16[8,16,2048]{2,1,0:T(8,128)(2,1)S(1)} %get-tuple-element.67.up_x), channel_id=1, source_target_pairs={{0,2},{2,0},{4,6},{6,4},{8,10},{10,8},{12,14},{14,12},{1,3},{3,1},... | collective-permute-start | bytes 1572872 | tf_op jit(solution)/shard_map/ppermute | solution.py:25
  27.7 14.4 %collective-permute-start.11 = (bf16[8,16,2048]{2,1,0:T(8,128)(2,1)S(1)}, bf16[8,16,2048]{2,1,0:T(8,128)(2,1)S(1)}, u32[]{:S(2)}, u32[]{:S(2)}) collective-permute-start(bf16[8,16,2048]{2,1,0:T(8,128)(2,1)S(1)} %get-tuple-element.68.up_z), channel_id=1, source_target_pairs={{0,4},{2,6},{4,0},{6,2},{8,12},{10,14},{12,8},{14,10},{1,5},{3,7},... | collective-permute-start | bytes 1572872 | tf_op jit(solution)/shard_map/ppermute | solution.py:25
  31.4 1.6 %collective-permute-start.8 = (bf16[128,1024]{1,0:T(8,128)(2,1)S(1)}, bf16[128,1024]{1,0:T(8,128)(2,1)S(1)}, u32[]{:S(2)}, u32[]{:S(2)}) collective-permute-start(bf16[128,1024]{1,0:T(8,128)(2,1)S(1)} %silu.1.mine), channel_id=1, source_target_pairs={{0,1},{1,0},{2,3},{3,2},{4,5},{5,4},{6,7},{7,6},{8,9},{9,8},{10,11... | collective-permute-start | bytes 786440 | tf_op jit(solution)/shard_map/ppermute | solution.py:25
  34.1 17.6 %copy-start.3 = (s32[64]{0:T(128)S(1)}, s32[64]{0:T(128)}, u32[]{:S(2)}) copy-start(s32[64]{0:T(128)} %page_table.1) | copy-start | bytes 772
  34.1 8.1 %collective-permute-start.9 = (f32[16,128]{1,0:T(8,128)S(1)}, f32[16,128]{1,0:T(8,128)S(1)}, u32[]{:S(2)}, u32[]{:S(2)}) collective-permute-start(f32[16,128]{1,0:T(8,128)S(1)} %shrink.1.a), channel_id=1, source_target_pairs={{0,2},{2,0},{4,6},{6,4},{8,10},{10,8},{12,14},{14,12},{1,3},{3,1},... | collective-permute-start | bytes 24584 | tf_op jit(solution)/shard_map/ppermute | solution.py:25
  42.2 3.7 %collective-permute-start.12 = (f32[16,128]{1,0:T(8,128)S(1)}, f32[16,128]{1,0:T(8,128)S(1)}, u32[]{:S(2)}, u32[]{:S(2)}) collective-permute-start(f32[16,128]{1,0:T(8,128)S(1)} %plus.3.a), channel_id=1, source_target_pairs={{0,4},{2,6},{4,0},{6,2},{8,12},{10,14},{12,8},{14,10},{1,5},{3,7},... | collective-permute-start | bytes 24584 | tf_op jit(solution)/shard_map/ppermute | solution.py:25
  42.7 8.3 %collective-permute-start.14 = (bf16[48,2048]{1,0:T(8,128)(2,1)S(1)}, bf16[48,2048]{1,0:T(8,128)(2,1)S(1)}, u32[]{:S(2)}, u32[]{:S(2)}) collective-permute-start(bf16[48,2048]{1,0:T(8,128)(2,1)S(1)} %get-tuple-element.76), channel_id=1, source_target_pairs={{0,2},{2,0},{4,6},{6,4},{8,10},{10,8},{12,14},{14,12},{1,3},{3,1},... | collective-permute-start | bytes 589832 | tf_op jit(solution)/shard_map/ppermute | solution.py:25
  45.9 5.8 %collective-permute-start.15 = (bf16[48,2048]{1,0:T(8,128)(2,1)S(1)}, bf16[48,2048]{1,0:T(8,128)(2,1)S(1)}, u32[]{:S(2)}, u32[]{:S(2)}) collective-permute-start(bf16[48,2048]{1,0:T(8,128)(2,1)S(1)} %get-tuple-element.77), channel_id=1, source_target_pairs={{0,4},{2,6},{4,0},{6,2},{8,12},{10,14},{12,8},{14,10},{1,5},{3,7},... | collective-permute-start | bytes 589832 | tf_op jit(solution)/shard_map/ppermute | solution.py:25
  46.4 4.7 %collective-permute-start.13 = (f32[16,128]{1,0:T(8,128)S(1)}, f32[16,128]{1,0:T(8,128)S(1)}, u32[]{:S(2)}, u32[]{:S(2)}) collective-permute-start(f32[16,128]{1,0:T(8,128)S(1)} %plus.4.a), channel_id=1, source_target_pairs={{0,8},{2,10},{4,12},{6,14},{8,0},{10,2},{12,4},{14,6},{1,9},{3,11}... | collective-permute-start | bytes 24584 | tf_op jit(solution)/shard_map/ppermute | solution.py:25
  53.2 13.0 %collective-permute-start.20 = (bf16[16,4096]{1,0:T(8,128)(2,1)S(1)}, bf16[16,4096]{1,0:T(8,128)(2,1)S(1)}, u32[]{:S(2)}, u32[]{:S(2)}) collective-permute-start(bf16[16,4096]{1,0:T(8,128)(2,1)S(1)} %get-tuple-element.83), channel_id=1, source_target_pairs={{0,8},{2,10},{4,12},{6,14},{8,0},{10,2},{12,4},{14,6},{1,9},{3,11}... | collective-permute-start | bytes 393224 | tf_op jit(solution)/shard_map/ppermute | solution.py:25
  55.6 10.6 %collective-permute-start.16 = (bf16[16,4096]{1,0:T(8,128)(2,1)S(1)}, bf16[16,4096]{1,0:T(8,128)(2,1)S(1)}, u32[]{:S(2)}, u32[]{:S(2)}) collective-permute-start(bf16[16,4096]{1,0:T(8,128)(2,1)S(1)} %get-tuple-element.79), channel_id=1, source_target_pairs={{0,2},{2,0},{4,6},{6,4},{8,10},{10,8},{12,14},{14,12},{1,3},{3,1},... | collective-permute-start | bytes 393224 | tf_op jit(solution)/shard_map/ppermute | solution.py:25
  56.6 9.6 %collective-permute-start.17 = (bf16[16,4096]{1,0:T(8,128)(2,1)S(1)}, bf16[16,4096]{1,0:T(8,128)(2,1)S(1)}, u32[]{:S(2)}, u32[]{:S(2)}) collective-permute-start(bf16[16,4096]{1,0:T(8,128)(2,1)S(1)} %get-tuple-element.80), channel_id=1, source_target_pairs={{0,4},{2,6},{4,0},{6,2},{8,12},{10,14},{12,8},{14,10},{1,5},{3,7},... | collective-permute-start | bytes 393224 | tf_op jit(solution)/shard_map/ppermute | solution.py:25
  57.8 7.3 %collective-permute-start.18 = (bf16[16,2048]{1,0:T(8,128)(2,1)S(1)}, bf16[16,2048]{1,0:T(8,128)(2,1)S(1)}, u32[]{:S(2)}, u32[]{:S(2)}) collective-permute-start(bf16[16,2048]{1,0:T(8,128)(2,1)S(1)} %get-tuple-element.81), channel_id=1, source_target_pairs={{0,10},{2,8},{4,14},{6,12},{8,2},{10,0},{12,6},{14,4},{1,11},{3,9}... | collective-permute-start | bytes 196616 | tf_op jit(solution)/shard_map/ppermute | solution.py:25
  60.1 6.1 %collective-permute-start.19 = (bf16[16,2048]{1,0:T(8,128)(2,1)S(1)}, bf16[16,2048]{1,0:T(8,128)(2,1)S(1)}, u32[]{:S(2)}, u32[]{:S(2)}) collective-permute-start(bf16[16,2048]{1,0:T(8,128)(2,1)S(1)} %get-tuple-element.82), channel_id=1, source_target_pairs={{0,12},{2,14},{4,8},{6,10},{8,4},{10,6},{12,0},{14,2},{1,13},{3,15... | collective-permute-start | bytes 196616 | tf_op jit(solution)/shard_map/ppermute | solution.py:25
